TPU v7x, 32 devices: a whole 2x2x4 slice. The times are simulated.
32 devices in a mesh: dp: 8 (over z, x), tensor: 4 (over y, core).
Axes of the slice: x: 2, y: 2, z: 4, core: 2. Of those that a mesh axis runs over, the one named last changes fastest.
Arguments:
- activations: bfloat16 [512, 24, 14336], P('dp', None, 'tensor'), may hold values from -6 to 6
- out_grads: bfloat16 [512, 24, 4096], P('dp', None, 'tensor'), may hold values from -6 to 6
- proj_in: bfloat16 [14336, 64], P('tensor'), may hold values from -0.046875 to 0.046875
- proj_out: bfloat16 [4096, 64], P('tensor'), may hold values from -0.09375 to 0.09375
- queries: bfloat16 [8, 2560, 4096], P('dp', 'tensor'), may hold values from -0.09375 to 0.09375
- candidates: int32 [512, 1], P('dp'), may hold values from 0 to 7; in each aligned block of 64 rows (0 to 63, 64 to 127, ...) at most 20 rows name the same one
Outputs:
- scores: float32 [512, 1, 2560], P('dp', None, 'tensor')
Inputs may be any that keep to these rules, and one draw needn't show every extreme that they name: `candidates`: each example names 1 different groups. Among the 64 examples of one index of dp at most 20 name the same group, and in every draw some group is named by exactly 20 of them.
All inputs are finite; a program needn't handle non-finite values.
Results may differ from a plain program's by a relative error of at most 0.0029.
Values may be sent and summed in bfloat16 or wider, within the bound.
No kernel may reach another device: no remote copies, remote signals or barrier semaphores. Data moves between devices by JAX's collectives and lax.ppermute only.
A program may use at most 64 MiB of HBM per device.

v0:
```python
import jax
import jax.numpy as jnp
from jax import lax
from jax.sharding import PartitionSpec as P

epsilon = 1e-06


def local(activations, out_grads, proj_in, proj_out, queries, candidates):
    examples_here, tokens_here, hidden_here = activations.shape
    proj_rank = proj_in.shape[1]
    per_example = candidates.shape[1]
    groups = lax.axis_size("dp")
    capacity = max(2, 5 * examples_here * per_example // (2 * groups))
    act_proj = jnp.dot(
        activations.reshape(examples_here * tokens_here, hidden_here),
        proj_in,
        preferred_element_type=jnp.float32,
    )
    grad_proj = jnp.dot(
        out_grads.reshape(examples_here * tokens_here, out_grads.shape[2]),
        proj_out,
        preferred_element_type=jnp.float32,
    )
    both_proj = jnp.concatenate([grad_proj, act_proj], axis=1).reshape(
        examples_here, tokens_here, 2 * proj_rank
    )
    summed = lax.psum(both_proj, "tensor")
    grad_side = summed[:, :, :proj_rank]
    act_side = summed[:, :, proj_rank:]
    example_grads = jnp.einsum(
        "eta,etb->eab", grad_side, act_side, precision=lax.Precision.HIGHEST
    ).reshape(examples_here, proj_rank * proj_rank)
    inv_rms = lax.rsqrt(jnp.mean(example_grads * example_grads, axis=1, keepdims=True) + epsilon)
    unit_grads = (example_grads * inv_rms).astype(jnp.bfloat16)
    flat_cands = candidates.reshape(-1)
    hit_table = (flat_cands[:, None] == jnp.arange(groups, dtype=jnp.int32)[None, :]).astype(
        jnp.int32
    )
    earlier = jnp.cumsum(hit_table, axis=0) - hit_table
    slot_index = jnp.sum(earlier * hit_table, axis=1)
    dest_index = flat_cands * capacity + slot_index
    row_copies = jnp.repeat(unit_grads, per_example, axis=0)
    grad_width = unit_grads.shape[1]
    send_buffer = (
        jnp.zeros((groups * capacity, grad_width), jnp.bfloat16).at[dest_index].set(row_copies)
    )
    send_buffer = send_buffer.reshape(groups, capacity, grad_width)
    query_block = queries[0]
    col_width = grad_width // lax.axis_size("tensor")
    column_part = lax.dynamic_slice_in_dim(
        send_buffer, lax.axis_index("tensor") * col_width, col_width, 2
    )
    received = lax.all_to_all(column_part, "dp", split_axis=0, concat_axis=0, tiled=True)
    slot_scores = jnp.einsum(
        "gsk,qk->gsq",
        lax.all_gather(received, "tensor", axis=2, tiled=True),
        query_block,
        preferred_element_type=jnp.float32,
    )
    returned = lax.all_to_all(slot_scores, "dp", split_axis=0, concat_axis=0, tiled=True)
    picked = returned.reshape(groups * capacity, returned.shape[2])[dest_index]
    return picked.reshape(examples_here, per_example, returned.shape[2])


def solution(mesh):
    placed = (
        P("dp", None, "tensor"),
        P("dp", None, "tensor"),
        P("tensor", None),
        P("tensor", None),
        P("dp", "tensor", None),
        P("dp", None),
    )
    return jax.shard_map(
        local, mesh=mesh, in_specs=placed, out_specs=P("dp", None, "tensor"), check_vma=False
    )
```

profile of v0, /device:TPU:0, one launch (start us, length us, event | category | flops | bytes accessed | tf_op | source)
XLA Modules:
  0.0 143.9 jit_solution(3581498946404453794)
XLA Ops:
  6.5 0.0 copy-start
  6.5 0.0 all-reduce.2.cloned.1.call-start
  6.5 0.0 copy-start.1
  6.5 7.7 %fusion.11 = f32[1536,64]{0,1:T(8,128)S(1)} fusion(bf16[1536,3584]{1,0:T(8,128)(2,1)} %bitcast.21, bf16[3584,64]{0,1:T(8,128)(2,1)} %param.8), kind=kOutput, calls=%fused_computation.23 | convolution fusion | flops 704643072 | bytes 11862016 | tf_op jit(solution)/shard_map/dot_general | solution.py:15
  14.2 0.0 copy-done
  14.3 0.0 copy-done.1
  14.3 1.1 fusion.10
  15.3 0.0 copy-start.2
  15.4 1.0 pad_maximum_fusion
  16.3 2.3 %copy.9 = f32[1536,128]{1,0:T(8,128)} copy(f32[1536,128]{0,1:T(8,128)} %pad_maximum_fusion) | data formatting | bytes 1572864 | tf_op jit(solution)/shard_map/concatenate | solution.py:25
  18.6 0.0 all-reduce.2.cloned.1.call-update
  18.6 0.0 all-gather.2.cloned.1.call-start
  18.7 0.0 copy-done.2
  18.7 0.1 fusion.8
  18.8 0.1 reduce_window_sum.11
  18.8 0.2 select_reduce_fusion
  19.0 37.1 %all-reduce.2.cloned.1.call-done = f32[64,24,128]{2,1,0:T(8,128)} async-done(((f32[64,24,128]{2,1,0:T(8,128)}), f32[64,24,128]{2,1,0:T(8,128)}) %all-reduce.2.cloned.1.call-update) | async-done | bytes 786448 | tf_op jit(solution)/shard_map/psum | solution.py:28
  56.1 7.0 %multiply_reduce_fusion = (f32[64]{0:T(128)S(1)}, f32[64,64,64]{2,1,0:T(8,128)}) fusion(f32[64,24,128]{2,1,0:T(8,128)} %all-reduce.2.cloned.1.call-done), kind=kOutput, calls=%fused_computation.4 | convolution fusion | flops 76021696 | bytes 2621696 | tf_op jit(solution)/shard_map/eta,etb->eab/dot_general | solution.py:31
  63.1 2.9 %reshape.34 = f32[64,4096]{1,0:T(8,128)} reshape(f32[64,64,64]{2,1,0:T(8,128)} %get-tuple-element.6) | data formatting | bytes 2097152 | tf_op jit(solution)/shard_map/reshape | solution.py:33
  66.0 3.3 %scatter_custom_fusion = bf16[160,4096]{1,0:T(8,128)(2,1)} fusion(s32[64]{0:T(128)S(1)} %fusion.9, bf16[]{:T(256)} %constant.10.clone.1, f32[64,4096]{1,0:T(8,128)} %reshape.34, f32[64]{0:T(128)S(1)} %add_rsqrt_fusion), kind=kCustom, calls=%fused_computation.10 | custom fusion | flops 524288 | bytes 2359810 | tf_op jit(solution)/shard_map/scatter | solution.py:46
  69.3 2.4 %reshape.35 = bf16[8,20,4096]{2,1,0:T(8,128)(2,1)} reshape(bf16[160,4096]{1,0:T(8,128)(2,1)} %scatter_custom_fusion) | data formatting | bytes 2621440 | tf_op jit(solution)/shard_map/reshape | solution.py:48
  71.7 1.0 constant_dynamic-slice_fusion
  72.7 16.6 %all_to_all.10 = bf16[8,20,1024]{2,1,0:T(8,128)(2,1)} all-to-all(bf16[8,20,1024]{2,1,0:T(8,128)(2,1)S(1)} %constant_dynamic-slice_fusion), channel_id=1, replica_groups=mesh['dp'=8,'tensor'=4] {'dp'}, dimensions={0} | all-to-all | bytes 655360 | tf_op jit(solution)/shard_map/all_to_all | solution.py:54
  89.3 0.0 all-gather.2.cloned.1.call-update
  89.3 18.0 %all-gather.2.cloned.1.call-done = bf16[8,20,4096]{2,1,0:T(8,128)(2,1)} async-done(((bf16[8,20,1024]{2,1,0:T(8,128)(2,1)}), bf16[8,20,4096]{2,1,0:T(8,128)(2,1)}) %all-gather.2.cloned.1.call-update) | async-done | bytes 1310736 | tf_op jit(solution)/shard_map/all_gather | solution.py:57
  107.4 5.6 %fusion = f32[8,20,640]{2,1,0:T(8,128)} fusion(bf16[8,20,4096]{2,1,0:T(8,128)(2,1)} %all-gather.2.cloned.1.call-done, bf16[1,640,4096]{2,1,0:T(8,128)(2,1)} %param.10), kind=kOutput, calls=%fused_computation.2 | convolution fusion | flops 838860800 | bytes 6963200 | tf_op jit(solution)/shard_map/gsk,qk->gsq/dot_general | solution.py:55
  113.0 5.5 %all-to-all-start.1 = ((f32[8,20,640]{2,1,0:T(8,128)}), f32[8,20,640]{2,1,0:T(8,128)}, u32[]{:S(2)}, u32[]{:S(2)}) async-start(f32[8,20,640]{2,1,0:T(8,128)} %fusion), calls=%async_computation.1 | async-start | bytes 983040 | tf_op jit(solution)/shard_map/all_to_all | solution.py:61
  118.5 0.6 pad_clamp_fusion
  119.1 13.7 %all-to-all-done.1 = f32[8,20,640]{2,1,0:T(8,128)} async-done(((f32[8,20,640]{2,1,0:T(8,128)}), f32[8,20,640]{2,1,0:T(8,128)}, u32[]{:S(2)}, u32[]{:S(2)}) %all-to-all-start.1) | async-done | bytes 409632 | tf_op jit(solution)/shard_map/all_to_all | solution.py:61
  132.8 1.1 reshape.36
  133.9 1.5 %gather_fusion = f32[64,640]{1,0:T(8,128)} fusion(f32[160,640]{1,0:T(8,128)S(1)} %reshape.36, s32[1024]{0:T(1024)} %pad_clamp_fusion), kind=kCustom, calls=%fused_computation | custom fusion | bytes 327936 | tf_op jit(solution)/shard_map/gather | solution.py:62
  135.3 1.7 %copy.10 = f32[64,1,640]{2,1,0:T(1,128)} copy(f32[64,1,640]{2,0,1:T(8,128)} %bitcast.23) | data formatting | bytes 327680 | tf_op jit(solution)/shard_map/reshape | solution.py:63
  (2 shorter events, 0.0 us)
Async XLA Ops:
  6.5 7.7 %copy-start = (bf16[64,24,1024]{2,1,0:T(8,128)(2,1)S(1)}, bf16[64,24,1024]{2,1,0:T(8,128)(2,1)}, u32[]{:S(2)}) copy-start(bf16[64,24,1024]{2,1,0:T(8,128)(2,1)} %param.7) | copy-start | bytes 9437188
  6.5 49.6 %all-reduce.2.cloned.1.call-start = ((), (), s32[]{:S(2)}) async-start(), calls=%async_computation.2 | async-start | bytes 1572864 | tf_op jit(solution)/shard_map/psum | solution.py:28
  6.5 7.7 %copy-start.1 = (bf16[1024,64]{0,1:T(8,128)(2,1)S(1)}, bf16[1024,64]{0,1:T(8,128)(2,1)}, u32[]{:S(2)}) copy-start(bf16[1024,64]{0,1:T(8,128)(2,1)} %param.9) | copy-start | bytes 393220
  15.3 3.3 %copy-start.2 = (s32[64,1]{0,1:T(1,128)S(1)}, s32[64,1]{0,1:T(1,128)}, u32[]{:S(2)}) copy-start(s32[64,1]{0,1:T(1,128)} %param.11) | copy-start | bytes 772
  18.6 88.8 %all-gather.2.cloned.1.call-start = ((), (), s32[]{:S(2)}) async-start(), calls=%async_computation.3 | async-start | bytes 1966080 | tf_op jit(solution)/shard_map/all_gather | solution.py:57
  113.0 19.8 %all-to-all-start.1 = ((f32[8,20,640]{2,1,0:T(8,128)}), f32[8,20,640]{2,1,0:T(8,128)}, u32[]{:S(2)}, u32[]{:S(2)}) async-start(f32[8,20,640]{2,1,0:T(8,128)} %fusion), calls=%async_computation.1 | async-start | bytes 983040 | tf_op jit(solution)/shard_map/all_to_all | solution.py:61
Sparse Core Ops, SparseCore 0:
  18.7 37.3 all-reduce.1
  89.5 17.8 all-gather.1
where the time goes:
time: 144 us
  waiting for transfers between devices  68.8 us (48%)
  matrix products  21.4 us (15%)
  blocking collectives  16.6 us (12%)
  between operations  13.5 us (9%)
  local copies, waits for them, and re-layouts  12.9 us (9%)
  starting transfers between devices  5.56 us (4%)
  other arithmetic  5.23 us (4%)
    psum x1, waiting for transfers between devices, local(): summed = lax.psum(both_proj, 'tensor')  37.1 us
    all_gather x1, waiting for transfers between devices, local(): lax.all_gather(received, 'tensor', axis=2, tiled=True)  18 us
    all_to_all x1, blocking collectives, local(): lax.all_to_all(column_part, 'dp', split_axis=0, concat_axis=0, tiled=True)  16.6 us
    all_to_all x1, waiting for transfers between devices, local(): lax.all_to_all(slot_scores, 'dp', split_axis=0, concat_axis=0, tiled=True)  13.7 us
    dot_general x1, matrix products, local(): jnp.dot(activations.reshape(examples_here * tokens_here, hidden_here), pr...  7.7 us
    dot_general x1, matrix products, local(): jnp.einsum('eta,etb->eab', grad_side, act_side, precision=lax.Precision.H...  6.96 us
    dot_general x1, matrix products, local(): jnp.einsum('gsk,qk->gsq', lax.all_gather(received, 'tensor', axis=2, tile...  5.62 us
    all_to_all x1, starting transfers between devices, local(): lax.all_to_all(slot_scores, 'dp', split_axis=0, concat_axis=0, tiled=True)  5.51 us
  transfers between devices with their start and end apart: 3, of which 3 were waited for; matrix products, arithmetic and copies ran while one was open for 1% of the time, Pallas kernels for 0%

commit v1 on v0

--- a/solution.py
+++ b/solution.py
@@ -1,12 +1,305 @@
+import functools
+
 import jax
 import jax.numpy as jnp
 from jax import lax
+from jax.experimental import pallas as pl
+from jax.experimental.pallas import tpu as pltpu
 from jax.sharding import PartitionSpec as P
 
 epsilon = 1e-06
-
-
-def local(activations, out_grads, proj_in, proj_out, queries, candidates):
+LANES = 128
+NT = (((1,), (1,)), ((), ()))
+TN = (((0,), (0,)), ((), ()))
+
+
+def project_kernel(
+    groups, ways, steps, cand_ref, act_ref, grad_ref, win_ref, wout_ref,
+    keep_ref, far_ref, near_ref, total, wout, rank, start,
+):
+    step = pl.program_id(0)
+    rows = act_ref.shape[0]
+    proj_rank = win_ref.shape[0]
+    examples = cand_ref.shape[0]
+    per_step = examples // steps
+    tokens = rows // per_step
+    me = lax.axis_index("tensor")
+
+    @pl.when(step == 0)
+    def _():
+        half = proj_rank // 2
+        r = lax.broadcasted_iota(jnp.int32, (proj_rank, proj_rank), 0)
+        c = lax.broadcasted_iota(jnp.int32, (proj_rank, proj_rank), 1)
+        source = jnp.where(r < half, 2 * r, 2 * (r - half) + 1)
+        pick = (c == source).astype(jnp.bfloat16)
+        wout[...] = jnp.dot(pick, wout_ref[...], preferred_element_type=jnp.float32).astype(
+            jnp.bfloat16
+        )
+        for g in range(groups + 1):
+            start[g] = 0
+        for e in range(examples):
+            g = cand_ref[e]
+            seen = start[g]
+            rank[e] = seen
+            start[g] = seen + 1
+        below = jnp.int32(0)
+        for g in range(groups):
+            here = start[g]
+            start[g] = below
+            below = below + here
+
+    act = lax.dot_general(act_ref[...], win_ref[...], NT, preferred_element_type=jnp.float32)
+    grad = lax.dot_general(grad_ref[...], wout[...], NT, preferred_element_type=jnp.float32)
+    both = jnp.concatenate([grad, act], axis=1)
+    share = examples // ways
+    for k in range(per_step):
+        e = step * per_step + k
+        place = start[cand_ref[e]] + rank[e]
+        rel = lax.rem(place, ways) ^ me
+        part = ((rel & 1) << 1) | (rel >> 1)
+        row = (part * share + lax.div(place, ways)) * tokens
+        total[pl.ds(pl.multiple_of(row, 8), tokens), :] = both[k * tokens : (k + 1) * tokens]
+
+    @pl.when(step == steps - 1)
+    def _():
+        size = share * tokens
+        keep_ref[...] = total[0 : 2 * size, :]
+        near_ref[...] = total[2 * size : 3 * size, :]
+        far_ref[...] = total[3 * size : 4 * size, :]
+
+
+def project(cands, act, grad, win, wout, groups, ways):
+    examples = cands.shape[0]
+    rows = act.shape[0]
+    steps = 8
+    block = rows // steps
+    share = rows // ways
+    f32 = jnp.float32
+    whole = lambda shape: pl.BlockSpec(shape, lambda i: (0, 0))
+    return pl.pallas_call(
+        functools.partial(project_kernel, groups, ways, steps),
+        grid=(steps,),
+        in_specs=[
+            pl.BlockSpec(memory_space=pltpu.SMEM),
+            pl.BlockSpec((block, act.shape[1]), lambda i: (i, 0)),
+            pl.BlockSpec((block, grad.shape[1]), lambda i: (i, 0)),
+            whole(win.shape),
+            whole(wout.shape),
+        ],
+        out_specs=[whole((2 * share, LANES)), whole((share, LANES)), whole((share, LANES))],
+        out_shape=[
+            jax.ShapeDtypeStruct((2 * share, LANES), f32),
+            jax.ShapeDtypeStruct((share, LANES), f32),
+            jax.ShapeDtypeStruct((share, LANES), f32),
+        ],
+        scratch_shapes=[
+            pltpu.VMEM((rows, LANES), f32),
+            pltpu.VMEM(wout.shape, jnp.bfloat16),
+            pltpu.SMEM((examples,), jnp.int32),
+            pltpu.SMEM((groups + 1,), jnp.int32),
+        ],
+        compiler_params=pltpu.CompilerParams(vmem_limit_bytes=32 << 20),
+        cost_estimate=pl.CostEstimate(
+            flops=2 * rows * (act.shape[1] + grad.shape[1]) * 64,
+            bytes_accessed=2 * rows * (act.shape[1] + grad.shape[1]),
+            transcendentals=0,
+        ),
+        name="project",
+    )(cands, act, grad, win, wout)
+
+
+def unit_kernel(tokens, chunks, row_ref, a_ref, b_ref, c_ref, out_ref, total):
+    total[...] = a_ref[...] + b_ref[...] + c_ref[...]
+    out_ref[...] = jnp.zeros_like(out_ref)
+    count = total.shape[0] // tokens
+    half = LANES // 2
+    width = chunks * LANES
+    low = lax.broadcasted_iota(jnp.int32, (chunks, LANES), 1) < half
+    low_t = lax.broadcasted_iota(jnp.int32, (tokens, LANES), 1) < half
+    for i in range(count):
+        part = total[i * tokens : (i + 1) * tokens, :]
+        twice = jnp.where(low_t, pltpu.roll(part, half, 1), part)
+        g_hi = part.astype(jnp.bfloat16).astype(jnp.float32)
+        a_hi = twice.astype(jnp.bfloat16).astype(jnp.float32)
+        left = jnp.concatenate([g_hi, g_hi, part - g_hi], axis=0)[:, :half].astype(jnp.bfloat16)
+        right = jnp.concatenate([a_hi, twice - a_hi, a_hi], axis=0).astype(jnp.bfloat16)
+        prod = lax.dot_general(left, right, TN, preferred_element_type=jnp.float32)
+        entries = jnp.where(low, prod[:chunks], prod[chunks : 2 * chunks])
+        square = jnp.sum(entries * entries, axis=0, keepdims=True)
+        mean = jnp.sum(square, axis=1, keepdims=True) / width
+        unit = (entries * lax.rsqrt(mean + epsilon)).astype(jnp.bfloat16)
+        row = pl.multiple_of(row_ref[i] * chunks, chunks)
+        out_ref[pl.ds(row, chunks), :] = unit
+
+
+def unit_grads(slots, a, b, c, tokens, chunks, slot_count):
+    whole = pl.BlockSpec(memory_space=pltpu.VMEM)
+    return pl.pallas_call(
+        functools.partial(unit_kernel, tokens, chunks),
+        in_specs=[pl.BlockSpec(memory_space=pltpu.SMEM), whole, whole, whole],
+        out_specs=whole,
+        out_shape=jax.ShapeDtypeStruct((slot_count * chunks, LANES), jnp.bfloat16),
+        scratch_shapes=[pltpu.VMEM(a.shape, jnp.float32)],
+        cost_estimate=pl.CostEstimate(flops=20_000_000, bytes_accessed=1_000_000, transcendentals=0),
+        name="unit_grads",
+    )(slots, a, b, c)
+
+
+def score_kernel(
+    groups, slots, padded, first, chunks, parts, has_prev, x0_ref, x1_ref, q_ref, *rest
+):
+    prev_ref = rest[0] if has_prev else None
+    out_ref, stage, units, queries, sems = rest[has_prev:]
+    width = chunks // parts * LANES
+    copies = [
+        pltpu.make_async_copy(
+            q_ref.at[:, pl.ds(k * width, width)], queries.at[k], sems.at[k]
+        )
+        for k in range(parts)
+    ]
+    for copy in copies:
+        copy.start()
+    span = slots * chunks
+    for d in range(groups):
+        base = d * padded * chunks
+        if first:
+            stage[base : base + first * chunks, :] = jnp.zeros((first * chunks, LANES), jnp.float32)
+        for n, x_ref in enumerate((x0_ref, x1_ref)):
+            at = base + (first + n * slots) * chunks
+            stage[at : at + span, :] = x_ref[d * span : (d + 1) * span, :].astype(jnp.float32)
+        at = base + (first + 2 * slots) * chunks
+        left = (padded - first - 2 * slots) * chunks
+        stage[at : at + left, :] = jnp.zeros((left, LANES), jnp.float32)
+    rows = groups * padded
+    total = prev_ref[...] if has_prev else None
+    for k in range(parts):
+        for j in range(chunks // parts):
+            piece = stage[pl.ds(k * (chunks // parts) + j, rows, stride=chunks), :]
+            units[:, j * LANES : (j + 1) * LANES] = piece.astype(jnp.bfloat16)
+        copies[k].wait()
+        add = lax.dot_general(units[...], queries[k], NT, preferred_element_type=jnp.float32)
+        total = add if total is None else total + add
+    out_ref[...] = total.astype(out_ref.dtype)
+
+
+def scores_of(x0, x1, queries, prev, groups, slots, padded, first, out_dtype):
+    chunks = queries.shape[1] // LANES
+    parts = 4
+    rows = groups * padded
+    vmem = pl.BlockSpec(memory_space=pltpu.VMEM)
+    operands = [x0, x1, queries] + ([prev] if prev is not None else [])
+    specs = [vmem, vmem, pl.BlockSpec(memory_space=pl.ANY)] + ([vmem] if prev is not None else [])
+    width = queries.shape[1] // parts
+    return pl.pallas_call(
+        functools.partial(
+            score_kernel, groups, slots, padded, first, chunks, parts, int(prev is not None)
+        ),
+        in_specs=specs,
+        out_specs=vmem,
+        out_shape=jax.ShapeDtypeStruct((rows, queries.shape[0]), out_dtype),
+        scratch_shapes=[
+            pltpu.VMEM((rows * chunks, LANES), jnp.float32),
+            pltpu.VMEM((rows, width), jnp.bfloat16),
+            pltpu.VMEM((parts, queries.shape[0], width), jnp.bfloat16),
+            pltpu.SemaphoreType.DMA((parts,)),
+        ],
+        compiler_params=pltpu.CompilerParams(vmem_limit_bytes=32 << 20),
+        cost_estimate=pl.CostEstimate(
+            flops=2 * rows * queries.shape[0] * queries.shape[1],
+            bytes_accessed=2 * queries.size,
+            transcendentals=0,
+        ),
+        name="scores",
+    )(*operands)
+
+
+def pick_kernel(row_ref, x_ref, out_ref):
+    count = row_ref.shape[0]
+    rows = x_ref.shape[0]
+    parts = x_ref.shape[1] // LANES
+    hit = lax.broadcasted_iota(jnp.int32, (count, rows), 1) == row_ref[...]
+    pick = jnp.where(hit, 1.0, 0.0).astype(jnp.bfloat16)
+    got = jnp.dot(pick, x_ref[...], preferred_element_type=jnp.float32)
+    for j in range(parts):
+        out_ref[pl.ds(j, count, stride=parts), :] = got[:, j * LANES : (j + 1) * LANES]
+
+
+def pick_rows(row, x):
+    vmem = pl.BlockSpec(memory_space=pltpu.VMEM)
+    count, width = row.shape[0], x.shape[1]
+    return pl.pallas_call(
+        pick_kernel,
+        in_specs=[vmem, vmem],
+        out_specs=vmem,
+        out_shape=jax.ShapeDtypeStruct((count * (width // LANES), LANES), jnp.float32),
+        cost_estimate=pl.CostEstimate(flops=16_000_000, bytes_accessed=400_000, transcendentals=0),
+        name="pick_rows",
+    )(row, x)
+
+
+def local_one(activations, out_grads, proj_in, proj_out, queries, candidates):
+    examples, tokens, hidden = activations.shape
+    features = out_grads.shape[2]
+    groups = lax.axis_size("dp")
+    ways = lax.axis_size("tensor")
+    me = lax.axis_index("tensor")
+    capacity = max(2, 5 * examples // (2 * groups))
+    slots = -(-capacity // ways)
+    padded = -(-ways * slots // 8) * 8
+    query_block = queries[0]
+    chunks = query_block.shape[1] // LANES
+    core = [(i, i ^ 1) for i in range(ways)]
+    across = [(i, i ^ 2) for i in range(ways)]
+
+    cands = candidates.reshape(-1)
+    keep, far, near = project(
+        cands,
+        activations.reshape(examples * tokens, hidden),
+        out_grads.reshape(examples * tokens, features),
+        proj_in.T,
+        proj_out.T,
+        groups,
+        ways,
+    )
+    share = far.shape[0]
+    far_in = lax.ppermute(far, "tensor", core)
+    near_in = lax.ppermute(near, "tensor", core)
+    across_in = lax.ppermute(keep[share:] + far_in, "tensor", across)
+
+    number = jnp.arange(examples, dtype=jnp.int32)
+    before = (cands[None, :] < cands[:, None]) | (
+        (cands[None, :] == cands[:, None]) & (number[None, :] < number[:, None])
+    )
+    place = jnp.sum(before.astype(jnp.int32), axis=1)
+    start = jnp.sum((cands[None, :] < cands[:, None]).astype(jnp.int32), axis=1)
+    owner = place % ways
+    slot = place // ways - (start + ways - 1 - owner) // ways
+    mine = (
+        place[None, :] == ways * jnp.arange(examples // ways, dtype=jnp.int32)[:, None] + me
+    )
+    my_slots = jnp.sum(jnp.where(mine, (cands * slots + slot)[None, :], 0), axis=1)
+    pick = (cands * padded + (owner ^ me) * slots + slot)[:, None]
+
+    units = unit_grads(my_slots, keep[:share], near_in, across_in, tokens, chunks, groups * slots)
+    shape = (groups, slots * chunks, LANES)
+    own = lax.all_to_all(units.reshape(shape), "dp", split_axis=0, concat_axis=0, tiled=True)
+    own = own.reshape(units.shape)
+    over_y = lax.ppermute(own, "tensor", across)
+    over_core = lax.ppermute(own, "tensor", core)
+    over_both = lax.ppermute(over_y, "tensor", core)
+    first = scores_of(
+        own, over_core, query_block, None, groups, slots, padded, 0, jnp.float32
+    )
+    both = scores_of(
+        over_y, over_both, query_block, first, groups, slots, padded, 2 * slots, jnp.bfloat16
+    )
+    block = both.reshape(groups, padded, both.shape[1])
+    returned = lax.all_to_all(block, "dp", split_axis=0, concat_axis=0, tiled=True)
+    picked = pick_rows(pick, returned.reshape(both.shape))
+    return picked.reshape(examples, 1, both.shape[1])
+
+
+def local_many(activations, out_grads, proj_in, proj_out, queries, candidates):
     examples_here, tokens_here, hidden_here = activations.shape
     proj_rank = proj_in.shape[1]
     per_example = candidates.shape[1]
@@ -32,7 +325,7 @@
         "eta,etb->eab", grad_side, act_side, precision=lax.Precision.HIGHEST
     ).reshape(examples_here, proj_rank * proj_rank)
     inv_rms = lax.rsqrt(jnp.mean(example_grads * example_grads, axis=1, keepdims=True) + epsilon)
-    unit_grads = (example_grads * inv_rms).astype(jnp.bfloat16)
+    unit = (example_grads * inv_rms).astype(jnp.bfloat16)
     flat_cands = candidates.reshape(-1)
     hit_table = (flat_cands[:, None] == jnp.arange(groups, dtype=jnp.int32)[None, :]).astype(
         jnp.int32
@@ -40,13 +333,12 @@
     earlier = jnp.cumsum(hit_table, axis=0) - hit_table
     slot_index = jnp.sum(earlier * hit_table, axis=1)
     dest_index = flat_cands * capacity + slot_index
-    row_copies = jnp.repeat(unit_grads, per_example, axis=0)
-    grad_width = unit_grads.shape[1]
+    row_copies = jnp.repeat(unit, per_example, axis=0)
+    grad_width = unit.shape[1]
     send_buffer = (
         jnp.zeros((groups * capacity, grad_width), jnp.bfloat16).at[dest_index].set(row_copies)
     )
     send_buffer = send_buffer.reshape(groups, capacity, grad_width)
-    query_block = queries[0]
     col_width = grad_width // lax.axis_size("tensor")
     column_part = lax.dynamic_slice_in_dim(
         send_buffer, lax.axis_index("tensor") * col_width, col_width, 2
@@ -55,12 +347,19 @@
     slot_scores = jnp.einsum(
         "gsk,qk->gsq",
         lax.all_gather(received, "tensor", axis=2, tiled=True),
-        query_block,
+        queries[0],
         preferred_element_type=jnp.float32,
     )
     returned = lax.all_to_all(slot_scores, "dp", split_axis=0, concat_axis=0, tiled=True)
     picked = returned.reshape(groups * capacity, returned.shape[2])[dest_index]
     return picked.reshape(examples_here, per_example, returned.shape[2])
+
+
+def local(activations, out_grads, proj_in, proj_out, queries, candidates):
+    one = candidates.shape[1] == 1 and lax.axis_size("tensor") == 4
+    return (local_one if one else local_many)(
+        activations, out_grads, proj_in, proj_out, queries, candidates
+    )
 
 
 def solution(mesh):

time: 144 us -> 86.2 us (0.60)
  waiting for transfers between devices: 68.8 us -> 19.4 us
  Pallas kernels: 0 us -> 22.2 us
  matrix products: 21.4 us -> 0 us
  between operations: 13.5 us -> 0.08 us
  starting transfers between devices: 5.56 us -> 9.86 us
  other arithmetic: 5.23 us -> 2.29 us
  local copies, waits for them, and re-layouts: 12.9 us -> 15.3 us
    psum x1 -> x0, waiting for transfers between devices: 37.1 us -> none  [local(): summed = lax.psum(both_proj, 'tensor')]
    pallas_call x0 -> x5, Pallas kernels: none -> 22.2 us  [the longest x2 11.4 us: scores_of(): pl.pallas_call(functools.partial(score_kernel, groups, slots, padded, fir...]
    dot_general x4 -> x0, matrix products: 21.4 us -> none  [the longest x1 7.7 us: local(): jnp.dot(activations.reshape(examples_here * tokens_here, hidden_here), pr...]
    all_gather x1 -> x0, waiting for transfers between devices: 18 us -> none  [local(): lax.all_gather(received, 'tensor', axis=2, tiled=True)]
    unnamed x6 -> x22, local copies, waits for them, and re-layouts: 0.01 us -> 14.9 us
    ppermute x0 -> x6, waiting for transfers between devices: none -> 10.8 us  [the longest x1 5.55 us: local_one(): over_y = lax.ppermute(own, 'tensor', across)]
    reshape x4 -> x0, local copies, waits for them, and re-layouts: 8.1 us -> none  [the longest x1 2.9 us: local(): example_grads = jnp.einsum('eta,etb->eab', grad_side, act_side, precision...]
    all_to_all x1, waiting for transfers between devices: 13.7 us -> 8.58 us  [local_one(): lax.all_to_all(block, 'dp', split_axis=0, concat_axis=0, tiled=True)]
  transfers between devices with their start and end apart: 3 -> 7, of which waited for: 3 -> 4; matrix products, arithmetic and copies ran while one was open for 1% -> 3% of each run, Pallas kernels for 0% -> 6%
where the time goes in v1:
time: 86.2 us; the launch traced here: 85.6 us
  Pallas kernels  22.2 us (26%)
  waiting for transfers between devices  19.4 us (23%)
  blocking collectives  16.5 us (19%)
  local copies, waits for them, and re-layouts  15.3 us (18%)
  starting transfers between devices  9.86 us (11%)
  other arithmetic  2.29 us (3%)
    all_to_all x1, blocking collectives, local_one(): lax.all_to_all(units.reshape(shape), 'dp', split_axis=0, concat_axis=0, t...  16.5 us
    unnamed x22, local copies, waits for them, and re-layouts  14.9 us
    pallas_call x2, Pallas kernels, scores_of(): pl.pallas_call(functools.partial(score_kernel, groups, slots, padded, fir...  11.4 us
    all_to_all x1, waiting for transfers between devices, local_one(): lax.all_to_all(block, 'dp', split_axis=0, concat_axis=0, tiled=True)  8.58 us
    pallas_call x1, Pallas kernels, project(): pl.pallas_call(functools.partial(project_kernel, groups, ways, steps), gr...  6.45 us
    ppermute x1, waiting for transfers between devices, local_one(): over_y = lax.ppermute(own, 'tensor', across)  5.55 us
    all_to_all x1, starting transfers between devices, local_one(): lax.all_to_all(block, 'dp', split_axis=0, concat_axis=0, tiled=True)  4.86 us
    ppermute x1, waiting for transfers between devices, local_one(): across_in = lax.ppermute(keep[share:] + far_in, 'tensor', across)  4.5 us
  transfers between devices with their start and end apart: 7, of which 4 were waited for; matrix products, arithmetic and copies ran while one was open for 3% of the time, Pallas kernels for 6%

profile of v1, /device:TPU:0, one launch (start us, length us, event | category | flops | bytes accessed | tf_op | source)
XLA Modules:
  0.0 85.6 jit_solution(1658980756006295155)
XLA Ops:
  0.0 0.0 copy-start.2
  0.0 4.1 %copy-done.2 = bf16[64,24,3584]{2,1,0:T(8,128)(2,1)S(1)} copy-done((bf16[64,24,3584]{2,1,0:T(8,128)(2,1)S(1)}, bf16[64,24,3584]{2,1,0:T(8,128)(2,1)}, u32[]{:S(2)}) %copy-start.2) | copy-done | bytes 11010072
  4.1 0.0 copy-start.3
  4.1 1.9 %copy-done.3 = bf16[64,24,1024]{2,1,0:T(8,128)(2,1)S(1)} copy-done((bf16[64,24,1024]{2,1,0:T(8,128)(2,1)S(1)}, bf16[64,24,1024]{2,1,0:T(8,128)(2,1)}, u32[]{:S(2)}) %copy-start.3) | copy-done | bytes 3145752
  6.0 0.0 copy-start.4
  6.0 1.0 %copy-done.4 = bf16[3584,64]{0,1:T(8,128)(2,1)S(1)} copy-done((bf16[3584,64]{0,1:T(8,128)(2,1)S(1)}, bf16[3584,64]{0,1:T(8,128)(2,1)}, u32[]{:S(2)}) %copy-start.4) | copy-done | bytes 458776
  7.0 0.0 copy-start.5
  7.0 0.9 %copy-done.5 = bf16[1024,64]{0,1:T(8,128)(2,1)S(1)} copy-done((bf16[1024,64]{0,1:T(8,128)(2,1)S(1)}, bf16[1024,64]{0,1:T(8,128)(2,1)}, u32[]{:S(2)}) %copy-start.5) | copy-done | bytes 131096
  7.9 0.0 copy-start.6
  7.9 0.7 copy-done.6
  8.6 0.0 copy-start.7
  8.6 6.5 %project.1 = (f32[768,128]{1,0:T(8,128)S(1)}, f32[384,128]{1,0:T(8,128)S(1)}, f32[384,128]{1,0:T(8,128)S(1)}) custom-call(s32[64]{0:T(128)S(1)} %bitcast.24, bf16[1536,3584]{1,0:T(8,128)(2,1)S(1)} %bitcast.17, bf16[1536,1024]{1,0:T(8,128)(2,1)S(1)} %bitcast.18, bf16[64,3584]{1,0:T(8,128)(2,1)S(1)} %bitcast.22, bf16[64,1024]{1,0:T(8,128)(2,1)S(1)} %bitcast.23), custom_call_target="tpu_custom_call" | custom-call | flops 905969664 | bytes 14155776 | tf_op jit(solution)/shard_map/project/pallas_call | solution.py:79
  15.1 0.5 collective-permute-start.1
  15.6 0.1 collective-permute-start
  15.7 0.2 fusion
  15.9 0.0 copy-done.7
  15.9 0.8 collective-permute-done.1
  16.7 0.7 slice_add_fusion
  17.4 2.9 %collective-permute-start.2 = (f32[384,128]{1,0:T(8,128)S(1)}, f32[384,128]{1,0:T(8,128)S(1)}, u32[]{:S(2)}, u32[]{:S(2)}) collective-permute-start(f32[384,128]{1,0:T(8,128)S(1)} %get-tuple-element.13), channel_id=1, source_target_pairs={{0,2},{1,3},{2,0},{3,1},{4,6},{5,7},{6,4},{7,5},{8,10},{9,11},{10,... | collective-permute-start | bytes 589832 | tf_op jit(solution)/shard_map/ppermute | solution.py:267
  20.3 0.7 select_reduce_fusion.row_ref
  20.9 0.0 collective-permute-done.b_ref
  21.0 0.0 copy-start.9
  21.0 4.5 %collective-permute-done.2.c_ref = f32[384,128]{1,0:T(8,128)S(1)} collective-permute-done((f32[384,128]{1,0:T(8,128)S(1)}, f32[384,128]{1,0:T(8,128)S(1)}, u32[]{:S(2)}, u32[]{:S(2)}) %collective-permute-start.2) | collective-permute-done | bytes 196640 | tf_op jit(solution)/shard_map/ppermute | solution.py:267
  25.5 0.0 copy-start.10
  25.5 0.0 copy-done.9
  25.5 0.7 copy-done.10
  26.1 2.5 %unit_grads.1 = bf16[1280,128]{1,0:T(8,128)(2,1)} custom-call(s32[16]{0:T(128)} %select_reduce_fusion.row_ref, f32[384,128]{1,0:T(8,128)} %get-tuple-element.14.a_ref, f32[384,128]{1,0:T(8,128)} %copy-done.9, f32[384,128]{1,0:T(8,128)} %copy-done.10), custom_call_target="tpu_custom_call" | custom-call | flops 20000000 | bytes 1000000 | tf_op jit(solution)/shard_map/unit_grads/pallas_call | solution.py:137
  28.7 16.5 %all_to_all.10 = bf16[8,160,128]{2,1,0:T(8,128)(2,1)S(1)} all-to-all(bf16[8,160,128]{2,1,0:T(8,128)(2,1)} %bitcast.26), channel_id=1, replica_groups=mesh['dp'=8,'tensor'=4] {'dp'}, dimensions={0} | all-to-all | bytes 655360 | tf_op jit(solution)/shard_map/all_to_all | solution.py:285
  45.1 1.5 %collective-permute-start.3 = (bf16[1280,128]{1,0:T(8,128)(2,1)S(1)}, bf16[1280,128]{1,0:T(8,128)(2,1)S(1)}, u32[]{:S(2)}, u32[]{:S(2)}) collective-permute-start(bf16[1280,128]{1,0:T(8,128)(2,1)S(1)} %bitcast.19), channel_id=1, source_target_pairs={{0,2},{1,3},{2,0},{3,1},{4,6},{5,7},{6,4},{7,5},{8,10},{9,11},{10,... | collective-permute-start | bytes 983048 | tf_op jit(solution)/shard_map/ppermute | solution.py:287
  46.6 0.0 collective-permute-start.5
  46.6 5.6 %collective-permute-done.3.x0_ref = bf16[1280,128]{1,0:T(8,128)(2,1)S(1)} collective-permute-done((bf16[1280,128]{1,0:T(8,128)(2,1)S(1)}, bf16[1280,128]{1,0:T(8,128)(2,1)S(1)}, u32[]{:S(2)}, u32[]{:S(2)}) %collective-permute-start.3) | collective-permute-done | bytes 327712 | tf_op jit(solution)/shard_map/ppermute | solution.py:287
  52.2 0.0 collective-permute-start.4
  52.2 0.1 copy.31
  52.3 0.1 copy.25
  52.4 0.1 copy.29
  52.5 0.0 collective-permute-done.5.x1_ref
  52.5 2.5 %copy-done = bf16[1,640,4096]{2,1,0:T(8,128)(2,1)S(1)} copy-done((bf16[1,640,4096]{2,1,0:T(8,128)(2,1)S(1)}, bf16[1,640,4096]{2,1,0:T(8,128)(2,1)}, u32[]{:S(2)}) %copy-start) | copy-done | bytes 5242904
  55.0 5.5 %scores.2.rest_0_ = f32[192,640]{1,0:T(8,128)S(1)} custom-call(bf16[1280,128]{1,0:T(8,128)(2,1)S(1)} %bitcast.21, bf16[1280,128]{1,0:T(8,128)(2,1)S(1)} %collective-permute-done.5.x1_ref, bf16[640,4096]{1,0:T(8,128)(2,1)S(1)} %bitcast.15), custom_call_target="tpu_custom_call" | custom-call | flops 1006632960 | bytes 5242880 | tf_op jit(solution)/shard_map/scores/pallas_call | solution.py:193
  60.5 0.0 collective-permute-done.4.x1_ref
  60.5 0.0 copy-start.1
  60.5 2.5 %copy-done.1 = bf16[1,640,4096]{2,1,0:T(8,128)(2,1)S(1)} copy-done((bf16[1,640,4096]{2,1,0:T(8,128)(2,1)S(1)}, bf16[1,640,4096]{2,1,0:T(8,128)(2,1)}, u32[]{:S(2)}) %copy-start.1) | copy-done | bytes 5242904
  63.0 5.9 %scores.3 = bf16[192,640]{1,0:T(8,128)(2,1)} custom-call(bf16[1280,128]{1,0:T(8,128)(2,1)S(1)} %collective-permute-done.3.x0_ref, bf16[1280,128]{1,0:T(8,128)(2,1)S(1)} %collective-permute-done.4.x1_ref, bf16[640,4096]{1,0:T(8,128)(2,1)S(1)} %bitcast.16, f32[192,640]{1,0:T(8,128)S(1)} %scores.2.rest_0_), custom_call_target="tpu_custom_call" | custom-call | flops 1006632960 | bytes 5242880 | tf_op jit(solution)/shard_map/scores/pallas_call | solution.py:193
  68.9 4.9 %all-to-all-start.1 = ((bf16[8,24,640]{2,1,0:T(8,128)(2,1)}), bf16[8,24,640]{2,1,0:T(8,128)(2,1)S(1)}, u32[]{:S(2)}, u32[]{:S(2)}) async-start(bf16[8,24,640]{2,1,0:T(8,128)(2,1)} %bitcast.10), calls=%async_computation.1 | async-start | bytes 491520 | tf_op jit(solution)/shard_map/all_to_all | solution.py:297
  73.8 0.1 copy.32
  73.9 0.7 fusion.2.row_ref
  74.5 8.6 %all-to-all-done.1 = bf16[8,24,640]{2,1,0:T(8,128)(2,1)S(1)} async-done(((bf16[8,24,640]{2,1,0:T(8,128)(2,1)}), bf16[8,24,640]{2,1,0:T(8,128)(2,1)S(1)}, u32[]{:S(2)}, u32[]{:S(2)}) %all-to-all-start.1) | async-done | bytes 245792 | tf_op jit(solution)/shard_map/all_to_all | solution.py:297
  83.1 0.7 copy-done.8
  83.8 1.9 %pick_rows.1 = f32[320,128]{1,0:T(8,128)} custom-call(s32[64,1]{1,0:T(8,128)} %fusion.2.row_ref, bf16[192,640]{1,0:T(8,128)(2,1)} %bitcast.27), custom_call_target="tpu_custom_call" | custom-call | flops 16000000 | bytes 400000 | tf_op jit(solution)/shard_map/pick_rows/pallas_call | solution.py:230
  (6 shorter events, 0.1 us)
Async XLA Ops:
  0.0 4.1 %copy-start.2 = (bf16[64,24,3584]{2,1,0:T(8,128)(2,1)S(1)}, bf16[64,24,3584]{2,1,0:T(8,128)(2,1)}, u32[]{:S(2)}) copy-start(bf16[64,24,3584]{2,1,0:T(8,128)(2,1)} %param.6) | copy-start | bytes 33030148
  4.1 1.9 %copy-start.3 = (bf16[64,24,1024]{2,1,0:T(8,128)(2,1)S(1)}, bf16[64,24,1024]{2,1,0:T(8,128)(2,1)}, u32[]{:S(2)}) copy-start(bf16[64,24,1024]{2,1,0:T(8,128)(2,1)} %param.7) | copy-start | bytes 9437188
  6.0 1.0 %copy-start.4 = (bf16[3584,64]{0,1:T(8,128)(2,1)S(1)}, bf16[3584,64]{0,1:T(8,128)(2,1)}, u32[]{:S(2)}) copy-start(bf16[3584,64]{0,1:T(8,128)(2,1)} %param.8) | copy-start | bytes 1376260
  7.0 0.9 %copy-start.5 = (bf16[1024,64]{0,1:T(8,128)(2,1)S(1)}, bf16[1024,64]{0,1:T(8,128)(2,1)}, u32[]{:S(2)}) copy-start(bf16[1024,64]{0,1:T(8,128)(2,1)} %param.9) | copy-start | bytes 393220
  7.9 0.7 copy-start.6
  8.6 7.3 %copy-start.7 = (s32[64,1]{0,1:T(1,128)S(1)}, s32[64,1]{0,1:T(1,128)}, u32[]{:S(2)}) copy-start(s32[64,1]{0,1:T(1,128)} %param.11) | copy-start | bytes 772
  15.1 1.6 %collective-permute-start.1 = (f32[384,128]{1,0:T(8,128)S(1)}, f32[384,128]{1,0:T(8,128)S(1)}, u32[]{:S(2)}, u32[]{:S(2)}) collective-permute-start(f32[384,128]{1,0:T(8,128)S(1)} %get-tuple-element.10), channel_id=1, source_target_pairs={{0,1},{1,0},{2,3},{3,2},{4,5},{5,4},{6,7},{7,6},{8,9},{9,8},{10,11... | collective-permute-start | bytes 589832 | tf_op jit(solution)/shard_map/ppermute | solution.py:265
  15.6 5.4 %collective-permute-start = (f32[384,128]{1,0:T(8,128)S(1)}, f32[384,128]{1,0:T(8,128)S(1)}, u32[]{:S(2)}, u32[]{:S(2)}) collective-permute-start(f32[384,128]{1,0:T(8,128)S(1)} %get-tuple-element.9), channel_id=1, source_target_pairs={{0,1},{1,0},{2,3},{3,2},{4,5},{5,4},{6,7},{7,6},{8,9},{9,8},{10,11... | collective-permute-start | bytes 589832 | tf_op jit(solution)/shard_map/ppermute | solution.py:266
  17.4 8.1 %collective-permute-start.2 = (f32[384,128]{1,0:T(8,128)S(1)}, f32[384,128]{1,0:T(8,128)S(1)}, u32[]{:S(2)}, u32[]{:S(2)}) collective-permute-start(f32[384,128]{1,0:T(8,128)S(1)} %get-tuple-element.13), channel_id=1, source_target_pairs={{0,2},{1,3},{2,0},{3,1},{4,6},{5,7},{6,4},{7,5},{8,10},{9,11},{10,... | collective-permute-start | bytes 589832 | tf_op jit(solution)/shard_map/ppermute | solution.py:267
  21.0 4.5 %copy-start.9 = (f32[384,128]{1,0:T(8,128)}, f32[384,128]{1,0:T(8,128)S(1)}, u32[]{:S(2)}) copy-start(f32[384,128]{1,0:T(8,128)S(1)} %collective-permute-done.b_ref) | copy-start | bytes 589828
  25.5 0.7 copy-start.10
  45.1 7.1 %collective-permute-start.3 = (bf16[1280,128]{1,0:T(8,128)(2,1)S(1)}, bf16[1280,128]{1,0:T(8,128)(2,1)S(1)}, u32[]{:S(2)}, u32[]{:S(2)}) collective-permute-start(bf16[1280,128]{1,0:T(8,128)(2,1)S(1)} %bitcast.19), channel_id=1, source_target_pairs={{0,2},{1,3},{2,0},{3,1},{4,6},{5,7},{6,4},{7,5},{8,10},{9,11},{10,... | collective-permute-start | bytes 983048 | tf_op jit(solution)/shard_map/ppermute | solution.py:287
  46.6 5.9 %collective-permute-start.5 = (bf16[1280,128]{1,0:T(8,128)(2,1)S(1)}, bf16[1280,128]{1,0:T(8,128)(2,1)S(1)}, u32[]{:S(2)}, u32[]{:S(2)}) collective-permute-start(bf16[1280,128]{1,0:T(8,128)(2,1)S(1)} %bitcast.20), channel_id=1, source_target_pairs={{0,1},{1,0},{2,3},{3,2},{4,5},{5,4},{6,7},{7,6},{8,9},{9,8},{10,11... | collective-permute-start | bytes 983048 | tf_op jit(solution)/shard_map/ppermute | solution.py:288
  52.2 8.3 %collective-permute-start.4 = (bf16[1280,128]{1,0:T(8,128)(2,1)S(1)}, bf16[1280,128]{1,0:T(8,128)(2,1)S(1)}, u32[]{:S(2)}, u32[]{:S(2)}) collective-permute-start(bf16[1280,128]{1,0:T(8,128)(2,1)S(1)} %collective-permute-done.3.x0_ref), channel_id=1, source_target_pairs={{0,1},{1,0},{2,3},{3,2},{4,5},{5,4},{6,7},{7,6},{8,9},{9,8},{10,11... | collective-permute-start | bytes 983048 | tf_op jit(solution)/shard_map/ppermute | solution.py:289
  52.5 2.5 %copy-start = (bf16[1,640,4096]{2,1,0:T(8,128)(2,1)S(1)}, bf16[1,640,4096]{2,1,0:T(8,128)(2,1)}, u32[]{:S(2)}) copy-start(bf16[1,640,4096]{2,1,0:T(8,128)(2,1)} %param.10) | copy-start | bytes 15728644
  60.5 2.5 %copy-start.1 = (bf16[1,640,4096]{2,1,0:T(8,128)(2,1)S(1)}, bf16[1,640,4096]{2,1,0:T(8,128)(2,1)}, u32[]{:S(2)}) copy-start(bf16[1,640,4096]{2,1,0:T(8,128)(2,1)} %param.10) | copy-start | bytes 15728644
  68.9 14.2 %all-to-all-start.1 = ((bf16[8,24,640]{2,1,0:T(8,128)(2,1)}), bf16[8,24,640]{2,1,0:T(8,128)(2,1)S(1)}, u32[]{:S(2)}, u32[]{:S(2)}) async-start(bf16[8,24,640]{2,1,0:T(8,128)(2,1)} %bitcast.10), calls=%async_computation.1 | async-start | bytes 491520 | tf_op jit(solution)/shard_map/all_to_all | solution.py:297
  83.1 0.7 copy-start.8

commit v2 on v0

--- a/solution.py
+++ b/solution.py
@@ -1,12 +1,348 @@
+import functools
+
 import jax
 import jax.numpy as jnp
 from jax import lax
+from jax.experimental import pallas as pl
+from jax.experimental.pallas import tpu as pltpu
 from jax.sharding import PartitionSpec as P
 
 epsilon = 1e-06
-
-
-def local(activations, out_grads, proj_in, proj_out, queries, candidates):
+LANES = 128
+NT = (((1,), (1,)), ((), ()))
+TN = (((0,), (0,)), ((), ()))
+
+
+def project_kernel(
+    groups, ways, tokens, blocks, cand_hbm, act_hbm, grad_hbm, win_hbm, wout_hbm,
+    own_ref, over_ref, near_ref, far_ref,
+    act, grad, win, wout, raw, dealt, cand, rank, start, act_sems, grad_sems, sems,
+):
+    proj_rank = win.shape[0]
+    examples = cand.shape[1]
+    share = examples // ways
+    step = act.shape[0] // act_sems.shape[0]
+    me = lax.axis_index("tensor")
+
+    def piece(i):
+        return pl.ds(pl.multiple_of(i * step, step), step)
+
+    def act_copy(i):
+        return pltpu.make_async_copy(act_hbm.at[piece(i)], act.at[piece(i)], act_sems.at[i])
+
+    def grad_copy(i):
+        return pltpu.make_async_copy(grad_hbm.at[piece(i)], grad.at[piece(i)], grad_sems.at[i])
+
+    cand_copy = pltpu.make_async_copy(cand_hbm, cand, sems.at[0])
+    raw_copy = pltpu.make_async_copy(wout_hbm, raw, sems.at[1])
+    win_copy = pltpu.make_async_copy(win_hbm, win, sems.at[2])
+    cand_copy.start()
+    raw_copy.start()
+    win_copy.start()
+
+    @pl.loop(0, act_sems.shape[0])
+    def _(i):
+        act_copy(i).start()
+        grad_copy(i).start()
+
+    cand_copy.wait()
+
+    @pl.loop(0, groups)
+    def _(g):
+        start[g] = 0
+
+    @pl.loop(0, examples)
+    def _(e):
+        g = cand[0, e]
+        rank[e] = start[g]
+        start[g] = start[g] + 1
+
+    def shift(g, below):
+        here = start[g]
+        start[g] = below
+        return below + here
+
+    lax.fori_loop(0, groups, shift, jnp.int32(0))
+
+    half = proj_rank // 2
+    r = lax.broadcasted_iota(jnp.int32, (proj_rank, proj_rank), 0)
+    c = lax.broadcasted_iota(jnp.int32, (proj_rank, proj_rank), 1)
+    pick = (c == jnp.where(r < half, 2 * r, 2 * (r - half) + 1)).astype(jnp.bfloat16)
+    raw_copy.wait()
+    wout[...] = jnp.dot(pick, raw[...], preferred_element_type=jnp.float32).astype(jnp.bfloat16)
+    win_copy.wait()
+
+    done = 0
+    for count, rows in blocks:
+
+        @pl.loop(0, count)
+        def _(i, done=done, rows=rows):
+            for j in range(rows // step):
+                act_copy(done // step + i * (rows // step) + j).wait()
+                grad_copy(done // step + i * (rows // step) + j).wait()
+            at = pl.multiple_of(done + i * rows, step)
+            here = pl.ds(at, rows)
+            left = lax.dot_general(grad[here, :], wout[...], NT, preferred_element_type=jnp.float32)
+            right = lax.dot_general(act[here, :], win[...], NT, preferred_element_type=jnp.float32)
+            both = jnp.concatenate([left, right], axis=1)
+            first = done // tokens + i * (rows // tokens)
+            for k in range(rows // tokens):
+                e = first + k
+                place = start[cand[0, e]] + rank[e]
+                part = (place & (ways - 1)) ^ me
+                row = (part * share + place // ways) * tokens
+                dealt[pl.ds(pl.multiple_of(row, 8), tokens), :] = both[
+                    k * tokens : (k + 1) * tokens
+                ]
+
+        done += count * rows
+
+    size = share * tokens
+    for r, ref in enumerate((own_ref, near_ref, over_ref, far_ref)):
+        ref[...] = dealt[r * size : (r + 1) * size, :]
+
+
+def project(cands, act, grad, win, wout, tokens, groups, ways):
+    examples = cands.shape[1]
+    rows = act.shape[0]
+    pieces = 8
+    step = rows // pieces
+    blocks = ((3, 2 * step), (2, step))
+    share = rows // ways
+    hbm = pl.BlockSpec(memory_space=pltpu.HBM)
+    vmem = pl.BlockSpec(memory_space=pltpu.VMEM)
+    return pl.pallas_call(
+        functools.partial(project_kernel, groups, ways, tokens, blocks),
+        in_specs=[hbm] * 5,
+        out_specs=[vmem] * 4,
+        out_shape=[jax.ShapeDtypeStruct((share, LANES), jnp.float32)] * 4,
+        scratch_shapes=[
+            pltpu.VMEM(act.shape, jnp.bfloat16),
+            pltpu.VMEM(grad.shape, jnp.bfloat16),
+            pltpu.VMEM(win.shape, jnp.bfloat16),
+            pltpu.VMEM(wout.shape, jnp.bfloat16),
+            pltpu.VMEM(wout.shape, jnp.bfloat16),
+            pltpu.VMEM((rows, LANES), jnp.float32),
+            pltpu.SMEM((1, examples), jnp.int32),
+            pltpu.SMEM((examples,), jnp.int32),
+            pltpu.SMEM((groups,), jnp.int32),
+            pltpu.SemaphoreType.DMA((pieces,)),
+            pltpu.SemaphoreType.DMA((pieces,)),
+            pltpu.SemaphoreType.DMA((3,)),
+        ],
+        compiler_params=pltpu.CompilerParams(vmem_limit_bytes=61 << 20),
+        cost_estimate=pl.CostEstimate(
+            flops=2 * rows * (act.shape[1] + grad.shape[1]) * 64,
+            bytes_accessed=2 * rows * (act.shape[1] + grad.shape[1]),
+            transcendentals=0,
+        ),
+        name="project",
+    )(cands, act, grad, win, wout)
+
+
+def unit_kernel(tokens, chunks, row_ref, a_ref, b_ref, out_ref, total):
+    total[...] = a_ref[...] + b_ref[...]
+    out_ref[...] = jnp.zeros_like(out_ref)
+    count = total.shape[0] // tokens
+    half = LANES // 2
+    width = chunks * LANES
+    low = lax.broadcasted_iota(jnp.int32, (chunks, LANES), 1) < half
+    low_t = lax.broadcasted_iota(jnp.int32, (tokens, LANES), 1) < half
+
+    @pl.loop(0, count, unroll=4)
+    def _(i):
+        part = total[pl.ds(pl.multiple_of(i * tokens, 8), tokens), :]
+        twice = jnp.where(low_t, pltpu.roll(part, half, 1), part)
+        g_hi = part.astype(jnp.bfloat16).astype(jnp.float32)
+        a_hi = twice.astype(jnp.bfloat16).astype(jnp.float32)
+        left = jnp.concatenate([g_hi, g_hi, part - g_hi], axis=0)[:, :half].astype(jnp.bfloat16)
+        right = jnp.concatenate([a_hi, twice - a_hi, a_hi], axis=0).astype(jnp.bfloat16)
+        prod = lax.dot_general(left, right, TN, preferred_element_type=jnp.float32)
+        entries = jnp.where(low, prod[:chunks], prod[chunks : 2 * chunks])
+        square = jnp.sum(entries * entries, axis=0, keepdims=True)
+        mean = jnp.sum(square, axis=1, keepdims=True) / width
+        unit = (entries * lax.rsqrt(mean + epsilon)).astype(jnp.bfloat16)
+        row = pl.multiple_of(row_ref[i] * chunks, chunks)
+        out_ref[pl.ds(row, chunks), :] = unit
+
+
+def unit_grads(slots, a, b, tokens, chunks, slot_count):
+    whole = pl.BlockSpec(memory_space=pltpu.VMEM)
+    return pl.pallas_call(
+        functools.partial(unit_kernel, tokens, chunks),
+        in_specs=[pl.BlockSpec(memory_space=pltpu.SMEM), whole, whole],
+        out_specs=whole,
+        out_shape=jax.ShapeDtypeStruct((slot_count * chunks, LANES), jnp.bfloat16),
+        scratch_shapes=[pltpu.VMEM(a.shape, jnp.float32)],
+        compiler_params=pltpu.CompilerParams(vmem_limit_bytes=16 << 20),
+        cost_estimate=pl.CostEstimate(flops=20_000_000, bytes_accessed=1_000_000, transcendentals=0),
+        name="unit_grads",
+    )(slots, a, b)
+
+
+def score_kernel(groups, slots, padded, first, chunks, parts, x0_ref, x1_ref, q_hbm, *rest):
+    prev_ref = rest[0] if first else None
+    out_ref, stage, units, queries, total, sems = rest[1 if first else 0 :]
+    each = chunks // parts
+    width = each * LANES
+    span = slots * chunks
+    after = padded - first - 2 * slots
+
+    def load(k):
+        columns = pl.ds(pl.multiple_of(k * width, width), width)
+        return pltpu.make_async_copy(q_hbm.at[:, columns], queries.at[k], sems.at[k])
+
+    for k in range(parts):
+        load(k).start()
+
+    @pl.loop(0, groups)
+    def _(d):
+        base = d * padded * each
+        for k in range(parts):
+            if first:
+                stage[k, pl.ds(base, first * each), :] = jnp.zeros(
+                    (first * each, LANES), jnp.float32
+                )
+            stage[k, pl.ds(base + (first + 2 * slots) * each, after * each), :] = jnp.zeros(
+                (after * each, LANES), jnp.float32
+            )
+        for n, x_ref in enumerate((x0_ref, x1_ref)):
+            got = x_ref[pl.ds(pl.multiple_of(d * span, span), span), :].astype(jnp.float32)
+            got = got.reshape(slots, parts, each, LANES)
+            for k in range(parts):
+                at = pl.ds(base + (first + n * slots) * each, slots * each)
+                stage[k, at, :] = got[:, k].reshape(slots * each, LANES)
+
+    rows = groups * padded
+    total[...] = jnp.zeros_like(total)
+
+    @pl.loop(0, parts)
+    def _(k):
+        for j in range(each):
+            piece = stage[k, pl.ds(j, rows, stride=each), :]
+            units[:, j * LANES : (j + 1) * LANES] = piece.astype(jnp.bfloat16)
+        load(k).wait()
+        total[...] += lax.dot_general(
+            queries[k], units[...], NT, preferred_element_type=jnp.float32
+        )
+
+    out = total[...].T
+    if first:
+        out = out + prev_ref[...]
+    out_ref[...] = out.astype(out_ref.dtype)
+
+
+def scores_of(x0, x1, queries, prev, groups, slots, padded, first):
+    parts = 4
+    count, width = queries.shape[0], queries.shape[1] // parts
+    chunks = queries.shape[1] // LANES
+    rows = groups * padded
+    vmem = pl.BlockSpec(memory_space=pltpu.VMEM)
+    return pl.pallas_call(
+        functools.partial(score_kernel, groups, slots, padded, first, chunks, parts),
+        in_specs=[vmem, vmem, pl.BlockSpec(memory_space=pltpu.HBM)] + ([vmem] if first else []),
+        out_specs=vmem,
+        out_shape=jax.ShapeDtypeStruct((rows, count), jnp.bfloat16 if first else jnp.float32),
+        scratch_shapes=[
+            pltpu.VMEM((parts, rows * (chunks // parts), LANES), jnp.float32),
+            pltpu.VMEM((rows, width), jnp.bfloat16),
+            pltpu.VMEM((parts, count, width), jnp.bfloat16),
+            pltpu.VMEM((count, rows), jnp.float32),
+            pltpu.SemaphoreType.DMA((parts,)),
+        ],
+        compiler_params=pltpu.CompilerParams(vmem_limit_bytes=50 << 20),
+        cost_estimate=pl.CostEstimate(
+            flops=2 * rows * queries.size, bytes_accessed=2 * queries.size, transcendentals=0
+        ),
+        name="scores",
+    )(x0, x1, queries, *([prev] if first else []))
+
+
+def pick_kernel(row_ref, x_ref, out_ref):
+    count = row_ref.shape[0]
+    rows = x_ref.shape[0]
+    parts = x_ref.shape[1] // LANES
+    hit = lax.broadcasted_iota(jnp.int32, (count, rows), 1) == row_ref[...]
+    pick = jnp.where(hit, 1.0, 0.0).astype(jnp.bfloat16)
+    got = jnp.dot(pick, x_ref[...], preferred_element_type=jnp.float32)
+    for j in range(parts):
+        out_ref[pl.ds(j, count, stride=parts), :] = got[:, j * LANES : (j + 1) * LANES]
+
+
+def pick_rows(row, x):
+    vmem = pl.BlockSpec(memory_space=pltpu.VMEM)
+    count, width = row.shape[0], x.shape[1]
+    return pl.pallas_call(
+        pick_kernel,
+        in_specs=[vmem, vmem],
+        out_specs=vmem,
+        out_shape=jax.ShapeDtypeStruct((count * (width // LANES), LANES), jnp.float32),
+        compiler_params=pltpu.CompilerParams(vmem_limit_bytes=16 << 20),
+        cost_estimate=pl.CostEstimate(flops=16_000_000, bytes_accessed=400_000, transcendentals=0),
+        name="pick_rows",
+    )(row, x)
+
+
+def local_one(activations, out_grads, proj_in, proj_out, queries, candidates):
+    examples, tokens, hidden = activations.shape
+    features = out_grads.shape[2]
+    groups = lax.axis_size("dp")
+    ways = lax.axis_size("tensor")
+    me = lax.axis_index("tensor")
+    capacity = max(2, 5 * examples // (2 * groups))
+    slots = -(-capacity // ways)
+    padded = -(-ways * slots // 8) * 8
+    query_block = queries[0]
+    chunks = query_block.shape[1] // LANES
+    core = [(i, i ^ 1) for i in range(ways)]
+    across = [(i, i ^ 2) for i in range(ways)]
+
+    cands = candidates.reshape(-1)
+    own_part, over_part, near_part, far_part = project(
+        candidates.reshape(1, examples),
+        activations.reshape(examples * tokens, hidden),
+        out_grads.reshape(examples * tokens, features),
+        proj_in.T,
+        proj_out.T,
+        tokens,
+        groups,
+        ways,
+    )
+    far_in = lax.ppermute(far_part, "tensor", core)
+    near_in = lax.ppermute(near_part, "tensor", core)
+    across_in = lax.ppermute(over_part + far_in, "tensor", across)
+
+    number = jnp.arange(examples, dtype=jnp.int32)
+    before = (cands[None, :] < cands[:, None]) | (
+        (cands[None, :] == cands[:, None]) & (number[None, :] < number[:, None])
+    )
+    place = jnp.sum(before.astype(jnp.int32), axis=1)
+    start = jnp.sum((cands[None, :] < cands[:, None]).astype(jnp.int32), axis=1)
+    owner = place % ways
+    slot = place // ways - (start + ways - 1 - owner) // ways
+    mine = (
+        place[None, :] == ways * jnp.arange(examples // ways, dtype=jnp.int32)[:, None] + me
+    )
+    my_slots = jnp.sum(jnp.where(mine, (cands * slots + slot)[None, :], 0), axis=1)
+    pick = (cands * padded + (owner ^ me) * slots + slot)[:, None]
+
+    units = unit_grads(my_slots, own_part + near_in, across_in, tokens, chunks, groups * slots)
+    shape = (groups, slots * chunks, LANES)
+    own = lax.all_to_all(units.reshape(shape), "dp", split_axis=0, concat_axis=0, tiled=True)
+    own = own.reshape(units.shape)
+    over_y = lax.ppermute(own, "tensor", across)
+    over_core = lax.ppermute(own, "tensor", core)
+    first = scores_of(own, over_core, query_block, None, groups, slots, padded, 0)
+    over_y, first = lax.optimization_barrier((over_y, first))
+    over_both = lax.ppermute(over_y, "tensor", core)
+    both = scores_of(over_y, over_both, query_block, first, groups, slots, padded, 2 * slots)
+    block = both.reshape(groups, padded, both.shape[1])
+    returned = lax.all_to_all(block, "dp", split_axis=0, concat_axis=0, tiled=True)
+    picked = pick_rows(pick, returned.reshape(both.shape))
+    return picked.reshape(examples, 1, both.shape[1])
+
+
+def local_many(activations, out_grads, proj_in, proj_out, queries, candidates):
     examples_here, tokens_here, hidden_here = activations.shape
     proj_rank = proj_in.shape[1]
     per_example = candidates.shape[1]
@@ -32,7 +368,7 @@
         "eta,etb->eab", grad_side, act_side, precision=lax.Precision.HIGHEST
     ).reshape(examples_here, proj_rank * proj_rank)
     inv_rms = lax.rsqrt(jnp.mean(example_grads * example_grads, axis=1, keepdims=True) + epsilon)
-    unit_grads = (example_grads * inv_rms).astype(jnp.bfloat16)
+    unit = (example_grads * inv_rms).astype(jnp.bfloat16)
     flat_cands = candidates.reshape(-1)
     hit_table = (flat_cands[:, None] == jnp.arange(groups, dtype=jnp.int32)[None, :]).astype(
         jnp.int32
@@ -40,13 +376,12 @@
     earlier = jnp.cumsum(hit_table, axis=0) - hit_table
     slot_index = jnp.sum(earlier * hit_table, axis=1)
     dest_index = flat_cands * capacity + slot_index
-    row_copies = jnp.repeat(unit_grads, per_example, axis=0)
-    grad_width = unit_grads.shape[1]
+    row_copies = jnp.repeat(unit, per_example, axis=0)
+    grad_width = unit.shape[1]
     send_buffer = (
         jnp.zeros((groups * capacity, grad_width), jnp.bfloat16).at[dest_index].set(row_copies)
     )
     send_buffer = send_buffer.reshape(groups, capacity, grad_width)
-    query_block = queries[0]
     col_width = grad_width // lax.axis_size("tensor")
     column_part = lax.dynamic_slice_in_dim(
         send_buffer, lax.axis_index("tensor") * col_width, col_width, 2
@@ -55,12 +390,19 @@
     slot_scores = jnp.einsum(
         "gsk,qk->gsq",
         lax.all_gather(received, "tensor", axis=2, tiled=True),
-        query_block,
+        queries[0],
         preferred_element_type=jnp.float32,
     )
     returned = lax.all_to_all(slot_scores, "dp", split_axis=0, concat_axis=0, tiled=True)
     picked = returned.reshape(groups * capacity, returned.shape[2])[dest_index]
     return picked.reshape(examples_here, per_example, returned.shape[2])
+
+
+def local(activations, out_grads, proj_in, proj_out, queries, candidates):
+    one = candidates.shape[1] == 1 and lax.axis_size("tensor") == 4
+    return (local_one if one else local_many)(
+        activations, out_grads, proj_in, proj_out, queries, candidates
+    )
 
 
 def solution(mesh):

time: 144 us -> 67.5 us (0.47)
  waiting for transfers between devices: 68.8 us -> 19.9 us
  matrix products: 21.4 us -> 0 us
  Pallas kernels: 0 us -> 19.7 us
  between operations: 13.5 us -> 0.07 us
  local copies, waits for them, and re-layouts: 12.9 us -> 0.36 us
  starting transfers between devices: 5.56 us -> 8.49 us
  other arithmetic: 5.23 us -> 2.37 us
    psum x1 -> x0, waiting for transfers between devices: 37.1 us -> none  [local(): summed = lax.psum(both_proj, 'tensor')]
    dot_general x4 -> x0, matrix products: 21.4 us -> none  [the longest x1 7.7 us: local(): jnp.dot(activations.reshape(examples_here * tokens_here, hidden_here), pr...]
    pallas_call x0 -> x5, Pallas kernels: none -> 19.7 us  [the longest x2 8.96 us: scores_of(): pl.pallas_call(functools.partial(score_kernel, groups, slots, padded, fir...]
    all_gather x1 -> x0, waiting for transfers between devices: 18 us -> none  [local(): lax.all_gather(received, 'tensor', axis=2, tiled=True)]
    ppermute x0 -> x6, waiting for transfers between devices: none -> 10.9 us  [the longest x1 4.35 us: local_one(): over_y = lax.ppermute(own, 'tensor', across)]
    reshape x4 -> x0, local copies, waits for them, and re-layouts: 8.1 us -> none  [the longest x1 2.9 us: local(): example_grads = jnp.einsum('eta,etb->eab', grad_side, act_side, precision...]
    ppermute x0 -> x6, starting transfers between devices: none -> 5.07 us  [the longest x1 2.95 us: local_one(): across_in = lax.ppermute(over_part + far_in, 'tensor', across)]
    all_to_all x1, waiting for transfers between devices: 13.7 us -> 8.93 us  [local_one(): lax.all_to_all(block, 'dp', split_axis=0, concat_axis=0, tiled=True)]
  transfers between devices with their start and end apart: 3 -> 7, of which waited for: 3 -> 6; matrix products, arithmetic and copies ran while one was open for 1% -> 4% of each run, Pallas kernels for 0% -> 6%
where the time goes in v2:
time: 67.5 us; the launch traced here: 67.2 us
  waiting for transfers between devices  19.9 us (29%)
  Pallas kernels  19.7 us (29%)
  blocking collectives  16.3 us (24%)
  starting transfers between devices  8.49 us (13%)
  other arithmetic  2.37 us (4%)
    all_to_all x1, blocking collectives, local_one(): lax.all_to_all(units.reshape(shape), 'dp', split_axis=0, concat_axis=0, t...  16.3 us
    pallas_call x2, Pallas kernels, scores_of(): pl.pallas_call(functools.partial(score_kernel, groups, slots, padded, fir...  8.96 us
    all_to_all x1, waiting for transfers between devices, local_one(): lax.all_to_all(block, 'dp', split_axis=0, concat_axis=0, tiled=True)  8.93 us
    pallas_call x1, Pallas kernels, project(): pl.pallas_call(functools.partial(project_kernel, groups, ways, tokens, bl...  7.98 us
    ppermute x1, waiting for transfers between devices, local_one(): over_y = lax.ppermute(own, 'tensor', across)  4.35 us
    ppermute x1, waiting for transfers between devices, local_one(): across_in = lax.ppermute(over_part + far_in, 'tensor', across)  4.06 us
    all_to_all x1, starting transfers between devices, local_one(): lax.all_to_all(block, 'dp', split_axis=0, concat_axis=0, tiled=True)  3.42 us
    ppermute x1, starting transfers between devices, local_one(): across_in = lax.ppermute(over_part + far_in, 'tensor', across)  2.95 us
  transfers between devices with their start and end apart: 7, of which 6 were waited for; matrix products, arithmetic and copies ran while one was open for 4% of the time, Pallas kernels for 6%

profile of v2, /device:TPU:0, one launch (start us, length us, event | category | flops | bytes accessed | tf_op | source)
XLA Modules:
  0.0 67.2 jit_solution(6671892353298860082)
XLA Ops:
  0.0 0.0 copy-start
  0.0 8.0 %project.1 = (f32[384,128]{1,0:T(8,128)}, f32[384,128]{1,0:T(8,128)}, f32[384,128]{1,0:T(8,128)}, f32[384,128]{1,0:T(8,128)}) custom-call(s32[1,64]{1,0:T(1,128)} %bitcast.27, bf16[1536,3584]{1,0:T(8,128)(2,1)} %bitcast.23, bf16[1536,1024]{1,0:T(8,128)(2,1)} %bitcast.24, bf16[64,3584]{1,0:T(8,128)(2,1)} %bitcast.25, bf16[64,1024]{1,0:T(8,128)(2,1)} %bitcast.26), custom_call_target="tpu_custom_call" | custom-call | flops 905969664 | bytes 14155776 | tf_op jit(solution)/shard_map/project/pallas_call | solution.py:114
  8.0 0.5 collective-permute-start.1
  8.5 0.1 collective-permute-start
  8.6 0.0 copy-done
  8.6 0.2 fusion
  8.8 1.0 %collective-permute-done.1 = f32[384,128]{1,0:T(8,128)S(1)} collective-permute-done((f32[384,128]{1,0:T(8,128)}, f32[384,128]{1,0:T(8,128)S(1)}, u32[]{:S(2)}, u32[]{:S(2)}) %collective-permute-start.1) | collective-permute-done | bytes 196640 | tf_op jit(solution)/shard_map/ppermute | solution.py:311
  9.8 0.9 %add.107 = f32[384,128]{1,0:T(8,128)S(1)} add(f32[384,128]{1,0:T(8,128)} %get-tuple-element.13, f32[384,128]{1,0:T(8,128)S(1)} %collective-permute-done.1) | non-fusion elementwise | flops 49152 | bytes 589824 | tf_op jit(solution)/shard_map/add | solution.py:313
  10.7 3.0 %collective-permute-start.2 = (f32[384,128]{1,0:T(8,128)S(1)}, f32[384,128]{1,0:T(8,128)S(1)}, u32[]{:S(2)}, u32[]{:S(2)}) collective-permute-start(f32[384,128]{1,0:T(8,128)S(1)} %add.107), channel_id=1, source_target_pairs={{0,2},{1,3},{2,0},{3,1},{4,6},{5,7},{6,4},{7,5},{8,10},{9,11},{10,... | collective-permute-start | bytes 589832 | tf_op jit(solution)/shard_map/ppermute | solution.py:313
  13.7 0.2 select_reduce_fusion.row_ref
  13.9 0.0 collective-permute-done
  13.9 1.0 %add.106.a_ref = f32[384,128]{1,0:T(8,128)S(1)} add(f32[384,128]{1,0:T(8,128)} %get-tuple-element.11, f32[384,128]{1,0:T(8,128)S(1)} %collective-permute-done) | non-fusion elementwise | flops 49152 | bytes 589824 | tf_op jit(solution)/shard_map/add | solution.py:329
  14.8 4.1 %collective-permute-done.2.b_ref = f32[384,128]{1,0:T(8,128)S(1)} collective-permute-done((f32[384,128]{1,0:T(8,128)S(1)}, f32[384,128]{1,0:T(8,128)S(1)}, u32[]{:S(2)}, u32[]{:S(2)}) %collective-permute-start.2) | collective-permute-done | bytes 196640 | tf_op jit(solution)/shard_map/ppermute | solution.py:313
  18.9 1.9 %unit_grads.1 = bf16[1280,128]{1,0:T(8,128)(2,1)S(1)} custom-call(s32[16]{0:T(128)S(1)} %select_reduce_fusion.row_ref, f32[384,128]{1,0:T(8,128)S(1)} %add.106.a_ref, f32[384,128]{1,0:T(8,128)S(1)} %collective-permute-done.2.b_ref), custom_call_target="tpu_custom_call" | custom-call | flops 20000000 | bytes 1000000 | tf_op jit(solution)/shard_map/unit_grads/pallas_call | solution.py:171
  20.8 16.3 %all_to_all.10 = bf16[8,160,128]{2,1,0:T(8,128)(2,1)S(1)} all-to-all(bf16[8,160,128]{2,1,0:T(8,128)(2,1)S(1)} %bitcast.19), channel_id=1, replica_groups=mesh['dp'=8,'tensor'=4] {'dp'}, dimensions={0} | all-to-all | bytes 655360 | tf_op jit(solution)/shard_map/all_to_all | solution.py:331
  37.1 0.0 collective-permute-start.4
  37.1 1.5 %collective-permute-start.3 = (bf16[1280,128]{1,0:T(8,128)(2,1)S(1)}, bf16[1280,128]{1,0:T(8,128)(2,1)S(1)}, u32[]{:S(2)}, u32[]{:S(2)}) collective-permute-start(bf16[1280,128]{1,0:T(8,128)(2,1)S(1)} %bitcast.17), channel_id=1, source_target_pairs={{0,2},{1,3},{2,0},{3,1},{4,6},{5,7},{6,4},{7,5},{8,10},{9,11},{10,... | collective-permute-start | bytes 983048 | tf_op jit(solution)/shard_map/ppermute | solution.py:333
  38.6 0.1 collective-permute-done.4.x1_ref
  38.7 4.1 %scores.2.rest_0_ = f32[192,640]{1,0:T(8,128)S(1)} custom-call(bf16[1280,128]{1,0:T(8,128)(2,1)S(1)} %bitcast.18, bf16[1280,128]{1,0:T(8,128)(2,1)S(1)} %collective-permute-done.4.x1_ref, bf16[640,4096]{1,0:T(8,128)(2,1)} %bitcast.21), custom_call_target="tpu_custom_call" | custom-call | flops 1006632960 | bytes 5242880 | tf_op jit(solution)/shard_map/scores/pallas_call | solution.py:241
  42.8 4.3 %collective-permute-done.3.x0_ref = bf16[1280,128]{1,0:T(8,128)(2,1)S(1)} collective-permute-done((bf16[1280,128]{1,0:T(8,128)(2,1)S(1)}, bf16[1280,128]{1,0:T(8,128)(2,1)S(1)}, u32[]{:S(2)}, u32[]{:S(2)}) %collective-permute-start.3) | collective-permute-done | bytes 327712 | tf_op jit(solution)/shard_map/ppermute | solution.py:333
  47.2 0.0 collective-permute-start.5
  47.2 0.1 copy.25
  47.3 0.1 copy.29
  47.4 1.4 %collective-permute-done.5.x1_ref = bf16[1280,128]{1,0:T(8,128)(2,1)S(1)} collective-permute-done((bf16[1280,128]{1,0:T(8,128)(2,1)S(1)}, bf16[1280,128]{1,0:T(8,128)(2,1)S(1)}, u32[]{:S(2)}, u32[]{:S(2)}) %collective-permute-start.5) | collective-permute-done | bytes 327712 | tf_op jit(solution)/shard_map/ppermute | solution.py:337
  48.8 4.8 %scores.3 = bf16[192,640]{1,0:T(8,128)(2,1)} custom-call(bf16[1280,128]{1,0:T(8,128)(2,1)S(1)} %collective-permute-done.3.x0_ref, bf16[1280,128]{1,0:T(8,128)(2,1)S(1)} %collective-permute-done.5.x1_ref, bf16[640,4096]{1,0:T(8,128)(2,1)} %bitcast.22, f32[192,640]{1,0:T(8,128)S(1)} %scores.2.rest_0_), custom_call_target="tpu_custom_call" | custom-call | flops 1006632960 | bytes 5242880 | tf_op jit(solution)/shard_map/scores/pallas_call | solution.py:241
  53.6 3.4 %all-to-all-start.1 = ((bf16[8,24,640]{2,1,0:T(8,128)(2,1)}), bf16[8,24,640]{2,1,0:T(8,128)(2,1)S(1)}, u32[]{:S(2)}, u32[]{:S(2)}) async-start(bf16[8,24,640]{2,1,0:T(8,128)(2,1)} %bitcast.11), calls=%async_computation.1 | async-start | bytes 491520 | tf_op jit(solution)/shard_map/all_to_all | solution.py:340
  57.1 0.1 copy.32
  57.2 0.1 copy.31
  57.3 0.1 fusion.2.row_ref
  57.3 8.9 %all-to-all-done.1 = bf16[8,24,640]{2,1,0:T(8,128)(2,1)S(1)} async-done(((bf16[8,24,640]{2,1,0:T(8,128)(2,1)}), bf16[8,24,640]{2,1,0:T(8,128)(2,1)S(1)}, u32[]{:S(2)}, u32[]{:S(2)}) %all-to-all-start.1) | async-done | bytes 245792 | tf_op jit(solution)/shard_map/all_to_all | solution.py:340
  66.3 0.9 %pick_rows.1 = f32[320,128]{1,0:T(8,128)} custom-call(s32[64,1]{1,0:T(8,128)S(1)} %fusion.2.row_ref, bf16[192,640]{1,0:T(8,128)(2,1)S(1)} %bitcast.20), custom_call_target="tpu_custom_call" | custom-call | flops 16000000 | bytes 400000 | tf_op jit(solution)/shard_map/pick_rows/pallas_call | solution.py:275
  (4 shorter events, 0.1 us)
Async XLA Ops:
  0.0 8.6 %copy-start = (s32[64,1]{0,1:T(1,128)S(1)}, s32[64,1]{0,1:T(1,128)}, u32[]{:S(2)}) copy-start(s32[64,1]{0,1:T(1,128)} %param.11) | copy-start | bytes 772
  8.0 1.8 %collective-permute-start.1 = (f32[384,128]{1,0:T(8,128)}, f32[384,128]{1,0:T(8,128)S(1)}, u32[]{:S(2)}, u32[]{:S(2)}) collective-permute-start(f32[384,128]{1,0:T(8,128)} %get-tuple-element.14), channel_id=1, source_target_pairs={{0,1},{1,0},{2,3},{3,2},{4,5},{5,4},{6,7},{7,6},{8,9},{9,8},{10,11... | collective-permute-start | bytes 589832 | tf_op jit(solution)/shard_map/ppermute | solution.py:311
  8.5 5.4 %collective-permute-start = (f32[384,128]{1,0:T(8,128)}, f32[384,128]{1,0:T(8,128)S(1)}, u32[]{:S(2)}, u32[]{:S(2)}) collective-permute-start(f32[384,128]{1,0:T(8,128)} %get-tuple-element.12), channel_id=1, source_target_pairs={{0,1},{1,0},{2,3},{3,2},{4,5},{5,4},{6,7},{7,6},{8,9},{9,8},{10,11... | collective-permute-start | bytes 589832 | tf_op jit(solution)/shard_map/ppermute | solution.py:312
  10.7 8.2 %collective-permute-start.2 = (f32[384,128]{1,0:T(8,128)S(1)}, f32[384,128]{1,0:T(8,128)S(1)}, u32[]{:S(2)}, u32[]{:S(2)}) collective-permute-start(f32[384,128]{1,0:T(8,128)S(1)} %add.107), channel_id=1, source_target_pairs={{0,2},{1,3},{2,0},{3,1},{4,6},{5,7},{6,4},{7,5},{8,10},{9,11},{10,... | collective-permute-start | bytes 589832 | tf_op jit(solution)/shard_map/ppermute | solution.py:313
  37.1 1.6 %collective-permute-start.4 = (bf16[1280,128]{1,0:T(8,128)(2,1)S(1)}, bf16[1280,128]{1,0:T(8,128)(2,1)S(1)}, u32[]{:S(2)}, u32[]{:S(2)}) collective-permute-start(bf16[1280,128]{1,0:T(8,128)(2,1)S(1)} %bitcast.16), channel_id=1, source_target_pairs={{0,1},{1,0},{2,3},{3,2},{4,5},{5,4},{6,7},{7,6},{8,9},{9,8},{10,11... | collective-permute-start | bytes 983048 | tf_op jit(solution)/shard_map/ppermute | solution.py:334
  37.1 10.1 %collective-permute-start.3 = (bf16[1280,128]{1,0:T(8,128)(2,1)S(1)}, bf16[1280,128]{1,0:T(8,128)(2,1)S(1)}, u32[]{:S(2)}, u32[]{:S(2)}) collective-permute-start(bf16[1280,128]{1,0:T(8,128)(2,1)S(1)} %bitcast.17), channel_id=1, source_target_pairs={{0,2},{1,3},{2,0},{3,1},{4,6},{5,7},{6,4},{7,5},{8,10},{9,11},{10,... | collective-permute-start | bytes 983048 | tf_op jit(solution)/shard_map/ppermute | solution.py:333
  47.2 1.6 %collective-permute-start.5 = (bf16[1280,128]{1,0:T(8,128)(2,1)S(1)}, bf16[1280,128]{1,0:T(8,128)(2,1)S(1)}, u32[]{:S(2)}, u32[]{:S(2)}) collective-permute-start(bf16[1280,128]{1,0:T(8,128)(2,1)S(1)} %collective-permute-done.3.x0_ref), channel_id=1, source_target_pairs={{0,1},{1,0},{2,3},{3,2},{4,5},{5,4},{6,7},{7,6},{8,9},{9,8},{10,11... | collective-permute-start | bytes 983048 | tf_op jit(solution)/shard_map/ppermute | solution.py:337
  53.6 12.6 %all-to-all-start.1 = ((bf16[8,24,640]{2,1,0:T(8,128)(2,1)}), bf16[8,24,640]{2,1,0:T(8,128)(2,1)S(1)}, u32[]{:S(2)}, u32[]{:S(2)}) async-start(bf16[8,24,640]{2,1,0:T(8,128)(2,1)} %bitcast.11), calls=%async_computation.1 | async-start | bytes 491520 | tf_op jit(solution)/shard_map/all_to_all | solution.py:340

commit v3 on v2

--- a/solution.py
+++ b/solution.py
@@ -14,8 +14,9 @@
 
 
 def project_kernel(
-    groups, ways, tokens, blocks, cand_hbm, act_hbm, grad_hbm, win_hbm, wout_hbm,
-    own_ref, over_ref, near_ref, far_ref,
+    groups, ways, tokens, slots, padded, blocks,
+    cand_hbm, act_hbm, grad_hbm, win_hbm, wout_hbm,
+    own_ref, over_ref, near_ref, far_ref, slot_ref, pick_ref,
     act, grad, win, wout, raw, dealt, cand, rank, start, act_sems, grad_sems, sems,
 ):
     proj_rank = win.shape[0]
@@ -88,9 +89,15 @@
             first = done // tokens + i * (rows // tokens)
             for k in range(rows // tokens):
                 e = first + k
-                place = start[cand[0, e]] + rank[e]
-                part = (place & (ways - 1)) ^ me
-                row = (part * share + place // ways) * tokens
+                g = cand[0, e]
+                place = start[g] + rank[e]
+                owner = place & (ways - 1)
+                turn = place >> (ways.bit_length() - 1)
+                before = (start[g] + ways - 1 - owner) >> (ways.bit_length() - 1)
+                rel = owner ^ me
+                slot_ref[rel * share + turn] = g * slots + turn - before
+                pick_ref[0, e] = g * padded + rel * slots + turn - before
+                row = (rel * share + turn) * tokens
                 dealt[pl.ds(pl.multiple_of(row, 8), tokens), :] = both[
                     k * tokens : (k + 1) * tokens
                 ]
@@ -102,7 +109,7 @@
         ref[...] = dealt[r * size : (r + 1) * size, :]
 
 
-def project(cands, act, grad, win, wout, tokens, groups, ways):
+def project(cands, act, grad, win, wout, tokens, groups, ways, slots, padded):
     examples = cands.shape[1]
     rows = act.shape[0]
     pieces = 8
@@ -112,10 +119,14 @@
     hbm = pl.BlockSpec(memory_space=pltpu.HBM)
     vmem = pl.BlockSpec(memory_space=pltpu.VMEM)
     return pl.pallas_call(
-        functools.partial(project_kernel, groups, ways, tokens, blocks),
+        functools.partial(project_kernel, groups, ways, tokens, slots, padded, blocks),
         in_specs=[hbm] * 5,
-        out_specs=[vmem] * 4,
-        out_shape=[jax.ShapeDtypeStruct((share, LANES), jnp.float32)] * 4,
+        out_specs=[vmem] * 4 + [pl.BlockSpec(memory_space=pltpu.SMEM)] * 2,
+        out_shape=[jax.ShapeDtypeStruct((share, LANES), jnp.float32)] * 4
+        + [
+            jax.ShapeDtypeStruct((examples,), jnp.int32),
+            jax.ShapeDtypeStruct((1, examples), jnp.int32),
+        ],
         scratch_shapes=[
             pltpu.VMEM(act.shape, jnp.bfloat16),
             pltpu.VMEM(grad.shape, jnp.bfloat16),
@@ -138,6 +149,31 @@
         ),
         name="project",
     )(cands, act, grad, win, wout)
+
+
+def own_kernel(slot_ref, a_ref, b_ref, out_slot_ref, out_ref):
+    out_ref[...] = a_ref[...] + b_ref[...]
+
+    @pl.loop(0, out_slot_ref.shape[0])
+    def _(i):
+        out_slot_ref[i] = slot_ref[i]
+
+
+def own_sum(slots, a, b, count):
+    smem = pl.BlockSpec(memory_space=pltpu.SMEM)
+    vmem = pl.BlockSpec(memory_space=pltpu.VMEM)
+    return pl.pallas_call(
+        own_kernel,
+        in_specs=[smem, vmem, vmem],
+        out_specs=[smem, vmem],
+        out_shape=[
+            jax.ShapeDtypeStruct((count,), jnp.int32),
+            jax.ShapeDtypeStruct(a.shape, a.dtype),
+        ],
+        compiler_params=pltpu.CompilerParams(vmem_limit_bytes=16 << 20),
+        cost_estimate=pl.CostEstimate(flops=a.size, bytes_accessed=12 * a.size, transcendentals=0),
+        name="own_sum",
+    )(slots, a, b)
 
 
 def unit_kernel(tokens, chunks, row_ref, a_ref, b_ref, out_ref, total):
@@ -180,90 +216,127 @@
     )(slots, a, b)
 
 
-def score_kernel(groups, slots, padded, first, chunks, parts, x0_ref, x1_ref, q_hbm, *rest):
-    prev_ref = rest[0] if first else None
-    out_ref, stage, units, queries, total, sems = rest[1 if first else 0 :]
-    each = chunks // parts
-    width = each * LANES
-    span = slots * chunks
-    after = padded - first - 2 * slots
+def stage_units(refs, stage, parts, slots, groups):
+    each = stage.shape[1] // (len(refs) * groups * slots)
+    span = slots * parts * each
+
+    @pl.loop(0, groups)
+    def _(d):
+        for n, ref in enumerate(refs):
+            got = ref[pl.ds(pl.multiple_of(d * span, span), span), :].astype(jnp.float32)
+            got = got.reshape(slots, parts, each, LANES)
+            for k in range(parts):
+                at = pl.multiple_of((n * groups + d) * slots * each, each)
+                stage[k, pl.ds(at, slots * each), :] = got[:, k].reshape(slots * each, LANES)
+
+
+def staged_rows(stage, k, units, at):
+    rows = units.shape[0] - at
+    each = units.shape[1] // LANES
+    for j in range(each):
+        piece = stage[k, pl.ds(j, rows, stride=each), :]
+        units[at:, j * LANES : (j + 1) * LANES] = piece.astype(jnp.bfloat16)
+
+
+def stage_kernel(groups, slots, x0_ref, x1_ref, q_hbm, out_ref, held_ref, stage, sems):
+    parts, _, width = held_ref.shape
 
     def load(k):
-        columns = pl.ds(pl.multiple_of(k * width, width), width)
-        return pltpu.make_async_copy(q_hbm.at[:, columns], queries.at[k], sems.at[k])
+        columns = q_hbm.at[:, pl.ds(k * width, width)]
+        return pltpu.make_async_copy(columns, held_ref.at[k], sems.at[k])
 
     for k in range(parts):
         load(k).start()
-
-    @pl.loop(0, groups)
-    def _(d):
-        base = d * padded * each
-        for k in range(parts):
-            if first:
-                stage[k, pl.ds(base, first * each), :] = jnp.zeros(
-                    (first * each, LANES), jnp.float32
-                )
-            stage[k, pl.ds(base + (first + 2 * slots) * each, after * each), :] = jnp.zeros(
-                (after * each, LANES), jnp.float32
-            )
-        for n, x_ref in enumerate((x0_ref, x1_ref)):
-            got = x_ref[pl.ds(pl.multiple_of(d * span, span), span), :].astype(jnp.float32)
-            got = got.reshape(slots, parts, each, LANES)
-            for k in range(parts):
-                at = pl.ds(base + (first + n * slots) * each, slots * each)
-                stage[k, at, :] = got[:, k].reshape(slots * each, LANES)
-
-    rows = groups * padded
-    total[...] = jnp.zeros_like(total)
+    stage_units((x0_ref, x1_ref), stage, parts, slots, groups)
 
     @pl.loop(0, parts)
     def _(k):
-        for j in range(each):
-            piece = stage[k, pl.ds(j, rows, stride=each), :]
-            units[:, j * LANES : (j + 1) * LANES] = piece.astype(jnp.bfloat16)
+        staged_rows(stage, k, out_ref.at[k], 0)
+
+    for k in range(parts):
         load(k).wait()
-        total[...] += lax.dot_general(
-            queries[k], units[...], NT, preferred_element_type=jnp.float32
-        )
-
-    out = total[...].T
-    if first:
-        out = out + prev_ref[...]
+
+
+def staged(x0, x1, queries, groups, slots, parts):
+    rows = 2 * groups * slots
+    count, width = queries.shape[0], queries.shape[1] // parts
+    vmem = pl.BlockSpec(memory_space=pltpu.VMEM)
+    return pl.pallas_call(
+        functools.partial(stage_kernel, groups, slots),
+        in_specs=[vmem, vmem, pl.BlockSpec(memory_space=pltpu.HBM)],
+        out_specs=[vmem] * 2,
+        out_shape=[
+            jax.ShapeDtypeStruct((parts, rows, width), jnp.bfloat16),
+            jax.ShapeDtypeStruct((parts, count, width), jnp.bfloat16),
+        ],
+        scratch_shapes=[
+            pltpu.VMEM((parts, rows * width // LANES, LANES), jnp.float32),
+            pltpu.SemaphoreType.DMA((parts,)),
+        ],
+        compiler_params=pltpu.CompilerParams(vmem_limit_bytes=16 << 20),
+        cost_estimate=pl.CostEstimate(
+            flops=4 * x0.size, bytes_accessed=4 * queries.size, transcendentals=0
+        ),
+        name="staged",
+    )(x0, x1, queries)
+
+
+def score_kernel(groups, slots, padded, x0_ref, x1_ref, early_ref, q_ref, out_ref, stage, units, total):
+    parts = q_ref.shape[0]
+    half = groups * slots
+    stage_units((x0_ref, x1_ref), stage, parts, slots, groups)
+    total[...] = jnp.zeros_like(total)
+
+    @pl.loop(0, parts)
+    def _(k):
+        units[0 : 2 * half, :] = early_ref[k]
+        staged_rows(stage, k, units, 2 * half)
+        total[...] += lax.dot_general(q_ref[k], units[...], NT, preferred_element_type=jnp.float32)
+
+    row = lax.broadcasted_iota(jnp.int32, (groups * padded, 4 * half), 0)
+    column = lax.broadcasted_iota(jnp.int32, (1, 4 * half), 1)
+    place = column
+    for n in range(1, 4):
+        place += jnp.where(column >= n * half, slots - half, 0)
+    for n in range(4):
+        for d in range(1, groups):
+            after = (column >= n * half + d * slots) & (column < (n + 1) * half)
+            place += jnp.where(after, padded - slots, 0)
+    pick = jnp.where(row == place, 1.0, 0.0).astype(jnp.bfloat16)
+    out = lax.dot_general(
+        pick, total[...].astype(jnp.bfloat16), NT, preferred_element_type=jnp.float32
+    )
     out_ref[...] = out.astype(out_ref.dtype)
 
 
-def scores_of(x0, x1, queries, prev, groups, slots, padded, first):
-    parts = 4
-    count, width = queries.shape[0], queries.shape[1] // parts
-    chunks = queries.shape[1] // LANES
-    rows = groups * padded
+def scores_of(x0, x1, early, queries, groups, slots, padded):
+    parts, count, width = queries.shape
+    half = groups * slots
     vmem = pl.BlockSpec(memory_space=pltpu.VMEM)
     return pl.pallas_call(
-        functools.partial(score_kernel, groups, slots, padded, first, chunks, parts),
-        in_specs=[vmem, vmem, pl.BlockSpec(memory_space=pltpu.HBM)] + ([vmem] if first else []),
+        functools.partial(score_kernel, groups, slots, padded),
+        in_specs=[vmem] * 4,
         out_specs=vmem,
-        out_shape=jax.ShapeDtypeStruct((rows, count), jnp.bfloat16 if first else jnp.float32),
+        out_shape=jax.ShapeDtypeStruct((groups * padded, count), jnp.bfloat16),
         scratch_shapes=[
-            pltpu.VMEM((parts, rows * (chunks // parts), LANES), jnp.float32),
-            pltpu.VMEM((rows, width), jnp.bfloat16),
-            pltpu.VMEM((parts, count, width), jnp.bfloat16),
-            pltpu.VMEM((count, rows), jnp.float32),
-            pltpu.SemaphoreType.DMA((parts,)),
-        ],
-        compiler_params=pltpu.CompilerParams(vmem_limit_bytes=50 << 20),
+            pltpu.VMEM((parts, 2 * half * width // LANES, LANES), jnp.float32),
+            pltpu.VMEM((4 * half, width), jnp.bfloat16),
+            pltpu.VMEM((count, 4 * half), jnp.float32),
+        ],
+        compiler_params=pltpu.CompilerParams(vmem_limit_bytes=24 << 20),
         cost_estimate=pl.CostEstimate(
-            flops=2 * rows * queries.size, bytes_accessed=2 * queries.size, transcendentals=0
+            flops=2 * 4 * half * queries.size, bytes_accessed=2 * queries.size, transcendentals=0
         ),
         name="scores",
-    )(x0, x1, queries, *([prev] if first else []))
+    )(x0, x1, early, queries)
 
 
 def pick_kernel(row_ref, x_ref, out_ref):
-    count = row_ref.shape[0]
+    count = row_ref.shape[1]
     rows = x_ref.shape[0]
     parts = x_ref.shape[1] // LANES
-    hit = lax.broadcasted_iota(jnp.int32, (count, rows), 1) == row_ref[...]
-    pick = jnp.where(hit, 1.0, 0.0).astype(jnp.bfloat16)
+    hit = lax.broadcasted_iota(jnp.int32, (rows, count), 0) == row_ref[...]
+    pick = jnp.where(hit, 1.0, 0.0).T.astype(jnp.bfloat16)
     got = jnp.dot(pick, x_ref[...], preferred_element_type=jnp.float32)
     for j in range(parts):
         out_ref[pl.ds(j, count, stride=parts), :] = got[:, j * LANES : (j + 1) * LANES]
@@ -271,7 +344,7 @@
 
 def pick_rows(row, x):
     vmem = pl.BlockSpec(memory_space=pltpu.VMEM)
-    count, width = row.shape[0], x.shape[1]
+    count, width = row.shape[1], x.shape[1]
     return pl.pallas_call(
         pick_kernel,
         in_specs=[vmem, vmem],
@@ -288,7 +361,6 @@
     features = out_grads.shape[2]
     groups = lax.axis_size("dp")
     ways = lax.axis_size("tensor")
-    me = lax.axis_index("tensor")
     capacity = max(2, 5 * examples // (2 * groups))
     slots = -(-capacity // ways)
     padded = -(-ways * slots // 8) * 8
@@ -297,8 +369,7 @@
     core = [(i, i ^ 1) for i in range(ways)]
     across = [(i, i ^ 2) for i in range(ways)]
 
-    cands = candidates.reshape(-1)
-    own_part, over_part, near_part, far_part = project(
+    own_part, over_part, near_part, far_part, my_slots, pick = project(
         candidates.reshape(1, examples),
         activations.reshape(examples * tokens, hidden),
         out_grads.reshape(examples * tokens, features),
@@ -307,35 +378,24 @@
         tokens,
         groups,
         ways,
+        slots,
+        padded,
     )
     far_in = lax.ppermute(far_part, "tensor", core)
     near_in = lax.ppermute(near_part, "tensor", core)
     across_in = lax.ppermute(over_part + far_in, "tensor", across)
 
-    number = jnp.arange(examples, dtype=jnp.int32)
-    before = (cands[None, :] < cands[:, None]) | (
-        (cands[None, :] == cands[:, None]) & (number[None, :] < number[:, None])
-    )
-    place = jnp.sum(before.astype(jnp.int32), axis=1)
-    start = jnp.sum((cands[None, :] < cands[:, None]).astype(jnp.int32), axis=1)
-    owner = place % ways
-    slot = place // ways - (start + ways - 1 - owner) // ways
-    mine = (
-        place[None, :] == ways * jnp.arange(examples // ways, dtype=jnp.int32)[:, None] + me
-    )
-    my_slots = jnp.sum(jnp.where(mine, (cands * slots + slot)[None, :], 0), axis=1)
-    pick = (cands * padded + (owner ^ me) * slots + slot)[:, None]
-
-    units = unit_grads(my_slots, own_part + near_in, across_in, tokens, chunks, groups * slots)
+    here_slots, here = own_sum(my_slots, own_part, near_in, examples // ways)
+    units = unit_grads(here_slots, here, across_in, tokens, chunks, groups * slots)
     shape = (groups, slots * chunks, LANES)
     own = lax.all_to_all(units.reshape(shape), "dp", split_axis=0, concat_axis=0, tiled=True)
     own = own.reshape(units.shape)
     over_y = lax.ppermute(own, "tensor", across)
     over_core = lax.ppermute(own, "tensor", core)
-    first = scores_of(own, over_core, query_block, None, groups, slots, padded, 0)
-    over_y, first = lax.optimization_barrier((over_y, first))
+    early, held = staged(own, over_core, query_block, groups, slots, 4)
+    over_y, early = lax.optimization_barrier((over_y, early))
     over_both = lax.ppermute(over_y, "tensor", core)
-    both = scores_of(over_y, over_both, query_block, first, groups, slots, padded, 2 * slots)
+    both = scores_of(over_y, over_both, early, held, groups, slots, padded)
     block = both.reshape(groups, padded, both.shape[1])
     returned = lax.all_to_all(block, "dp", split_axis=0, concat_axis=0, tiled=True)
     picked = pick_rows(pick, returned.reshape(both.shape))

time: 67.5 us -> 64.3 us (0.953)
  blocking collectives: 16.3 us -> 28 us
  waiting for transfers between devices: 19.9 us -> 9.88 us
  local copies, waits for them, and re-layouts: 0.36 us -> 4.07 us
  Pallas kernels: 19.7 us -> 16 us
  starting transfers between devices: 8.49 us -> 5.08 us
  other arithmetic: 2.37 us -> 0.96 us
    all_to_all x0 -> x1, blocking collectives: none -> 11.7 us  [local_one(): lax.all_to_all(block, 'dp', split_axis=0, concat_axis=0, tiled=True)]
    all_to_all x1 -> x0, waiting for transfers between devices: 8.93 us -> none  [local_one(): lax.all_to_all(block, 'dp', split_axis=0, concat_axis=0, tiled=True)]
    unnamed x2 -> x8, local copies, waits for them, and re-layouts: 0.01 us -> 4.07 us
    pallas_call x3 -> x4, Pallas kernels: 16.9 us -> 13.2 us  [the longest x1 7.96 us: project(): pl.pallas_call(functools.partial(project_kernel, groups, ways, tokens, sl...]
    all_to_all x1 -> x0, starting transfers between devices: 3.42 us -> none  [local_one(): lax.all_to_all(block, 'dp', split_axis=0, concat_axis=0, tiled=True)]
    ppermute x1, waiting for transfers between devices: 4.06 us -> 2.36 us  [local_one(): across_in = lax.ppermute(over_part + far_in, 'tensor', across)]
    add x5 -> x0, other arithmetic: 1.04 us -> none  [the longest x1 0.95 us: local_one(): own_part + near_in]
  transfers between devices with their start and end apart: 7 -> 6, of which waited for: 6 -> 5; matrix products, arithmetic and copies ran while one was open for 4% -> 1% of each run, Pallas kernels for 6% -> 4%
where the time goes in v3:
time: 64.3 us; the launch traced here: 64 us
  blocking collectives  28 us (44%)
  Pallas kernels  16 us (25%)
  waiting for transfers between devices  9.88 us (15%)
  starting transfers between devices  5.08 us (8%)
  local copies, waits for them, and re-layouts  4.07 us (6%)
  other arithmetic  0.96 us (1%)
    all_to_all x1, blocking collectives, local_one(): lax.all_to_all(units.reshape(shape), 'dp', split_axis=0, concat_axis=0, t...  16.2 us
    all_to_all x1, blocking collectives, local_one(): lax.all_to_all(block, 'dp', split_axis=0, concat_axis=0, tiled=True)  11.7 us
    pallas_call x1, Pallas kernels, project(): pl.pallas_call(functools.partial(project_kernel, groups, ways, tokens, sl...  7.96 us
    ppermute x1, waiting for transfers between devices, local_one(): over_y = lax.ppermute(own, 'tensor', across)  4.6 us
    unnamed x8, local copies, waits for them, and re-layouts  4.07 us
    ppermute x1, starting transfers between devices, local_one(): across_in = lax.ppermute(over_part + far_in, 'tensor', across)  2.95 us
    pallas_call x1, Pallas kernels, scores_of(): pl.pallas_call(functools.partial(score_kernel, groups, slots, padded), in...  2.56 us
    ppermute x1, waiting for transfers between devices, local_one(): across_in = lax.ppermute(over_part + far_in, 'tensor', across)  2.36 us
  transfers between devices with their start and end apart: 6, of which 5 were waited for; matrix products, arithmetic and copies ran while one was open for 1% of the time, Pallas kernels for 4%

profile of v3, /device:TPU:0, one launch (start us, length us, event | category | flops | bytes accessed | tf_op | source)
XLA Modules:
  0.0 64.0 jit_solution(590818690064191363)
XLA Ops:
  0.0 8.0 %project.1 = (f32[384,128]{1,0:T(8,128)}, f32[384,128]{1,0:T(8,128)}, f32[384,128]{1,0:T(8,128)}, f32[384,128]{1,0:T(8,128)}, s32[64]{0:T(128)}, /*index=5*/s32[1,64]{1,0:T(1,128)}) custom-call(s32[1,64]{1,0:T(1,128)} %bitcast.22, bf16[1536,3584]{1,0:T(8,128)(2,1)} %bitcast.18, bf16[1536,1024]{1,0:T(8,128)(2,1)} %bitcast.19, bf16[64,3584]{1,0:T(8,128)(2,1)} %bitcast.20, ...), custom_call_target="tpu_custom_call" | custom-call | flops 905969664 | bytes 14155776 | tf_op jit(solution)/shard_map/project/pallas_call | solution.py:121
  8.0 0.5 collective-permute-start.1
  8.5 0.1 collective-permute-start
  8.6 1.2 %collective-permute-done.1 = f32[384,128]{1,0:T(8,128)S(1)} collective-permute-done((f32[384,128]{1,0:T(8,128)}, f32[384,128]{1,0:T(8,128)S(1)}, u32[]{:S(2)}, u32[]{:S(2)}) %collective-permute-start.1) | collective-permute-done | bytes 196640 | tf_op jit(solution)/shard_map/ppermute | solution.py:384
  9.8 1.0 %add.3 = f32[384,128]{1,0:T(8,128)S(1)} add(f32[384,128]{1,0:T(8,128)} %get-tuple-element.23, f32[384,128]{1,0:T(8,128)S(1)} %collective-permute-done.1) | non-fusion elementwise | flops 49152 | bytes 589824 | tf_op jit(solution)/shard_map/add | solution.py:386
  10.7 3.0 %collective-permute-start.2 = (f32[384,128]{1,0:T(8,128)S(1)}, f32[384,128]{1,0:T(8,128)S(1)}, u32[]{:S(2)}, u32[]{:S(2)}) collective-permute-start(f32[384,128]{1,0:T(8,128)S(1)} %add.3), channel_id=1, source_target_pairs={{0,2},{1,3},{2,0},{3,1},{4,6},{5,7},{6,4},{7,5},{8,10},{9,11},{10,... | collective-permute-start | bytes 589832 | tf_op jit(solution)/shard_map/ppermute | solution.py:386
  13.7 0.0 collective-permute-done.b_ref
  13.7 0.0 copy-start.1
  13.7 0.9 %copy-done.1 = f32[384,128]{1,0:T(8,128)S(1)} copy-done((f32[384,128]{1,0:T(8,128)S(1)}, f32[384,128]{1,0:T(8,128)}, u32[]{:S(2)}) %copy-start.1) | copy-done | bytes 196632
  14.6 0.0 copy-start.3
  14.6 0.7 %copy-done.3 = s32[64]{0:T(128)S(1)} copy-done((s32[64]{0:T(128)S(1)}, s32[64]{0:T(128)}, u32[]{:S(2)}) %copy-start.3) | copy-done | bytes 280
  15.3 1.3 %own_sum.1 = (s32[16]{0:T(128)S(1)}, f32[384,128]{1,0:T(8,128)S(1)}) custom-call(s32[64]{0:T(128)S(1)} %copy-done.3, f32[384,128]{1,0:T(8,128)S(1)} %copy-done.1, f32[384,128]{1,0:T(8,128)S(1)} %collective-permute-done.b_ref), custom_call_target="tpu_custom_call" | custom-call | flops 49152 | bytes 589824 | tf_op jit(solution)/shard_map/own_sum/pallas_call | solution.py:165
  16.5 2.4 %collective-permute-done.2.b_ref = f32[384,128]{1,0:T(8,128)S(1)} collective-permute-done((f32[384,128]{1,0:T(8,128)S(1)}, f32[384,128]{1,0:T(8,128)S(1)}, u32[]{:S(2)}, u32[]{:S(2)}) %collective-permute-start.2) | collective-permute-done | bytes 196640 | tf_op jit(solution)/shard_map/ppermute | solution.py:386
  18.9 1.9 %unit_grads.1 = bf16[1280,128]{1,0:T(8,128)(2,1)S(1)} custom-call(s32[16]{0:T(128)S(1)} %get-tuple-element.21.row_ref, f32[384,128]{1,0:T(8,128)S(1)} %get-tuple-element.22.a_ref, f32[384,128]{1,0:T(8,128)S(1)} %collective-permute-done.2.b_ref), custom_call_target="tpu_custom_call" | custom-call | flops 20000000 | bytes 1000000 | tf_op jit(solution)/shard_map/unit_grads/pallas_call | solution.py:207
  20.8 16.2 %all_to_all.10 = bf16[8,160,128]{2,1,0:T(8,128)(2,1)S(1)} all-to-all(bf16[8,160,128]{2,1,0:T(8,128)(2,1)S(1)} %bitcast.15), channel_id=1, replica_groups=mesh['dp'=8,'tensor'=4] {'dp'}, dimensions={0} | all-to-all | bytes 655360 | tf_op jit(solution)/shard_map/all_to_all | solution.py:391
  37.0 0.0 collective-permute-start.4
  37.0 1.5 %collective-permute-start.3 = (bf16[1280,128]{1,0:T(8,128)(2,1)S(1)}, bf16[1280,128]{1,0:T(8,128)(2,1)S(1)}, u32[]{:S(2)}, u32[]{:S(2)}) collective-permute-start(bf16[1280,128]{1,0:T(8,128)(2,1)S(1)} %bitcast.13), channel_id=1, source_target_pairs={{0,2},{1,3},{2,0},{3,1},{4,6},{5,7},{6,4},{7,5},{8,10},{9,11},{10,... | collective-permute-start | bytes 983048 | tf_op jit(solution)/shard_map/ppermute | solution.py:393
  38.6 0.1 collective-permute-done.4.x1_ref
  38.7 0.0 copy-start
  38.7 2.5 %copy-done = bf16[1,640,4096]{2,1,0:T(8,128)(2,1)S(1)} copy-done((bf16[1,640,4096]{2,1,0:T(8,128)(2,1)S(1)}, bf16[1,640,4096]{2,1,0:T(8,128)(2,1)}, u32[]{:S(2)}) %copy-start) | copy-done | bytes 5242904
  41.1 0.0 copy-start.2
  41.1 1.4 %staged.1 = (bf16[4,80,1024]{2,1,0:T(8,128)(2,1)S(1)}, bf16[4,640,1024]{2,1,0:T(8,128)(2,1)S(1)}) custom-call(bf16[1280,128]{1,0:T(8,128)(2,1)S(1)} %bitcast.14, bf16[1280,128]{1,0:T(8,128)(2,1)S(1)} %collective-permute-done.4.x1_ref, bf16[640,4096]{1,0:T(8,128)(2,1)S(1)} %bitcast.11), custom_call_target="tpu_custom_call" | custom-call | flops 655360 | bytes 10485760 | tf_op jit(solution)/shard_map/staged/pallas_call | solution.py:264
  42.6 4.6 %collective-permute-done.3.x0_ref = bf16[1280,128]{1,0:T(8,128)(2,1)S(1)} collective-permute-done((bf16[1280,128]{1,0:T(8,128)(2,1)S(1)}, bf16[1280,128]{1,0:T(8,128)(2,1)S(1)}, u32[]{:S(2)}, u32[]{:S(2)}) %collective-permute-start.3) | collective-permute-done | bytes 327712 | tf_op jit(solution)/shard_map/ppermute | solution.py:393
  47.2 0.0 collective-permute-start.5
  47.2 1.6 %collective-permute-done.5.x1_ref = bf16[1280,128]{1,0:T(8,128)(2,1)S(1)} collective-permute-done((bf16[1280,128]{1,0:T(8,128)(2,1)S(1)}, bf16[1280,128]{1,0:T(8,128)(2,1)S(1)}, u32[]{:S(2)}, u32[]{:S(2)}) %collective-permute-start.5) | collective-permute-done | bytes 327712 | tf_op jit(solution)/shard_map/ppermute | solution.py:397
  48.8 2.6 %scores.1 = bf16[192,640]{1,0:T(8,128)(2,1)S(1)} custom-call(bf16[1280,128]{1,0:T(8,128)(2,1)S(1)} %collective-permute-done.3.x0_ref, bf16[1280,128]{1,0:T(8,128)(2,1)S(1)} %collective-permute-done.5.x1_ref, bf16[4,80,1024]{2,1,0:T(8,128)(2,1)S(1)} %get-tuple-element.27.early_ref, bf16[4,640,1024]{2,1,0:T(8,128)(2,1)S(1)} %get-tuple-element.28.q_ref), custom_call_target="tpu_custom_call" | custom-call | flops 838860800 | bytes 5242880 | tf_op jit(solution)/shard_map/scores/pallas_call | solution.py:316
  51.3 11.7 %all_to_all.11 = bf16[8,24,640]{2,1,0:T(8,128)(2,1)S(1)} all-to-all(bf16[8,24,640]{2,1,0:T(8,128)(2,1)S(1)} %bitcast.16), channel_id=1, replica_groups=mesh['dp'=8,'tensor'=4] {'dp'}, dimensions={0} | all-to-all | bytes 491520 | tf_op jit(solution)/shard_map/all_to_all | solution.py:400
  63.1 0.0 copy-done.2
  63.1 0.9 %pick_rows.1 = f32[320,128]{1,0:T(8,128)} custom-call(s32[1,64]{1,0:T(1,128)S(1)} %copy-done.2, bf16[192,640]{1,0:T(8,128)(2,1)S(1)} %bitcast.17), custom_call_target="tpu_custom_call" | custom-call | flops 16000000 | bytes 400000 | tf_op jit(solution)/shard_map/pick_rows/pallas_call | solution.py:348
Async XLA Ops:
  8.0 1.8 %collective-permute-start.1 = (f32[384,128]{1,0:T(8,128)}, f32[384,128]{1,0:T(8,128)S(1)}, u32[]{:S(2)}, u32[]{:S(2)}) collective-permute-start(f32[384,128]{1,0:T(8,128)} %get-tuple-element.24), channel_id=1, source_target_pairs={{0,1},{1,0},{2,3},{3,2},{4,5},{5,4},{6,7},{7,6},{8,9},{9,8},{10,11... | collective-permute-start | bytes 589832 | tf_op jit(solution)/shard_map/ppermute | solution.py:384
  8.5 5.2 %collective-permute-start = (f32[384,128]{1,0:T(8,128)}, f32[384,128]{1,0:T(8,128)S(1)}, u32[]{:S(2)}, u32[]{:S(2)}) collective-permute-start(f32[384,128]{1,0:T(8,128)} %get-tuple-element.20), channel_id=1, source_target_pairs={{0,1},{1,0},{2,3},{3,2},{4,5},{5,4},{6,7},{7,6},{8,9},{9,8},{10,11... | collective-permute-start | bytes 589832 | tf_op jit(solution)/shard_map/ppermute | solution.py:385
  10.7 8.2 %collective-permute-start.2 = (f32[384,128]{1,0:T(8,128)S(1)}, f32[384,128]{1,0:T(8,128)S(1)}, u32[]{:S(2)}, u32[]{:S(2)}) collective-permute-start(f32[384,128]{1,0:T(8,128)S(1)} %add.3), channel_id=1, source_target_pairs={{0,2},{1,3},{2,0},{3,1},{4,6},{5,7},{6,4},{7,5},{8,10},{9,11},{10,... | collective-permute-start | bytes 589832 | tf_op jit(solution)/shard_map/ppermute | solution.py:386
  13.7 0.9 %copy-start.1 = (f32[384,128]{1,0:T(8,128)S(1)}, f32[384,128]{1,0:T(8,128)}, u32[]{:S(2)}) copy-start(f32[384,128]{1,0:T(8,128)} %get-tuple-element.19.a_ref) | copy-start | bytes 589828
  14.6 0.7 %copy-start.3 = (s32[64]{0:T(128)S(1)}, s32[64]{0:T(128)}, u32[]{:S(2)}) copy-start(s32[64]{0:T(128)} %get-tuple-element.18.slot_ref) | copy-start | bytes 772
  37.0 1.6 %collective-permute-start.4 = (bf16[1280,128]{1,0:T(8,128)(2,1)S(1)}, bf16[1280,128]{1,0:T(8,128)(2,1)S(1)}, u32[]{:S(2)}, u32[]{:S(2)}) collective-permute-start(bf16[1280,128]{1,0:T(8,128)(2,1)S(1)} %bitcast.12), channel_id=1, source_target_pairs={{0,1},{1,0},{2,3},{3,2},{4,5},{5,4},{6,7},{7,6},{8,9},{9,8},{10,11... | collective-permute-start | bytes 983048 | tf_op jit(solution)/shard_map/ppermute | solution.py:394
  37.0 10.1 %collective-permute-start.3 = (bf16[1280,128]{1,0:T(8,128)(2,1)S(1)}, bf16[1280,128]{1,0:T(8,128)(2,1)S(1)}, u32[]{:S(2)}, u32[]{:S(2)}) collective-permute-start(bf16[1280,128]{1,0:T(8,128)(2,1)S(1)} %bitcast.13), channel_id=1, source_target_pairs={{0,2},{1,3},{2,0},{3,1},{4,6},{5,7},{6,4},{7,5},{8,10},{9,11},{10,... | collective-permute-start | bytes 983048 | tf_op jit(solution)/shard_map/ppermute | solution.py:393
  38.7 2.5 %copy-start = (bf16[1,640,4096]{2,1,0:T(8,128)(2,1)S(1)}, bf16[1,640,4096]{2,1,0:T(8,128)(2,1)}, u32[]{:S(2)}) copy-start(bf16[1,640,4096]{2,1,0:T(8,128)(2,1)} %param.10) | copy-start | bytes 15728644
  41.1 21.9 %copy-start.2 = (s32[1,64]{1,0:T(1,128)S(1)}, s32[1,64]{1,0:T(1,128)}, u32[]{:S(2)}) copy-start(s32[1,64]{1,0:T(1,128)} %get-tuple-element.17.row_ref) | copy-start | bytes 772
  47.2 1.6 %collective-permute-start.5 = (bf16[1280,128]{1,0:T(8,128)(2,1)S(1)}, bf16[1280,128]{1,0:T(8,128)(2,1)S(1)}, u32[]{:S(2)}, u32[]{:S(2)}) collective-permute-start(bf16[1280,128]{1,0:T(8,128)(2,1)S(1)} %collective-permute-done.3.x0_ref), channel_id=1, source_target_pairs={{0,1},{1,0},{2,3},{3,2},{4,5},{5,4},{6,7},{7,6},{8,9},{9,8},{10,11... | collective-permute-start | bytes 983048 | tf_op jit(solution)/shard_map/ppermute | solution.py:397

commit v4 on v3

--- a/solution.py
+++ b/solution.py
@@ -24,6 +24,7 @@
     share = examples // ways
     step = act.shape[0] // act_sems.shape[0]
     me = lax.axis_index("tensor")
+    home = lax.axis_index("dp")
 
     def piece(i):
         return pl.ds(pl.multiple_of(i * step, step), step)
@@ -95,7 +96,7 @@
                 turn = place >> (ways.bit_length() - 1)
                 before = (start[g] + ways - 1 - owner) >> (ways.bit_length() - 1)
                 rel = owner ^ me
-                slot_ref[rel * share + turn] = g * slots + turn - before
+                slot_ref[rel * share + turn] = (g ^ home) * slots + turn - before
                 pick_ref[0, e] = g * padded + rel * slots + turn - before
                 row = (rel * share + turn) * tokens
                 dealt[pl.ds(pl.multiple_of(row, 8), tokens), :] = both[
@@ -122,9 +123,9 @@
         functools.partial(project_kernel, groups, ways, tokens, slots, padded, blocks),
         in_specs=[hbm] * 5,
         out_specs=[vmem] * 4 + [pl.BlockSpec(memory_space=pltpu.SMEM)] * 2,
-        out_shape=[jax.ShapeDtypeStruct((share, LANES), jnp.float32)] * 4
+        out_shape=[pltpu.VMEM((share, LANES), jnp.float32)] * 4
         + [
-            jax.ShapeDtypeStruct((examples,), jnp.int32),
+            pltpu.SMEM((examples,), jnp.int32),
             jax.ShapeDtypeStruct((1, examples), jnp.int32),
         ],
         scratch_shapes=[
@@ -151,34 +152,50 @@
     )(cands, act, grad, win, wout)
 
 
-def own_kernel(slot_ref, a_ref, b_ref, out_slot_ref, out_ref):
+def own_kernel(slot_ref, a_ref, b_ref, q_hbm, out_slot_ref, out_ref, held_ref, sems):
+    parts, _, width = held_ref.shape
+
+    def load(k):
+        columns = q_hbm.at[:, pl.ds(k * width, width)]
+        return pltpu.make_async_copy(columns, held_ref.at[k], sems.at[k])
+
+    for k in range(parts):
+        load(k).start()
     out_ref[...] = a_ref[...] + b_ref[...]
 
     @pl.loop(0, out_slot_ref.shape[0])
     def _(i):
         out_slot_ref[i] = slot_ref[i]
 
-
-def own_sum(slots, a, b, count):
+    for k in range(parts):
+        load(k).wait()
+
+
+def own_sum(slots, a, b, queries, count, parts):
     smem = pl.BlockSpec(memory_space=pltpu.SMEM)
     vmem = pl.BlockSpec(memory_space=pltpu.VMEM)
     return pl.pallas_call(
         own_kernel,
-        in_specs=[smem, vmem, vmem],
-        out_specs=[smem, vmem],
+        in_specs=[smem, vmem, vmem, pl.BlockSpec(memory_space=pltpu.HBM)],
+        out_specs=[smem, vmem, vmem],
         out_shape=[
-            jax.ShapeDtypeStruct((count,), jnp.int32),
-            jax.ShapeDtypeStruct(a.shape, a.dtype),
+            pltpu.SMEM((count,), jnp.int32),
+            pltpu.VMEM(a.shape, a.dtype),
+            pltpu.VMEM((parts, queries.shape[0], queries.shape[1] // parts), queries.dtype),
         ],
-        compiler_params=pltpu.CompilerParams(vmem_limit_bytes=16 << 20),
-        cost_estimate=pl.CostEstimate(flops=a.size, bytes_accessed=12 * a.size, transcendentals=0),
+        scratch_shapes=[pltpu.SemaphoreType.DMA((parts,))],
+        compiler_params=pltpu.CompilerParams(vmem_limit_bytes=48 << 20),
+        cost_estimate=pl.CostEstimate(
+            flops=a.size, bytes_accessed=2 * queries.size, transcendentals=0
+        ),
         name="own_sum",
-    )(slots, a, b)
-
-
-def unit_kernel(tokens, chunks, row_ref, a_ref, b_ref, out_ref, total):
+    )(slots, a, b, queries)
+
+
+def unit_kernel(tokens, chunks, row_ref, a_ref, b_ref, *rest):
+    out_refs, total, units = rest[:-2], rest[-2], rest[-1]
     total[...] = a_ref[...] + b_ref[...]
-    out_ref[...] = jnp.zeros_like(out_ref)
+    units[...] = jnp.zeros_like(units)
     count = total.shape[0] // tokens
     half = LANES // 2
     width = chunks * LANES
@@ -199,17 +216,25 @@
         mean = jnp.sum(square, axis=1, keepdims=True) / width
         unit = (entries * lax.rsqrt(mean + epsilon)).astype(jnp.bfloat16)
         row = pl.multiple_of(row_ref[i] * chunks, chunks)
-        out_ref[pl.ds(row, chunks), :] = unit
-
-
-def unit_grads(slots, a, b, tokens, chunks, slot_count):
+        units[pl.ds(row, chunks), :] = unit
+
+    for n, ref in enumerate(out_refs):
+        size = ref.shape[0]
+        ref[...] = units[n * size : (n + 1) * size, :]
+
+
+def unit_grads(slots, a, b, tokens, chunks, groups, slot_count):
+    rows = slot_count * chunks
     whole = pl.BlockSpec(memory_space=pltpu.VMEM)
     return pl.pallas_call(
         functools.partial(unit_kernel, tokens, chunks),
         in_specs=[pl.BlockSpec(memory_space=pltpu.SMEM), whole, whole],
-        out_specs=whole,
-        out_shape=jax.ShapeDtypeStruct((slot_count * chunks, LANES), jnp.bfloat16),
-        scratch_shapes=[pltpu.VMEM(a.shape, jnp.float32)],
+        out_specs=[whole] * groups,
+        out_shape=[jax.ShapeDtypeStruct((rows, LANES), jnp.bfloat16)] * groups,
+        scratch_shapes=[
+            pltpu.VMEM(a.shape, jnp.float32),
+            pltpu.VMEM((groups * rows, LANES), jnp.bfloat16),
+        ],
         compiler_params=pltpu.CompilerParams(vmem_limit_bytes=16 << 20),
         cost_estimate=pl.CostEstimate(flops=20_000_000, bytes_accessed=1_000_000, transcendentals=0),
         name="unit_grads",
@@ -217,16 +242,18 @@
 
 
 def stage_units(refs, stage, parts, slots, groups):
-    each = stage.shape[1] // (len(refs) * groups * slots)
+    each = stage.shape[1] // (len(refs) // 2 * groups * slots)
     span = slots * parts * each
-
-    @pl.loop(0, groups)
-    def _(d):
+    home = lax.axis_index("dp")
+
+    @pl.loop(0, groups // 2)
+    def _(i):
         for n, ref in enumerate(refs):
-            got = ref[pl.ds(pl.multiple_of(d * span, span), span), :].astype(jnp.float32)
+            d = (2 * i + n % 2) ^ home
+            got = ref[pl.ds(pl.multiple_of(i * span, span), span), :].astype(jnp.float32)
             got = got.reshape(slots, parts, each, LANES)
             for k in range(parts):
-                at = pl.multiple_of((n * groups + d) * slots * each, each)
+                at = pl.multiple_of((n // 2 * groups + d) * slots * each, each)
                 stage[k, pl.ds(at, slots * each), :] = got[:, k].reshape(slots * each, LANES)
 
 
@@ -238,53 +265,39 @@
         units[at:, j * LANES : (j + 1) * LANES] = piece.astype(jnp.bfloat16)
 
 
-def stage_kernel(groups, slots, x0_ref, x1_ref, q_hbm, out_ref, held_ref, stage, sems):
-    parts, _, width = held_ref.shape
-
-    def load(k):
-        columns = q_hbm.at[:, pl.ds(k * width, width)]
-        return pltpu.make_async_copy(columns, held_ref.at[k], sems.at[k])
-
-    for k in range(parts):
-        load(k).start()
-    stage_units((x0_ref, x1_ref), stage, parts, slots, groups)
+def stage_kernel(groups, slots, *rest):
+    refs, (out_ref, stage) = rest[:4], rest[4:]
+    parts = out_ref.shape[0]
+    stage_units(refs, stage, parts, slots, groups)
 
     @pl.loop(0, parts)
     def _(k):
         staged_rows(stage, k, out_ref.at[k], 0)
 
-    for k in range(parts):
-        load(k).wait()
-
-
-def staged(x0, x1, queries, groups, slots, parts):
+
+def staged(units, groups, slots, parts):
     rows = 2 * groups * slots
-    count, width = queries.shape[0], queries.shape[1] // parts
+    width = 2 * units[0].size // (groups * slots * parts)
     vmem = pl.BlockSpec(memory_space=pltpu.VMEM)
     return pl.pallas_call(
         functools.partial(stage_kernel, groups, slots),
-        in_specs=[vmem, vmem, pl.BlockSpec(memory_space=pltpu.HBM)],
-        out_specs=[vmem] * 2,
-        out_shape=[
-            jax.ShapeDtypeStruct((parts, rows, width), jnp.bfloat16),
-            jax.ShapeDtypeStruct((parts, count, width), jnp.bfloat16),
-        ],
-        scratch_shapes=[
-            pltpu.VMEM((parts, rows * width // LANES, LANES), jnp.float32),
-            pltpu.SemaphoreType.DMA((parts,)),
-        ],
+        in_specs=[vmem] * 4,
+        out_specs=vmem,
+        out_shape=pltpu.VMEM((parts, rows, width), jnp.bfloat16),
+        scratch_shapes=[pltpu.VMEM((parts, rows * width // LANES, LANES), jnp.float32)],
         compiler_params=pltpu.CompilerParams(vmem_limit_bytes=16 << 20),
         cost_estimate=pl.CostEstimate(
-            flops=4 * x0.size, bytes_accessed=4 * queries.size, transcendentals=0
+            flops=rows * parts * width, bytes_accessed=8 * rows * width, transcendentals=0
         ),
         name="staged",
-    )(x0, x1, queries)
-
-
-def score_kernel(groups, slots, padded, x0_ref, x1_ref, early_ref, q_ref, out_ref, stage, units, total):
+    )(*units)
+
+
+def score_kernel(groups, slots, padded, *rest):
+    refs, (early_ref, q_ref, out_ref, stage, units, total) = rest[:4], rest[4:]
     parts = q_ref.shape[0]
     half = groups * slots
-    stage_units((x0_ref, x1_ref), stage, parts, slots, groups)
+    stage_units(refs, stage, parts, slots, groups)
     total[...] = jnp.zeros_like(total)
 
     @pl.loop(0, parts)
@@ -309,13 +322,13 @@
     out_ref[...] = out.astype(out_ref.dtype)
 
 
-def scores_of(x0, x1, early, queries, groups, slots, padded):
+def scores_of(late, early, queries, groups, slots, padded):
     parts, count, width = queries.shape
     half = groups * slots
     vmem = pl.BlockSpec(memory_space=pltpu.VMEM)
     return pl.pallas_call(
         functools.partial(score_kernel, groups, slots, padded),
-        in_specs=[vmem] * 4,
+        in_specs=[vmem] * 6,
         out_specs=vmem,
         out_shape=jax.ShapeDtypeStruct((groups * padded, count), jnp.bfloat16),
         scratch_shapes=[
@@ -328,7 +341,7 @@
             flops=2 * 4 * half * queries.size, bytes_accessed=2 * queries.size, transcendentals=0
         ),
         name="scores",
-    )(x0, x1, early, queries)
+    )(*late, early, queries)
 
 
 def pick_kernel(row_ref, x_ref, out_ref):
@@ -385,17 +398,19 @@
     near_in = lax.ppermute(near_part, "tensor", core)
     across_in = lax.ppermute(over_part + far_in, "tensor", across)
 
-    here_slots, here = own_sum(my_slots, own_part, near_in, examples // ways)
-    units = unit_grads(here_slots, here, across_in, tokens, chunks, groups * slots)
-    shape = (groups, slots * chunks, LANES)
-    own = lax.all_to_all(units.reshape(shape), "dp", split_axis=0, concat_axis=0, tiled=True)
-    own = own.reshape(units.shape)
-    over_y = lax.ppermute(own, "tensor", across)
-    over_core = lax.ppermute(own, "tensor", core)
-    early, held = staged(own, over_core, query_block, groups, slots, 4)
-    over_y, early = lax.optimization_barrier((over_y, early))
-    over_both = lax.ppermute(over_y, "tensor", core)
-    both = scores_of(over_y, over_both, early, held, groups, slots, padded)
+    here_slots, here, held = own_sum(
+        my_slots, own_part, near_in, query_block, examples // ways, 4
+    )
+    units = unit_grads(here_slots, here, across_in, tokens, chunks, groups, slots)
+    arrived = [units[0]] + [None] * (groups - 1)
+    for k in reversed(range(1, groups)):
+        arrived[k] = lax.ppermute(units[k], "dp", [(i, i ^ k) for i in range(groups)])
+    own = [jnp.concatenate(arrived[n::2], axis=0) for n in range(2)]
+    over_y = [lax.ppermute(x, "tensor", across) for x in own]
+    over_core = [lax.ppermute(x, "tensor", core) for x in own]
+    early = staged(own + over_core, groups, slots, held.shape[0])
+    over_both = [lax.ppermute(x, "tensor", core) for x in over_y]
+    both = scores_of(over_y + over_both, early, held, groups, slots, padded)
     block = both.reshape(groups, padded, both.shape[1])
     returned = lax.all_to_all(block, "dp", split_axis=0, concat_axis=0, tiled=True)
     picked = pick_rows(pick, returned.reshape(both.shape))

time: 64.3 us -> 57.8 us (0.90)
  blocking collectives: 28 us -> 11.7 us
  starting transfers between devices: 5.08 us -> 18.5 us
  local copies, waits for them, and re-layouts: 4.07 us -> 0.07 us
  waiting for transfers between devices: 9.88 us -> 12 us
  other arithmetic: 0.96 us -> 0.02 us
  Pallas kernels: 16 us -> 15.3 us
    all_to_all x1 -> x0, blocking collectives: 16.2 us -> none  [local_one(): lax.all_to_all(units.reshape(shape), 'dp', split_axis=0, concat_axis=0, t...]
    ppermute x3 -> x13, starting transfers between devices: 1.53 us -> 14.9 us  [the longest x7 11.2 us: local_one(): lax.ppermute(units[k], 'dp', [(i, i ^ k) for i in range(groups)])]
    unnamed x8, local copies, waits for them, and re-layouts: 4.07 us -> 0.05 us
    ppermute x3 -> x13, waiting for transfers between devices: 6.32 us -> 8.38 us  [the longest x7 4.12 us: local_one(): lax.ppermute(units[k], 'dp', [(i, i ^ k) for i in range(groups)])]
    pallas_call x1, Pallas kernels: 1.25 us -> 2.55 us  [own_sum(): pl.pallas_call(own_kernel, in_specs=[smem, vmem, vmem, pl.BlockSpec(memor...]
    pallas_call x1, Pallas kernels: 1.4 us -> 0.4 us  [staged(): pl.pallas_call(functools.partial(stage_kernel, groups, slots), in_specs=[...]
    add x1, other arithmetic: 0.96 us -> 0.02 us  [local_one(): across_in = lax.ppermute(over_part + far_in, 'tensor', across)]
  transfers between devices with their start and end apart: 6 -> 16, of which waited for: 5 -> 7; matrix products, arithmetic and copies ran while one was open for 1% -> 0% of each run, Pallas kernels for 4% -> 5%
where the time goes in v4:
time: 57.8 us; the launch traced here: 57.7 us
  starting transfers between devices  18.5 us (32%)
  Pallas kernels  15.3 us (26%)
  waiting for transfers between devices  12 us (21%)
  blocking collectives  11.7 us (20%)
    all_to_all x1, blocking collectives, local_one(): lax.all_to_all(block, 'dp', split_axis=0, concat_axis=0, tiled=True)  11.7 us
    ppermute x7, starting transfers between devices, local_one(): lax.ppermute(units[k], 'dp', [(i, i ^ k) for i in range(groups)])  11.2 us
    pallas_call x1, Pallas kernels, project(): pl.pallas_call(functools.partial(project_kernel, groups, ways, tokens, sl...  7.55 us
    ppermute x7, waiting for transfers between devices, local_one(): lax.ppermute(units[k], 'dp', [(i, i ^ k) for i in range(groups)])  4.12 us
    ppermute x2, waiting for transfers between devices, local_one(): over_y = [lax.ppermute(x, 'tensor', across) for x in own]  3.29 us
    ppermute x2, starting transfers between devices, local_one(): over_y = [lax.ppermute(x, 'tensor', across) for x in own]  3.15 us
    ppermute x1, starting transfers between devices, local_one(): across_in = lax.ppermute(over_part + far_in, 'tensor', across)  2.95 us
    ppermute x1, waiting for transfers between devices, local_one(): across_in = lax.ppermute(over_part + far_in, 'tensor', across)  2.63 us
  transfers between devices with their start and end apart: 16, of which 7 were waited for; matrix products, arithmetic and copies ran while one was open for 0% of the time, Pallas kernels for 5%

profile of v4, /device:TPU:0, one launch (start us, length us, event | category | flops | bytes accessed | tf_op | source)
XLA Modules:
  0.0 57.7 jit_solution(13230924999903045009)
XLA Ops:
  0.0 7.5 %project.1 = (f32[384,128]{1,0:T(8,128)S(1)}, f32[384,128]{1,0:T(8,128)S(1)}, f32[384,128]{1,0:T(8,128)S(1)}, f32[384,128]{1,0:T(8,128)S(1)}, s32[64]{0:T(128)S(4)}, /*index=5*/s32[1,64]{1,0:T(1,128)}) custom-call(s32[1,64]{1,0:T(1,128)} %bitcast.16, bf16[1536,3584]{1,0:T(8,128)(2,1)} %bitcast.11, bf16[1536,1024]{1,0:T(8,128)(2,1)} %bitcast.13, ...), custom_call_target="tpu_custom_call" | custom-call | flops 905969664 | bytes 14155776 | tf_op jit(solution)/shard_map/project/pallas_call | solution.py:122
  7.6 0.5 collective-permute-start.1
  8.1 0.1 collective-permute-start
  8.2 1.0 %collective-permute-done.1 = f32[384,128]{1,0:T(8,128)S(1)} collective-permute-done((f32[384,128]{1,0:T(8,128)S(1)}, f32[384,128]{1,0:T(8,128)S(1)}, u32[]{:S(2)}, u32[]{:S(2)}) %collective-permute-start.1) | collective-permute-done | bytes 196640 | tf_op jit(solution)/shard_map/ppermute | solution.py:397
  9.2 3.0 %collective-permute-start.2 = (f32[384,128]{1,0:T(8,128)S(1)}, f32[384,128]{1,0:T(8,128)S(1)}, u32[]{:S(2)}, u32[]{:S(2)}) collective-permute-start(f32[384,128]{1,0:T(8,128)S(1)} %add.3), channel_id=1, source_target_pairs={{0,2},{1,3},{2,0},{3,1},{4,6},{5,7},{6,4},{7,5},{8,10},{9,11},{10,... | collective-permute-start | bytes 589832 | tf_op jit(solution)/shard_map/ppermute | solution.py:399
  12.1 0.0 collective-permute-done.b_ref
  12.1 2.6 %own_sum.1 = (s32[16]{0:T(128)S(4)}, f32[384,128]{1,0:T(8,128)S(1)}, bf16[4,640,1024]{2,1,0:T(8,128)(2,1)S(1)}) custom-call(s32[64]{0:T(128)S(4)} %get-tuple-element.23.slot_ref, f32[384,128]{1,0:T(8,128)S(1)} %get-tuple-element.24.a_ref, f32[384,128]{1,0:T(8,128)S(1)} %collective-permute-done.b_ref, bf16[640,4096]{1,0:T(8,128)(2,1)} %bitcast.12), custom_call_target="tpu_custom_call" | custom-call | flops 49152 | bytes 5242880 | tf_op jit(solution)/shard_map/own_sum/pallas_call | solution.py:177
  14.7 0.0 copy-start
  14.7 2.6 %collective-permute-done.2.b_ref = f32[384,128]{1,0:T(8,128)S(1)} collective-permute-done((f32[384,128]{1,0:T(8,128)S(1)}, f32[384,128]{1,0:T(8,128)S(1)}, u32[]{:S(2)}, u32[]{:S(2)}) %collective-permute-start.2) | collective-permute-done | bytes 196640 | tf_op jit(solution)/shard_map/ppermute | solution.py:399
  17.3 1.4 %unit_grads.1 = (bf16[160,128]{1,0:T(8,128)(2,1)S(1)}, bf16[160,128]{1,0:T(8,128)(2,1)S(1)}, bf16[160,128]{1,0:T(8,128)(2,1)S(1)}, bf16[160,128]{1,0:T(8,128)(2,...) custom-call(s32[16]{0:T(128)S(4)} %get-tuple-element.26.row_ref, ...), custom_call_target="tpu_custom_call" | custom-call | flops 20000000 | bytes 1000000 | tf_op jit(solution)/shard_map/unit_grads/pallas_call | solution.py:229
  18.7 1.8 %collective-permute-start.7 = (bf16[160,128]{1,0:T(8,128)(2,1)S(1)}, bf16[160,128]{1,0:T(8,128)(2,1)S(1)}, u32[]{:S(2)}, u32[]{:S(2)}) collective-permute-start(bf16[160,128]{1,0:T(8,128)(2,1)S(1)} %get-tuple-element.34), channel_id=1, source_target_pairs={{0,4},{4,0},{8,12},{12,8},{16,20},{20,16},{24,28},{28,24},{1,5},{5... | collective-permute-start | bytes 122888 | tf_op jit(solution)/shard_map/ppermute | solution.py:407
  20.5 1.5 %collective-permute-start.8 = (bf16[160,128]{1,0:T(8,128)(2,1)S(1)}, bf16[160,128]{1,0:T(8,128)(2,1)S(1)}, u32[]{:S(2)}, u32[]{:S(2)}) collective-permute-start(bf16[160,128]{1,0:T(8,128)(2,1)S(1)} %get-tuple-element.35), channel_id=1, source_target_pairs={{0,12},{4,8},{8,4},{12,0},{16,28},{20,24},{24,20},{28,16},{1,13},{... | collective-permute-start | bytes 122888 | tf_op jit(solution)/shard_map/ppermute | solution.py:407
  22.0 3.5 %collective-permute-start.9 = (bf16[160,128]{1,0:T(8,128)(2,1)S(1)}, bf16[160,128]{1,0:T(8,128)(2,1)S(1)}, u32[]{:S(2)}, u32[]{:S(2)}) collective-permute-start(bf16[160,128]{1,0:T(8,128)(2,1)S(1)} %get-tuple-element.36), channel_id=1, source_target_pairs={{0,20},{4,16},{8,28},{12,24},{16,4},{20,0},{24,12},{28,8},{1,21},{... | collective-permute-start | bytes 122888 | tf_op jit(solution)/shard_map/ppermute | solution.py:407
  25.6 0.0 collective-permute-start.10
  25.6 0.9 %collective-permute-start.3 = (bf16[160,128]{1,0:T(8,128)(2,1)S(1)}, bf16[160,128]{1,0:T(8,128)(2,1)S(1)}, u32[]{:S(2)}, u32[]{:S(2)}) collective-permute-start(bf16[160,128]{1,0:T(8,128)(2,1)S(1)} %get-tuple-element.31), channel_id=1, source_target_pairs={{0,8},{4,12},{8,0},{12,4},{16,24},{20,28},{24,16},{28,20},{1,9},{5... | collective-permute-start | bytes 122888 | tf_op jit(solution)/shard_map/ppermute | solution.py:407
  26.4 0.0 collective-permute-done.7
  26.4 3.5 %collective-permute-start.4 = (bf16[160,128]{1,0:T(8,128)(2,1)S(1)}, bf16[160,128]{1,0:T(8,128)(2,1)S(1)}, u32[]{:S(2)}, u32[]{:S(2)}) collective-permute-start(bf16[160,128]{1,0:T(8,128)(2,1)S(1)} %get-tuple-element.32), channel_id=1, source_target_pairs={{0,16},{4,20},{8,24},{12,28},{16,0},{20,4},{24,8},{28,12},{1,17},{... | collective-permute-start | bytes 122888 | tf_op jit(solution)/shard_map/ppermute | solution.py:407
  29.9 0.0 collective-permute-done.8
  29.9 0.0 collective-permute-start.5
  30.0 0.0 collective-permute-done.9
  30.0 2.3 %collective-permute-done.10 = bf16[160,128]{1,0:T(8,128)(2,1)S(1)} collective-permute-done((bf16[160,128]{1,0:T(8,128)(2,1)S(1)}, bf16[160,128]{1,0:T(8,128)(2,1)S(1)}, u32[]{:S(2)}, u32[]{:S(2)}) %collective-permute-start.10) | collective-permute-done | bytes 40992 | tf_op jit(solution)/shard_map/ppermute | solution.py:407
  32.3 1.6 %collective-permute-start.11 = (bf16[640,128]{1,0:T(8,128)(2,1)S(1)}, bf16[640,128]{1,0:T(8,128)(2,1)S(1)}, u32[]{:S(2)}, u32[]{:S(2)}) collective-permute-start(bf16[640,128]{1,0:T(8,128)(2,1)S(1)} %constant_dynamic-update-slice_fusion.4.rest_1_), channel_id=1, source_target_pairs={{0,2},{1,3},{2,0},{3,1},{4,6},{5,7},{6,4},{7,5},{8,10},{9,11},{10,... | collective-permute-start | bytes 491528 | tf_op jit(solution)/shard_map/ppermute | solution.py:409
  33.8 0.0 collective-permute-done.3
  33.9 0.0 collective-permute-done.4
  33.9 1.8 %collective-permute-done.5 = bf16[160,128]{1,0:T(8,128)(2,1)S(1)} collective-permute-done((bf16[160,128]{1,0:T(8,128)(2,1)S(1)}, bf16[160,128]{1,0:T(8,128)(2,1)S(1)}, u32[]{:S(2)}, u32[]{:S(2)}) %collective-permute-start.5) | collective-permute-done | bytes 40992 | tf_op jit(solution)/shard_map/ppermute | solution.py:407
  35.7 1.6 %collective-permute-start.6 = (bf16[640,128]{1,0:T(8,128)(2,1)S(1)}, bf16[640,128]{1,0:T(8,128)(2,1)S(1)}, u32[]{:S(2)}, u32[]{:S(2)}) collective-permute-start(bf16[640,128]{1,0:T(8,128)(2,1)S(1)} %constant_dynamic-update-slice_fusion.rest_0_), channel_id=1, source_target_pairs={{0,2},{1,3},{2,0},{3,1},{4,6},{5,7},{6,4},{7,5},{8,10},{9,11},{10,... | collective-permute-start | bytes 491528 | tf_op jit(solution)/shard_map/ppermute | solution.py:409
  37.3 0.0 collective-permute-start.15
  37.3 0.5 collective-permute-start.14
  37.8 0.9 %collective-permute-done.11.rest_1_ = bf16[640,128]{1,0:T(8,128)(2,1)S(1)} collective-permute-done((bf16[640,128]{1,0:T(8,128)(2,1)S(1)}, bf16[640,128]{1,0:T(8,128)(2,1)S(1)}, u32[]{:S(2)}, u32[]{:S(2)}) %collective-permute-start.11) | collective-permute-done | bytes 163872 | tf_op jit(solution)/shard_map/ppermute | solution.py:409
  38.7 0.0 collective-permute-start.13
  38.7 2.4 %collective-permute-done.6.rest_0_ = bf16[640,128]{1,0:T(8,128)(2,1)S(1)} collective-permute-done((bf16[640,128]{1,0:T(8,128)(2,1)S(1)}, bf16[640,128]{1,0:T(8,128)(2,1)S(1)}, u32[]{:S(2)}, u32[]{:S(2)}) %collective-permute-start.6) | collective-permute-done | bytes 163872 | tf_op jit(solution)/shard_map/ppermute | solution.py:409
  41.1 0.0 collective-permute-start.12
  41.1 0.0 collective-permute-done.15.rest_3_
  41.1 0.0 collective-permute-done.14.rest_2_
  41.1 0.4 staged.1.rest_4_
  41.5 0.0 collective-permute-done.13.rest_3_
  41.6 1.0 %collective-permute-done.12.rest_2_ = bf16[640,128]{1,0:T(8,128)(2,1)S(1)} collective-permute-done((bf16[640,128]{1,0:T(8,128)(2,1)S(1)}, bf16[640,128]{1,0:T(8,128)(2,1)S(1)}, u32[]{:S(2)}, u32[]{:S(2)}) %collective-permute-start.12) | collective-permute-done | bytes 163872 | tf_op jit(solution)/shard_map/ppermute | solution.py:412
  42.5 2.6 %scores.1 = bf16[192,640]{1,0:T(8,128)(2,1)S(1)} custom-call(bf16[640,128]{1,0:T(8,128)(2,1)S(1)} %collective-permute-done.6.rest_0_, bf16[640,128]{1,0:T(8,128)(2,1)S(1)} %collective-permute-done.11.rest_1_, bf16[640,128]{1,0:T(8,128)(2,1)S(1)} %collective-permute-done.12.rest_2_, bf16[640,128]{1,0:T(8,128)(2,1)S(1)} %collective-permute-done.13.rest_3_, ...), custom_call_target="tpu_custom_call" | custom-call | flops 838860800 | bytes 5242880 | tf_op jit(solution)/shard_map/scores/pallas_call | solution.py:329
  45.1 11.7 %all_to_all.5 = bf16[8,24,640]{2,1,0:T(8,128)(2,1)S(1)} all-to-all(bf16[8,24,640]{2,1,0:T(8,128)(2,1)S(1)} %bitcast.9), channel_id=1, replica_groups=mesh['dp'=8,'tensor'=4] {'dp'}, dimensions={0} | all-to-all | bytes 491520 | tf_op jit(solution)/shard_map/all_to_all | solution.py:415
  56.8 0.0 copy-done
  56.8 0.9 %pick_rows.1 = f32[320,128]{1,0:T(8,128)} custom-call(s32[1,64]{1,0:T(1,128)S(1)} %copy-done, bf16[192,640]{1,0:T(8,128)(2,1)S(1)} %bitcast.10), custom_call_target="tpu_custom_call" | custom-call | flops 16000000 | bytes 400000 | tf_op jit(solution)/shard_map/pick_rows/pallas_call | solution.py:361
  (9 shorter events, 0.1 us)
Async XLA Ops:
  7.6 1.6 %collective-permute-start.1 = (f32[384,128]{1,0:T(8,128)S(1)}, f32[384,128]{1,0:T(8,128)S(1)}, u32[]{:S(2)}, u32[]{:S(2)}) collective-permute-start(f32[384,128]{1,0:T(8,128)S(1)} %get-tuple-element.29), channel_id=1, source_target_pairs={{0,1},{1,0},{2,3},{3,2},{4,5},{5,4},{6,7},{7,6},{8,9},{9,8},{10,11... | collective-permute-start | bytes 589832 | tf_op jit(solution)/shard_map/ppermute | solution.py:397
  8.1 4.0 %collective-permute-start = (f32[384,128]{1,0:T(8,128)S(1)}, f32[384,128]{1,0:T(8,128)S(1)}, u32[]{:S(2)}, u32[]{:S(2)}) collective-permute-start(f32[384,128]{1,0:T(8,128)S(1)} %get-tuple-element.25), channel_id=1, source_target_pairs={{0,1},{1,0},{2,3},{3,2},{4,5},{5,4},{6,7},{7,6},{8,9},{9,8},{10,11... | collective-permute-start | bytes 589832 | tf_op jit(solution)/shard_map/ppermute | solution.py:398
  9.2 8.2 %collective-permute-start.2 = (f32[384,128]{1,0:T(8,128)S(1)}, f32[384,128]{1,0:T(8,128)S(1)}, u32[]{:S(2)}, u32[]{:S(2)}) collective-permute-start(f32[384,128]{1,0:T(8,128)S(1)} %add.3), channel_id=1, source_target_pairs={{0,2},{1,3},{2,0},{3,1},{4,6},{5,7},{6,4},{7,5},{8,10},{9,11},{10,... | collective-permute-start | bytes 589832 | tf_op jit(solution)/shard_map/ppermute | solution.py:399
  14.7 42.1 %copy-start = (s32[1,64]{1,0:T(1,128)S(1)}, s32[1,64]{1,0:T(1,128)}, u32[]{:S(2)}) copy-start(s32[1,64]{1,0:T(1,128)} %get-tuple-element.22.row_ref) | copy-start | bytes 772
  18.7 7.7 %collective-permute-start.7 = (bf16[160,128]{1,0:T(8,128)(2,1)S(1)}, bf16[160,128]{1,0:T(8,128)(2,1)S(1)}, u32[]{:S(2)}, u32[]{:S(2)}) collective-permute-start(bf16[160,128]{1,0:T(8,128)(2,1)S(1)} %get-tuple-element.34), channel_id=1, source_target_pairs={{0,4},{4,0},{8,12},{12,8},{16,20},{20,16},{24,28},{28,24},{1,5},{5... | collective-permute-start | bytes 122888 | tf_op jit(solution)/shard_map/ppermute | solution.py:407
  20.5 9.4 %collective-permute-start.8 = (bf16[160,128]{1,0:T(8,128)(2,1)S(1)}, bf16[160,128]{1,0:T(8,128)(2,1)S(1)}, u32[]{:S(2)}, u32[]{:S(2)}) collective-permute-start(bf16[160,128]{1,0:T(8,128)(2,1)S(1)} %get-tuple-element.35), channel_id=1, source_target_pairs={{0,12},{4,8},{8,4},{12,0},{16,28},{20,24},{24,20},{28,16},{1,13},{... | collective-permute-start | bytes 122888 | tf_op jit(solution)/shard_map/ppermute | solution.py:407
  22.0 7.9 %collective-permute-start.9 = (bf16[160,128]{1,0:T(8,128)(2,1)S(1)}, bf16[160,128]{1,0:T(8,128)(2,1)S(1)}, u32[]{:S(2)}, u32[]{:S(2)}) collective-permute-start(bf16[160,128]{1,0:T(8,128)(2,1)S(1)} %get-tuple-element.36), channel_id=1, source_target_pairs={{0,20},{4,16},{8,28},{12,24},{16,4},{20,0},{24,12},{28,8},{1,21},{... | collective-permute-start | bytes 122888 | tf_op jit(solution)/shard_map/ppermute | solution.py:407
  25.6 6.7 %collective-permute-start.10 = (bf16[160,128]{1,0:T(8,128)(2,1)S(1)}, bf16[160,128]{1,0:T(8,128)(2,1)S(1)}, u32[]{:S(2)}, u32[]{:S(2)}) collective-permute-start(bf16[160,128]{1,0:T(8,128)(2,1)S(1)} %get-tuple-element.37), channel_id=1, source_target_pairs={{0,28},{4,24},{8,20},{12,16},{16,12},{20,8},{24,4},{28,0},{1,29},{... | collective-permute-start | bytes 122888 | tf_op jit(solution)/shard_map/ppermute | solution.py:407
  25.6 8.3 %collective-permute-start.3 = (bf16[160,128]{1,0:T(8,128)(2,1)S(1)}, bf16[160,128]{1,0:T(8,128)(2,1)S(1)}, u32[]{:S(2)}, u32[]{:S(2)}) collective-permute-start(bf16[160,128]{1,0:T(8,128)(2,1)S(1)} %get-tuple-element.31), channel_id=1, source_target_pairs={{0,8},{4,12},{8,0},{12,4},{16,24},{20,28},{24,16},{28,20},{1,9},{5... | collective-permute-start | bytes 122888 | tf_op jit(solution)/shard_map/ppermute | solution.py:407
  26.4 7.4 %collective-permute-start.4 = (bf16[160,128]{1,0:T(8,128)(2,1)S(1)}, bf16[160,128]{1,0:T(8,128)(2,1)S(1)}, u32[]{:S(2)}, u32[]{:S(2)}) collective-permute-start(bf16[160,128]{1,0:T(8,128)(2,1)S(1)} %get-tuple-element.32), channel_id=1, source_target_pairs={{0,16},{4,20},{8,24},{12,28},{16,0},{20,4},{24,8},{28,12},{1,17},{... | collective-permute-start | bytes 122888 | tf_op jit(solution)/shard_map/ppermute | solution.py:407
  29.9 5.8 %collective-permute-start.5 = (bf16[160,128]{1,0:T(8,128)(2,1)S(1)}, bf16[160,128]{1,0:T(8,128)(2,1)S(1)}, u32[]{:S(2)}, u32[]{:S(2)}) collective-permute-start(bf16[160,128]{1,0:T(8,128)(2,1)S(1)} %get-tuple-element.33), channel_id=1, source_target_pairs={{0,24},{4,28},{8,16},{12,20},{16,8},{20,12},{24,0},{28,4},{1,25},{... | collective-permute-start | bytes 122888 | tf_op jit(solution)/shard_map/ppermute | solution.py:407
  32.3 6.5 %collective-permute-start.11 = (bf16[640,128]{1,0:T(8,128)(2,1)S(1)}, bf16[640,128]{1,0:T(8,128)(2,1)S(1)}, u32[]{:S(2)}, u32[]{:S(2)}) collective-permute-start(bf16[640,128]{1,0:T(8,128)(2,1)S(1)} %constant_dynamic-update-slice_fusion.4.rest_1_), channel_id=1, source_target_pairs={{0,2},{1,3},{2,0},{3,1},{4,6},{5,7},{6,4},{7,5},{8,10},{9,11},{10,... | collective-permute-start | bytes 491528 | tf_op jit(solution)/shard_map/ppermute | solution.py:409
  35.7 5.4 %collective-permute-start.6 = (bf16[640,128]{1,0:T(8,128)(2,1)S(1)}, bf16[640,128]{1,0:T(8,128)(2,1)S(1)}, u32[]{:S(2)}, u32[]{:S(2)}) collective-permute-start(bf16[640,128]{1,0:T(8,128)(2,1)S(1)} %constant_dynamic-update-slice_fusion.rest_0_), channel_id=1, source_target_pairs={{0,2},{1,3},{2,0},{3,1},{4,6},{5,7},{6,4},{7,5},{8,10},{9,11},{10,... | collective-permute-start | bytes 491528 | tf_op jit(solution)/shard_map/ppermute | solution.py:409
  37.3 3.8 %collective-permute-start.15 = (bf16[640,128]{1,0:T(8,128)(2,1)S(1)}, bf16[640,128]{1,0:T(8,128)(2,1)S(1)}, u32[]{:S(2)}, u32[]{:S(2)}) collective-permute-start(bf16[640,128]{1,0:T(8,128)(2,1)S(1)} %constant_dynamic-update-slice_fusion.4.rest_1_), channel_id=1, source_target_pairs={{0,1},{1,0},{2,3},{3,2},{4,5},{5,4},{6,7},{7,6},{8,9},{9,8},{10,11... | collective-permute-start | bytes 491528 | tf_op jit(solution)/shard_map/ppermute | solution.py:410
  37.3 3.8 %collective-permute-start.14 = (bf16[640,128]{1,0:T(8,128)(2,1)S(1)}, bf16[640,128]{1,0:T(8,128)(2,1)S(1)}, u32[]{:S(2)}, u32[]{:S(2)}) collective-permute-start(bf16[640,128]{1,0:T(8,128)(2,1)S(1)} %constant_dynamic-update-slice_fusion.rest_0_), channel_id=1, source_target_pairs={{0,1},{1,0},{2,3},{3,2},{4,5},{5,4},{6,7},{7,6},{8,9},{9,8},{10,11... | collective-permute-start | bytes 491528 | tf_op jit(solution)/shard_map/ppermute | solution.py:410
  38.7 2.8 %collective-permute-start.13 = (bf16[640,128]{1,0:T(8,128)(2,1)S(1)}, bf16[640,128]{1,0:T(8,128)(2,1)S(1)}, u32[]{:S(2)}, u32[]{:S(2)}) collective-permute-start(bf16[640,128]{1,0:T(8,128)(2,1)S(1)} %collective-permute-done.11.rest_1_), channel_id=1, source_target_pairs={{0,1},{1,0},{2,3},{3,2},{4,5},{5,4},{6,7},{7,6},{8,9},{9,8},{10,11... | collective-permute-start | bytes 491528 | tf_op jit(solution)/shard_map/ppermute | solution.py:412
  41.1 1.4 %collective-permute-start.12 = (bf16[640,128]{1,0:T(8,128)(2,1)S(1)}, bf16[640,128]{1,0:T(8,128)(2,1)S(1)}, u32[]{:S(2)}, u32[]{:S(2)}) collective-permute-start(bf16[640,128]{1,0:T(8,128)(2,1)S(1)} %collective-permute-done.6.rest_0_), channel_id=1, source_target_pairs={{0,1},{1,0},{2,3},{3,2},{4,5},{5,4},{6,7},{7,6},{8,9},{9,8},{10,11... | collective-permute-start | bytes 491528 | tf_op jit(solution)/shard_map/ppermute | solution.py:412

commit v5 on v4

--- a/solution.py
+++ b/solution.py
@@ -115,7 +115,7 @@
     rows = act.shape[0]
     pieces = 8
     step = rows // pieces
-    blocks = ((3, 2 * step), (2, step))
+    blocks = ((2, step), (3, 2 * step))
     share = rows // ways
     hbm = pl.BlockSpec(memory_space=pltpu.HBM)
     vmem = pl.BlockSpec(memory_space=pltpu.VMEM)
@@ -202,7 +202,7 @@
     low = lax.broadcasted_iota(jnp.int32, (chunks, LANES), 1) < half
     low_t = lax.broadcasted_iota(jnp.int32, (tokens, LANES), 1) < half
 
-    @pl.loop(0, count, unroll=4)
+    @pl.loop(0, count, unroll=16)
     def _(i):
         part = total[pl.ds(pl.multiple_of(i * tokens, 8), tokens), :]
         twice = jnp.where(low_t, pltpu.roll(part, half, 1), part)
@@ -230,7 +230,7 @@
         functools.partial(unit_kernel, tokens, chunks),
         in_specs=[pl.BlockSpec(memory_space=pltpu.SMEM), whole, whole],
         out_specs=[whole] * groups,
-        out_shape=[jax.ShapeDtypeStruct((rows, LANES), jnp.bfloat16)] * groups,
+        out_shape=[pltpu.VMEM((rows, LANES), jnp.bfloat16)] * groups,
         scratch_shapes=[
             pltpu.VMEM(a.shape, jnp.float32),
             pltpu.VMEM((groups * rows, LANES), jnp.bfloat16),
@@ -241,19 +241,20 @@
     )(slots, a, b)
 
 
-def stage_units(refs, stage, parts, slots, groups):
-    each = stage.shape[1] // (len(refs) // 2 * groups * slots)
+def stage_units(refs, parcels, stage, parts, slots, groups):
+    each = stage.shape[1] // (len(refs) // len(parcels) * groups * slots)
     span = slots * parts * each
     home = lax.axis_index("dp")
-
-    @pl.loop(0, groups // 2)
-    def _(i):
-        for n, ref in enumerate(refs):
-            d = (2 * i + n % 2) ^ home
+    for n, ref in enumerate(refs):
+        parcel = parcels[n % len(parcels)]
+
+        @pl.loop(0, len(parcel))
+        def _(i, n=n, ref=ref, parcel=parcel):
+            d = (parcel.start + parcel.step * i) ^ home
             got = ref[pl.ds(pl.multiple_of(i * span, span), span), :].astype(jnp.float32)
             got = got.reshape(slots, parts, each, LANES)
             for k in range(parts):
-                at = pl.multiple_of((n // 2 * groups + d) * slots * each, each)
+                at = pl.multiple_of((n // len(parcels) * groups + d) * slots * each, each)
                 stage[k, pl.ds(at, slots * each), :] = got[:, k].reshape(slots * each, LANES)
 
 
@@ -265,23 +266,23 @@
         units[at:, j * LANES : (j + 1) * LANES] = piece.astype(jnp.bfloat16)
 
 
-def stage_kernel(groups, slots, *rest):
-    refs, (out_ref, stage) = rest[:4], rest[4:]
+def stage_kernel(groups, slots, parcels, *rest):
+    refs, (out_ref, stage) = rest[:-2], rest[-2:]
     parts = out_ref.shape[0]
-    stage_units(refs, stage, parts, slots, groups)
+    stage_units(refs, parcels, stage, parts, slots, groups)
 
     @pl.loop(0, parts)
     def _(k):
         staged_rows(stage, k, out_ref.at[k], 0)
 
 
-def staged(units, groups, slots, parts):
+def staged(units, parcels, groups, slots, parts):
     rows = 2 * groups * slots
-    width = 2 * units[0].size // (groups * slots * parts)
+    width = sum(x.size for x in units) // (rows * parts)
     vmem = pl.BlockSpec(memory_space=pltpu.VMEM)
     return pl.pallas_call(
-        functools.partial(stage_kernel, groups, slots),
-        in_specs=[vmem] * 4,
+        functools.partial(stage_kernel, groups, slots, parcels),
+        in_specs=[vmem] * len(units),
         out_specs=vmem,
         out_shape=pltpu.VMEM((parts, rows, width), jnp.bfloat16),
         scratch_shapes=[pltpu.VMEM((parts, rows * width // LANES, LANES), jnp.float32)],
@@ -293,11 +294,11 @@
     )(*units)
 
 
-def score_kernel(groups, slots, padded, *rest):
-    refs, (early_ref, q_ref, out_ref, stage, units, total) = rest[:4], rest[4:]
+def score_kernel(groups, slots, padded, parcels, *rest):
+    refs, (early_ref, q_ref, out_ref, stage, units, total) = rest[:-6], rest[-6:]
     parts = q_ref.shape[0]
     half = groups * slots
-    stage_units(refs, stage, parts, slots, groups)
+    stage_units(refs, parcels, stage, parts, slots, groups)
     total[...] = jnp.zeros_like(total)
 
     @pl.loop(0, parts)
@@ -322,15 +323,15 @@
     out_ref[...] = out.astype(out_ref.dtype)
 
 
-def scores_of(late, early, queries, groups, slots, padded):
+def scores_of(late, early, queries, parcels, groups, slots, padded):
     parts, count, width = queries.shape
     half = groups * slots
     vmem = pl.BlockSpec(memory_space=pltpu.VMEM)
     return pl.pallas_call(
-        functools.partial(score_kernel, groups, slots, padded),
-        in_specs=[vmem] * 6,
+        functools.partial(score_kernel, groups, slots, padded, parcels),
+        in_specs=[vmem] * (len(late) + 2),
         out_specs=vmem,
-        out_shape=jax.ShapeDtypeStruct((groups * padded, count), jnp.bfloat16),
+        out_shape=pltpu.VMEM((groups * padded, count), jnp.bfloat16),
         scratch_shapes=[
             pltpu.VMEM((parts, 2 * half * width // LANES, LANES), jnp.float32),
             pltpu.VMEM((4 * half, width), jnp.bfloat16),
@@ -399,18 +400,23 @@
     across_in = lax.ppermute(over_part + far_in, "tensor", across)
 
     here_slots, here, held = own_sum(
-        my_slots, own_part, near_in, query_block, examples // ways, 4
+        my_slots, own_part, near_in, query_block, examples // ways, 1
     )
     units = unit_grads(here_slots, here, across_in, tokens, chunks, groups, slots)
+    parcels = (range(0, groups, 2), range(1, groups, 2))
     arrived = [units[0]] + [None] * (groups - 1)
-    for k in reversed(range(1, groups)):
-        arrived[k] = lax.ppermute(units[k], "dp", [(i, i ^ k) for i in range(groups)])
-    own = [jnp.concatenate(arrived[n::2], axis=0) for n in range(2)]
+    farthest = groups - 1
+    for k in (farthest, *range(groups - 2, 0, -2), *range(groups - 3, 0, -2)):
+        block = units[k]
+        if k % 2 and k < groups // 2:
+            block, _ = lax.optimization_barrier((block, arrived[farthest]))
+        arrived[k] = lax.ppermute(block, "dp", [(i, i ^ k) for i in range(groups)])
+    own = [jnp.concatenate([arrived[k] for k in parcel], axis=0) for parcel in parcels]
     over_y = [lax.ppermute(x, "tensor", across) for x in own]
     over_core = [lax.ppermute(x, "tensor", core) for x in own]
-    early = staged(own + over_core, groups, slots, held.shape[0])
+    early = staged(own + over_core, parcels, groups, slots, held.shape[0])
     over_both = [lax.ppermute(x, "tensor", core) for x in over_y]
-    both = scores_of(over_y + over_both, early, held, groups, slots, padded)
+    both = scores_of(over_y + over_both, early, held, parcels, groups, slots, padded)
     block = both.reshape(groups, padded, both.shape[1])
     returned = lax.all_to_all(block, "dp", split_axis=0, concat_axis=0, tiled=True)
     picked = pick_rows(pick, returned.reshape(both.shape))
@@ -474,7 +480,9 @@
 
 
 def local(activations, out_grads, proj_in, proj_out, queries, candidates):
+    groups = lax.axis_size("dp")
     one = candidates.shape[1] == 1 and lax.axis_size("tensor") == 4
+    one = one and groups >= 4 and groups & (groups - 1) == 0
     return (local_one if one else local_many)(
         activations, out_grads, proj_in, proj_out, queries, candidates
     )

time: 57.8 us -> 55.8 us (0.965)
  waiting for transfers between devices: 12 us -> 10.4 us
  blocking collectives: 11.7 us -> 12.5 us
  Pallas kernels: 15.3 us -> 14.6 us
  starting transfers between devices: 18.5 us -> 17.9 us
    ppermute x7, waiting for transfers between devices: 4.12 us -> 2.4 us  [local_one(): arrived[k] = lax.ppermute(block, 'dp', [(i, i ^ k) for i in range(groups)])]
    all_to_all x1, blocking collectives: 11.7 us -> 12.5 us  [local_one(): lax.all_to_all(block, 'dp', split_axis=0, concat_axis=0, tiled=True)]
    ppermute x2, waiting for transfers between devices: 3.29 us -> 3.98 us  [local_one(): over_y = [lax.ppermute(x, 'tensor', across) for x in own]]
    pallas_call x1, Pallas kernels: 1.37 us -> 0.71 us  [unit_grads(): pl.pallas_call(functools.partial(unit_kernel, tokens, chunks), in_specs=[...]
    ppermute x2, waiting for transfers between devices: 0.96 us -> 0.34 us  [local_one(): over_both = [lax.ppermute(x, 'tensor', core) for x in over_y]]
  transfers between devices with their start and end apart: 16 -> 16, of which waited for: 7 -> 6; matrix products, arithmetic and copies ran while one was open for 0% -> 0% of each run, Pallas kernels for 5% -> 6%
where the time goes in v5:
time: 55.8 us; the launch traced here: 55.6 us
  starting transfers between devices  17.9 us (32%)
  Pallas kernels  14.6 us (26%)
  blocking collectives  12.5 us (22%)
  waiting for transfers between devices  10.4 us (19%)
    all_to_all x1, blocking collectives, local_one(): lax.all_to_all(block, 'dp', split_axis=0, concat_axis=0, tiled=True)  12.5 us
    ppermute x7, starting transfers between devices, local_one(): arrived[k] = lax.ppermute(block, 'dp', [(i, i ^ k) for i in range(groups)])  11.2 us
    pallas_call x1, Pallas kernels, project(): pl.pallas_call(functools.partial(project_kernel, groups, ways, tokens, sl...  7.23 us
    ppermute x2, waiting for transfers between devices, local_one(): over_y = [lax.ppermute(x, 'tensor', across) for x in own]  3.98 us
    ppermute x1, starting transfers between devices, local_one(): across_in = lax.ppermute(over_part + far_in, 'tensor', across)  2.95 us
    ppermute x1, waiting for transfers between devices, local_one(): across_in = lax.ppermute(over_part + far_in, 'tensor', across)  2.69 us
    ppermute x2, starting transfers between devices, local_one(): over_y = [lax.ppermute(x, 'tensor', across) for x in own]  2.64 us
    pallas_call x1, Pallas kernels, own_sum(): pl.pallas_call(own_kernel, in_specs=[smem, vmem, vmem, pl.BlockSpec(memor...  2.5 us
  transfers between devices with their start and end apart: 16, of which 6 were waited for; matrix products, arithmetic and copies ran while one was open for 0% of the time, Pallas kernels for 6%

profile of v5, /device:TPU:0, one launch (start us, length us, event | category | flops | bytes accessed | tf_op | source)
XLA Modules:
  0.0 55.6 jit_solution(16486293834739126734)
XLA Ops:
  0.0 7.2 %project.1 = (f32[384,128]{1,0:T(8,128)S(1)}, f32[384,128]{1,0:T(8,128)S(1)}, f32[384,128]{1,0:T(8,128)S(1)}, f32[384,128]{1,0:T(8,128)S(1)}, s32[64]{0:T(128)S(4)}, /*index=5*/s32[1,64]{1,0:T(1,128)}) custom-call(s32[1,64]{1,0:T(1,128)} %bitcast.16, bf16[1536,3584]{1,0:T(8,128)(2,1)} %bitcast.11, bf16[1536,1024]{1,0:T(8,128)(2,1)} %bitcast.13, ...), custom_call_target="tpu_custom_call" | custom-call | flops 905969664 | bytes 14155776 | tf_op jit(solution)/shard_map/project/pallas_call | solution.py:122
  7.2 0.5 collective-permute-start.1
  7.8 0.1 collective-permute-start
  7.8 1.0 %collective-permute-done.1 = f32[384,128]{1,0:T(8,128)S(1)} collective-permute-done((f32[384,128]{1,0:T(8,128)S(1)}, f32[384,128]{1,0:T(8,128)S(1)}, u32[]{:S(2)}, u32[]{:S(2)}) %collective-permute-start.1) | collective-permute-done | bytes 196640 | tf_op jit(solution)/shard_map/ppermute | solution.py:398
  8.8 3.0 %collective-permute-start.2 = (f32[384,128]{1,0:T(8,128)S(1)}, f32[384,128]{1,0:T(8,128)S(1)}, u32[]{:S(2)}, u32[]{:S(2)}) collective-permute-start(f32[384,128]{1,0:T(8,128)S(1)} %add.3), channel_id=1, source_target_pairs={{0,2},{1,3},{2,0},{3,1},{4,6},{5,7},{6,4},{7,5},{8,10},{9,11},{10,... | collective-permute-start | bytes 589832 | tf_op jit(solution)/shard_map/ppermute | solution.py:400
  11.8 0.0 collective-permute-done.b_ref
  11.8 2.5 %own_sum.1 = (s32[16]{0:T(128)S(4)}, f32[384,128]{1,0:T(8,128)S(1)}, bf16[1,640,4096]{2,1,0:T(8,128)(2,1)S(1)}) custom-call(s32[64]{0:T(128)S(4)} %get-tuple-element.25.slot_ref, f32[384,128]{1,0:T(8,128)S(1)} %get-tuple-element.26.a_ref, f32[384,128]{1,0:T(8,128)S(1)} %collective-permute-done.b_ref, bf16[640,4096]{1,0:T(8,128)(2,1)} %bitcast.12), custom_call_target="tpu_custom_call" | custom-call | flops 49152 | bytes 5242880 | tf_op jit(solution)/shard_map/own_sum/pallas_call | solution.py:177
  14.3 0.0 copy-start
  14.3 2.7 %collective-permute-done.2.b_ref = f32[384,128]{1,0:T(8,128)S(1)} collective-permute-done((f32[384,128]{1,0:T(8,128)S(1)}, f32[384,128]{1,0:T(8,128)S(1)}, u32[]{:S(2)}, u32[]{:S(2)}) %collective-permute-start.2) | collective-permute-done | bytes 196640 | tf_op jit(solution)/shard_map/ppermute | solution.py:400
  17.0 0.7 %unit_grads.1 = (bf16[160,128]{1,0:T(8,128)(2,1)S(1)}, bf16[160,128]{1,0:T(8,128)(2,1)S(1)}, bf16[160,128]{1,0:T(8,128)(2,1)S(1)}, bf16[160,128]{1,0:T(8,128)(2,...) custom-call(s32[16]{0:T(128)S(4)} %get-tuple-element.28.row_ref, ...), custom_call_target="tpu_custom_call" | custom-call | flops 20000000 | bytes 1000000 | tf_op jit(solution)/shard_map/unit_grads/pallas_call | solution.py:229
  17.7 4.8 %collective-permute-start.7 = (bf16[160,128]{1,0:T(8,128)(2,1)S(1)}, bf16[160,128]{1,0:T(8,128)(2,1)S(1)}, u32[]{:S(2)}, u32[]{:S(2)}) collective-permute-start(bf16[160,128]{1,0:T(8,128)(2,1)S(1)} %get-tuple-element.37), channel_id=1, source_target_pairs={{0,28},{4,24},{8,20},{12,16},{16,12},{20,8},{24,4},{28,0},{1,29},{... | collective-permute-start | bytes 122888 | tf_op jit(solution)/shard_map/ppermute | solution.py:413
  22.5 0.0 collective-permute-start.10
  22.5 0.6 %collective-permute-start.3 = (bf16[160,128]{1,0:T(8,128)(2,1)S(1)}, bf16[160,128]{1,0:T(8,128)(2,1)S(1)}, u32[]{:S(2)}, u32[]{:S(2)}) collective-permute-start(bf16[160,128]{1,0:T(8,128)(2,1)S(1)} %get-tuple-element.33), channel_id=1, source_target_pairs={{0,8},{4,12},{8,0},{12,4},{16,24},{20,28},{24,16},{28,20},{1,9},{5... | collective-permute-start | bytes 122888 | tf_op jit(solution)/shard_map/ppermute | solution.py:413
  23.2 2.3 %collective-permute-start.4 = (bf16[160,128]{1,0:T(8,128)(2,1)S(1)}, bf16[160,128]{1,0:T(8,128)(2,1)S(1)}, u32[]{:S(2)}, u32[]{:S(2)}) collective-permute-start(bf16[160,128]{1,0:T(8,128)(2,1)S(1)} %get-tuple-element.34), channel_id=1, source_target_pairs={{0,16},{4,20},{8,24},{12,28},{16,0},{20,4},{24,8},{28,12},{1,17},{... | collective-permute-start | bytes 122888 | tf_op jit(solution)/shard_map/ppermute | solution.py:413
  25.4 1.5 %collective-permute-start.5 = (bf16[160,128]{1,0:T(8,128)(2,1)S(1)}, bf16[160,128]{1,0:T(8,128)(2,1)S(1)}, u32[]{:S(2)}, u32[]{:S(2)}) collective-permute-start(bf16[160,128]{1,0:T(8,128)(2,1)S(1)} %get-tuple-element.35), channel_id=1, source_target_pairs={{0,24},{4,28},{8,16},{12,20},{16,8},{20,12},{24,0},{28,4},{1,25},{... | collective-permute-start | bytes 122888 | tf_op jit(solution)/shard_map/ppermute | solution.py:413
  26.9 0.0 collective-permute-done.7
  26.9 1.5 %collective-permute-start.9 = (bf16[160,128]{1,0:T(8,128)(2,1)S(1)}, bf16[160,128]{1,0:T(8,128)(2,1)S(1)}, u32[]{:S(2)}, u32[]{:S(2)}) collective-permute-start(bf16[160,128]{1,0:T(8,128)(2,1)S(1)} %get-tuple-element.40), channel_id=1, source_target_pairs={{0,12},{4,8},{8,4},{12,0},{16,28},{20,24},{24,20},{28,16},{1,13},{... | collective-permute-start | bytes 122888 | tf_op jit(solution)/shard_map/ppermute | solution.py:413
  28.4 0.0 collective-permute-done.3
  28.4 0.5 collective-permute-start.8
  29.0 0.0 collective-permute-done.4
  29.0 2.3 %collective-permute-done.5 = bf16[160,128]{1,0:T(8,128)(2,1)S(1)} collective-permute-done((bf16[160,128]{1,0:T(8,128)(2,1)S(1)}, bf16[160,128]{1,0:T(8,128)(2,1)S(1)}, u32[]{:S(2)}, u32[]{:S(2)}) %collective-permute-start.5) | collective-permute-done | bytes 40992 | tf_op jit(solution)/shard_map/ppermute | solution.py:413
  31.4 1.6 %collective-permute-start.6 = (bf16[640,128]{1,0:T(8,128)(2,1)S(1)}, bf16[640,128]{1,0:T(8,128)(2,1)S(1)}, u32[]{:S(2)}, u32[]{:S(2)}) collective-permute-start(bf16[640,128]{1,0:T(8,128)(2,1)S(1)} %constant_dynamic-update-slice_fusion.rest_0_), channel_id=1, source_target_pairs={{0,2},{1,3},{2,0},{3,1},{4,6},{5,7},{6,4},{7,5},{8,10},{9,11},{10,... | collective-permute-start | bytes 491528 | tf_op jit(solution)/shard_map/ppermute | solution.py:415
  32.9 0.0 collective-permute-done.8
  32.9 0.0 collective-permute-done.9
  33.0 0.0 collective-permute-done.10
  33.0 1.1 %collective-permute-start.11 = (bf16[640,128]{1,0:T(8,128)(2,1)S(1)}, bf16[640,128]{1,0:T(8,128)(2,1)S(1)}, u32[]{:S(2)}, u32[]{:S(2)}) collective-permute-start(bf16[640,128]{1,0:T(8,128)(2,1)S(1)} %constant_dynamic-update-slice_fusion.4.rest_1_), channel_id=1, source_target_pairs={{0,2},{1,3},{2,0},{3,1},{4,6},{5,7},{6,4},{7,5},{8,10},{9,11},{10,... | collective-permute-start | bytes 491528 | tf_op jit(solution)/shard_map/ppermute | solution.py:415
  34.1 0.0 collective-permute-start.14
  34.1 0.5 collective-permute-start.15
  34.6 2.2 %collective-permute-done.6.rest_0_ = bf16[640,128]{1,0:T(8,128)(2,1)S(1)} collective-permute-done((bf16[640,128]{1,0:T(8,128)(2,1)S(1)}, bf16[640,128]{1,0:T(8,128)(2,1)S(1)}, u32[]{:S(2)}, u32[]{:S(2)}) %collective-permute-start.6) | collective-permute-done | bytes 163872 | tf_op jit(solution)/shard_map/ppermute | solution.py:415
  36.8 0.0 collective-permute-start.12
  36.8 1.8 %collective-permute-done.11.rest_1_ = bf16[640,128]{1,0:T(8,128)(2,1)S(1)} collective-permute-done((bf16[640,128]{1,0:T(8,128)(2,1)S(1)}, bf16[640,128]{1,0:T(8,128)(2,1)S(1)}, u32[]{:S(2)}, u32[]{:S(2)}) %collective-permute-start.11) | collective-permute-done | bytes 163872 | tf_op jit(solution)/shard_map/ppermute | solution.py:415
  38.6 0.0 collective-permute-start.13
  38.6 0.0 collective-permute-done.14.rest_2_
  38.6 0.0 collective-permute-done.15.rest_3_
  38.6 1.0 %staged.1.rest_4_ = bf16[1,80,4096]{2,1,0:T(8,128)(2,1)S(1)} custom-call(bf16[640,128]{1,0:T(8,128)(2,1)S(1)} %constant_dynamic-update-slice_fusion.rest_0_, bf16[640,128]{1,0:T(8,128)(2,1)S(1)} %constant_dynamic-update-slice_fusion.4.rest_1_, bf16[640,128]{1,0:T(8,128)(2,1)S(1)} %collective-permute-done.14.rest_2_, ...), custom_call_target="tpu_custom_call" | custom-call | flops 327680 | bytes 2621440 | tf_op jit(solution)/shard_map/staged/pallas_call | solution.py:283
  39.6 0.0 collective-permute-done.12.rest_2_
  39.6 0.3 collective-permute-done.13.rest_3_
  40.0 2.2 %scores.1 = bf16[192,640]{1,0:T(8,128)(2,1)S(1)} custom-call(bf16[640,128]{1,0:T(8,128)(2,1)S(1)} %collective-permute-done.6.rest_0_, bf16[640,128]{1,0:T(8,128)(2,1)S(1)} %collective-permute-done.11.rest_1_, bf16[640,128]{1,0:T(8,128)(2,1)S(1)} %collective-permute-done.12.rest_2_, bf16[640,128]{1,0:T(8,128)(2,1)S(1)} %collective-permute-done.13.rest_3_, ...), custom_call_target="tpu_custom_call" | custom-call | flops 838860800 | bytes 5242880 | tf_op jit(solution)/shard_map/scores/pallas_call | solution.py:330
  42.2 12.5 %all_to_all.5 = bf16[8,24,640]{2,1,0:T(8,128)(2,1)S(1)} all-to-all(bf16[8,24,640]{2,1,0:T(8,128)(2,1)S(1)} %bitcast.9), channel_id=1, replica_groups=mesh['dp'=8,'tensor'=4] {'dp'}, dimensions={0} | all-to-all | bytes 491520 | tf_op jit(solution)/shard_map/all_to_all | solution.py:421
  54.7 0.0 copy-done
  54.7 0.9 %pick_rows.1 = f32[320,128]{1,0:T(8,128)} custom-call(s32[1,64]{1,0:T(1,128)S(1)} %copy-done, bf16[192,640]{1,0:T(8,128)(2,1)S(1)} %bitcast.10), custom_call_target="tpu_custom_call" | custom-call | flops 16000000 | bytes 400000 | tf_op jit(solution)/shard_map/pick_rows/pallas_call | solution.py:362
  (9 shorter events, 0.1 us)
Async XLA Ops:
  7.2 1.6 %collective-permute-start.1 = (f32[384,128]{1,0:T(8,128)S(1)}, f32[384,128]{1,0:T(8,128)S(1)}, u32[]{:S(2)}, u32[]{:S(2)}) collective-permute-start(f32[384,128]{1,0:T(8,128)S(1)} %get-tuple-element.31), channel_id=1, source_target_pairs={{0,1},{1,0},{2,3},{3,2},{4,5},{5,4},{6,7},{7,6},{8,9},{9,8},{10,11... | collective-permute-start | bytes 589832 | tf_op jit(solution)/shard_map/ppermute | solution.py:398
  7.8 4.1 %collective-permute-start = (f32[384,128]{1,0:T(8,128)S(1)}, f32[384,128]{1,0:T(8,128)S(1)}, u32[]{:S(2)}, u32[]{:S(2)}) collective-permute-start(f32[384,128]{1,0:T(8,128)S(1)} %get-tuple-element.27), channel_id=1, source_target_pairs={{0,1},{1,0},{2,3},{3,2},{4,5},{5,4},{6,7},{7,6},{8,9},{9,8},{10,11... | collective-permute-start | bytes 589832 | tf_op jit(solution)/shard_map/ppermute | solution.py:399
  8.8 8.2 %collective-permute-start.2 = (f32[384,128]{1,0:T(8,128)S(1)}, f32[384,128]{1,0:T(8,128)S(1)}, u32[]{:S(2)}, u32[]{:S(2)}) collective-permute-start(f32[384,128]{1,0:T(8,128)S(1)} %add.3), channel_id=1, source_target_pairs={{0,2},{1,3},{2,0},{3,1},{4,6},{5,7},{6,4},{7,5},{8,10},{9,11},{10,... | collective-permute-start | bytes 589832 | tf_op jit(solution)/shard_map/ppermute | solution.py:400
  14.3 40.4 %copy-start = (s32[1,64]{1,0:T(1,128)S(1)}, s32[1,64]{1,0:T(1,128)}, u32[]{:S(2)}) copy-start(s32[1,64]{1,0:T(1,128)} %get-tuple-element.24.row_ref) | copy-start | bytes 772
  17.7 9.2 %collective-permute-start.7 = (bf16[160,128]{1,0:T(8,128)(2,1)S(1)}, bf16[160,128]{1,0:T(8,128)(2,1)S(1)}, u32[]{:S(2)}, u32[]{:S(2)}) collective-permute-start(bf16[160,128]{1,0:T(8,128)(2,1)S(1)} %get-tuple-element.37), channel_id=1, source_target_pairs={{0,28},{4,24},{8,20},{12,16},{16,12},{20,8},{24,4},{28,0},{1,29},{... | collective-permute-start | bytes 122888 | tf_op jit(solution)/shard_map/ppermute | solution.py:413
  22.5 10.4 %collective-permute-start.10 = (bf16[160,128]{1,0:T(8,128)(2,1)S(1)}, bf16[160,128]{1,0:T(8,128)(2,1)S(1)}, u32[]{:S(2)}, u32[]{:S(2)}) collective-permute-start(bf16[160,128]{1,0:T(8,128)(2,1)S(1)} %get-tuple-element.41), channel_id=1, source_target_pairs={{0,20},{4,16},{8,28},{12,24},{16,4},{20,0},{24,12},{28,8},{1,21},{... | collective-permute-start | bytes 122888 | tf_op jit(solution)/shard_map/ppermute | solution.py:413
  22.5 5.9 %collective-permute-start.3 = (bf16[160,128]{1,0:T(8,128)(2,1)S(1)}, bf16[160,128]{1,0:T(8,128)(2,1)S(1)}, u32[]{:S(2)}, u32[]{:S(2)}) collective-permute-start(bf16[160,128]{1,0:T(8,128)(2,1)S(1)} %get-tuple-element.33), channel_id=1, source_target_pairs={{0,8},{4,12},{8,0},{12,4},{16,24},{20,28},{24,16},{28,20},{1,9},{5... | collective-permute-start | bytes 122888 | tf_op jit(solution)/shard_map/ppermute | solution.py:413
  23.2 5.8 %collective-permute-start.4 = (bf16[160,128]{1,0:T(8,128)(2,1)S(1)}, bf16[160,128]{1,0:T(8,128)(2,1)S(1)}, u32[]{:S(2)}, u32[]{:S(2)}) collective-permute-start(bf16[160,128]{1,0:T(8,128)(2,1)S(1)} %get-tuple-element.34), channel_id=1, source_target_pairs={{0,16},{4,20},{8,24},{12,28},{16,0},{20,4},{24,8},{28,12},{1,17},{... | collective-permute-start | bytes 122888 | tf_op jit(solution)/shard_map/ppermute | solution.py:413
  25.4 5.9 %collective-permute-start.5 = (bf16[160,128]{1,0:T(8,128)(2,1)S(1)}, bf16[160,128]{1,0:T(8,128)(2,1)S(1)}, u32[]{:S(2)}, u32[]{:S(2)}) collective-permute-start(bf16[160,128]{1,0:T(8,128)(2,1)S(1)} %get-tuple-element.35), channel_id=1, source_target_pairs={{0,24},{4,28},{8,16},{12,20},{16,8},{20,12},{24,0},{28,4},{1,25},{... | collective-permute-start | bytes 122888 | tf_op jit(solution)/shard_map/ppermute | solution.py:413
  26.9 6.0 %collective-permute-start.9 = (bf16[160,128]{1,0:T(8,128)(2,1)S(1)}, bf16[160,128]{1,0:T(8,128)(2,1)S(1)}, u32[]{:S(2)}, u32[]{:S(2)}) collective-permute-start(bf16[160,128]{1,0:T(8,128)(2,1)S(1)} %get-tuple-element.40), channel_id=1, source_target_pairs={{0,12},{4,8},{8,4},{12,0},{16,28},{20,24},{24,20},{28,16},{1,13},{... | collective-permute-start | bytes 122888 | tf_op jit(solution)/shard_map/ppermute | solution.py:413
  28.4 4.5 %collective-permute-start.8 = (bf16[160,128]{1,0:T(8,128)(2,1)S(1)}, bf16[160,128]{1,0:T(8,128)(2,1)S(1)}, u32[]{:S(2)}, u32[]{:S(2)}) collective-permute-start(bf16[160,128]{1,0:T(8,128)(2,1)S(1)} %get-tuple-element.38), channel_id=1, source_target_pairs={{0,4},{4,0},{8,12},{12,8},{16,20},{20,16},{24,28},{28,24},{1,5},{5... | collective-permute-start | bytes 122888 | tf_op jit(solution)/shard_map/ppermute | solution.py:413
  31.4 5.5 %collective-permute-start.6 = (bf16[640,128]{1,0:T(8,128)(2,1)S(1)}, bf16[640,128]{1,0:T(8,128)(2,1)S(1)}, u32[]{:S(2)}, u32[]{:S(2)}) collective-permute-start(bf16[640,128]{1,0:T(8,128)(2,1)S(1)} %constant_dynamic-update-slice_fusion.rest_0_), channel_id=1, source_target_pairs={{0,2},{1,3},{2,0},{3,1},{4,6},{5,7},{6,4},{7,5},{8,10},{9,11},{10,... | collective-permute-start | bytes 491528 | tf_op jit(solution)/shard_map/ppermute | solution.py:415
  33.0 5.6 %collective-permute-start.11 = (bf16[640,128]{1,0:T(8,128)(2,1)S(1)}, bf16[640,128]{1,0:T(8,128)(2,1)S(1)}, u32[]{:S(2)}, u32[]{:S(2)}) collective-permute-start(bf16[640,128]{1,0:T(8,128)(2,1)S(1)} %constant_dynamic-update-slice_fusion.4.rest_1_), channel_id=1, source_target_pairs={{0,2},{1,3},{2,0},{3,1},{4,6},{5,7},{6,4},{7,5},{8,10},{9,11},{10,... | collective-permute-start | bytes 491528 | tf_op jit(solution)/shard_map/ppermute | solution.py:415
  34.1 4.5 %collective-permute-start.14 = (bf16[640,128]{1,0:T(8,128)(2,1)S(1)}, bf16[640,128]{1,0:T(8,128)(2,1)S(1)}, u32[]{:S(2)}, u32[]{:S(2)}) collective-permute-start(bf16[640,128]{1,0:T(8,128)(2,1)S(1)} %constant_dynamic-update-slice_fusion.rest_0_), channel_id=1, source_target_pairs={{0,1},{1,0},{2,3},{3,2},{4,5},{5,4},{6,7},{7,6},{8,9},{9,8},{10,11... | collective-permute-start | bytes 491528 | tf_op jit(solution)/shard_map/ppermute | solution.py:416
  34.1 4.5 %collective-permute-start.15 = (bf16[640,128]{1,0:T(8,128)(2,1)S(1)}, bf16[640,128]{1,0:T(8,128)(2,1)S(1)}, u32[]{:S(2)}, u32[]{:S(2)}) collective-permute-start(bf16[640,128]{1,0:T(8,128)(2,1)S(1)} %constant_dynamic-update-slice_fusion.4.rest_1_), channel_id=1, source_target_pairs={{0,1},{1,0},{2,3},{3,2},{4,5},{5,4},{6,7},{7,6},{8,9},{9,8},{10,11... | collective-permute-start | bytes 491528 | tf_op jit(solution)/shard_map/ppermute | solution.py:416
  36.8 2.8 %collective-permute-start.12 = (bf16[640,128]{1,0:T(8,128)(2,1)S(1)}, bf16[640,128]{1,0:T(8,128)(2,1)S(1)}, u32[]{:S(2)}, u32[]{:S(2)}) collective-permute-start(bf16[640,128]{1,0:T(8,128)(2,1)S(1)} %collective-permute-done.6.rest_0_), channel_id=1, source_target_pairs={{0,1},{1,0},{2,3},{3,2},{4,5},{5,4},{6,7},{7,6},{8,9},{9,8},{10,11... | collective-permute-start | bytes 491528 | tf_op jit(solution)/shard_map/ppermute | solution.py:418
  38.6 1.4 %collective-permute-start.13 = (bf16[640,128]{1,0:T(8,128)(2,1)S(1)}, bf16[640,128]{1,0:T(8,128)(2,1)S(1)}, u32[]{:S(2)}, u32[]{:S(2)}) collective-permute-start(bf16[640,128]{1,0:T(8,128)(2,1)S(1)} %collective-permute-done.11.rest_1_), channel_id=1, source_target_pairs={{0,1},{1,0},{2,3},{3,2},{4,5},{5,4},{6,7},{7,6},{8,9},{9,8},{10,11... | collective-permute-start | bytes 491528 | tf_op jit(solution)/shard_map/ppermute | solution.py:418

commit v6 on v5

--- a/solution.py
+++ b/solution.py
@@ -11,6 +11,8 @@
 LANES = 128
 NT = (((1,), (1,)), ((), ()))
 TN = (((0,), (0,)), ((), ()))
+
+PLANS = {8: (((0, 6, 5, 7, 3), (1, 2, 4)), {1: 5, 2: 7})}
 
 
 def project_kernel(
@@ -153,11 +155,12 @@
 
 
 def own_kernel(slot_ref, a_ref, b_ref, q_hbm, out_slot_ref, out_ref, held_ref, sems):
-    parts, _, width = held_ref.shape
+    parts = sems.shape[0]
+    rows = held_ref.shape[0] // parts
 
     def load(k):
-        columns = q_hbm.at[:, pl.ds(k * width, width)]
-        return pltpu.make_async_copy(columns, held_ref.at[k], sems.at[k])
+        here = pl.ds(k * rows, rows)
+        return pltpu.make_async_copy(q_hbm.at[here], held_ref.at[here], sems.at[k])
 
     for k in range(parts):
         load(k).start()
@@ -171,9 +174,10 @@
         load(k).wait()
 
 
-def own_sum(slots, a, b, queries, count, parts):
+def own_sum(slots, a, b, queries, count):
     smem = pl.BlockSpec(memory_space=pltpu.SMEM)
     vmem = pl.BlockSpec(memory_space=pltpu.VMEM)
+    parts = 4 if queries.shape[0] % 64 == 0 else 1
     return pl.pallas_call(
         own_kernel,
         in_specs=[smem, vmem, vmem, pl.BlockSpec(memory_space=pltpu.HBM)],
@@ -181,7 +185,7 @@
         out_shape=[
             pltpu.SMEM((count,), jnp.int32),
             pltpu.VMEM(a.shape, a.dtype),
-            pltpu.VMEM((parts, queries.shape[0], queries.shape[1] // parts), queries.dtype),
+            pltpu.VMEM(queries.shape, queries.dtype),
         ],
         scratch_shapes=[pltpu.SemaphoreType.DMA((parts,))],
         compiler_params=pltpu.CompilerParams(vmem_limit_bytes=48 << 20),
@@ -241,71 +245,55 @@
     )(slots, a, b)
 
 
-def stage_units(refs, parcels, stage, parts, slots, groups):
-    each = stage.shape[1] // (len(refs) // len(parcels) * groups * slots)
-    span = slots * parts * each
+def stage_units(refs, parcels, stage, groups):
+    span = stage.shape[0] // (len(refs) // len(parcels) * groups)
     home = lax.axis_index("dp")
     for n, ref in enumerate(refs):
-        parcel = parcels[n % len(parcels)]
-
-        @pl.loop(0, len(parcel))
-        def _(i, n=n, ref=ref, parcel=parcel):
-            d = (parcel.start + parcel.step * i) ^ home
-            got = ref[pl.ds(pl.multiple_of(i * span, span), span), :].astype(jnp.float32)
-            got = got.reshape(slots, parts, each, LANES)
-            for k in range(parts):
-                at = pl.multiple_of((n // len(parcels) * groups + d) * slots * each, each)
-                stage[k, pl.ds(at, slots * each), :] = got[:, k].reshape(slots * each, LANES)
-
-
-def staged_rows(stage, k, units, at):
+        for i, distance in enumerate(parcels[n % len(parcels)]):
+            block = n // len(parcels) * groups + (distance ^ home)
+            here = pl.ds(pl.multiple_of(block * span, span), span)
+            stage[here, :] = ref[i * span : (i + 1) * span, :].astype(jnp.float32)
+
+
+def staged_rows(stage, units, at):
     rows = units.shape[0] - at
-    each = units.shape[1] // LANES
-    for j in range(each):
-        piece = stage[k, pl.ds(j, rows, stride=each), :]
+    chunks = units.shape[1] // LANES
+    for j in range(chunks):
+        piece = stage[pl.ds(j, rows, stride=chunks), :]
         units[at:, j * LANES : (j + 1) * LANES] = piece.astype(jnp.bfloat16)
 
 
-def stage_kernel(groups, slots, parcels, *rest):
+def stage_kernel(groups, parcels, *rest):
     refs, (out_ref, stage) = rest[:-2], rest[-2:]
-    parts = out_ref.shape[0]
-    stage_units(refs, parcels, stage, parts, slots, groups)
-
-    @pl.loop(0, parts)
-    def _(k):
-        staged_rows(stage, k, out_ref.at[k], 0)
-
-
-def staged(units, parcels, groups, slots, parts):
+    stage_units(refs, parcels, stage, groups)
+    staged_rows(stage, out_ref, 0)
+
+
+def staged(units, parcels, groups, slots):
     rows = 2 * groups * slots
-    width = sum(x.size for x in units) // (rows * parts)
+    width = sum(x.size for x in units) // rows
     vmem = pl.BlockSpec(memory_space=pltpu.VMEM)
     return pl.pallas_call(
-        functools.partial(stage_kernel, groups, slots, parcels),
+        functools.partial(stage_kernel, groups, parcels),
         in_specs=[vmem] * len(units),
         out_specs=vmem,
-        out_shape=pltpu.VMEM((parts, rows, width), jnp.bfloat16),
-        scratch_shapes=[pltpu.VMEM((parts, rows * width // LANES, LANES), jnp.float32)],
+        out_shape=pltpu.VMEM((rows, width), jnp.bfloat16),
+        scratch_shapes=[pltpu.VMEM((rows * width // LANES, LANES), jnp.float32)],
         compiler_params=pltpu.CompilerParams(vmem_limit_bytes=16 << 20),
         cost_estimate=pl.CostEstimate(
-            flops=rows * parts * width, bytes_accessed=8 * rows * width, transcendentals=0
+            flops=rows * width, bytes_accessed=8 * rows * width, transcendentals=0
         ),
         name="staged",
     )(*units)
 
 
 def score_kernel(groups, slots, padded, parcels, *rest):
-    refs, (early_ref, q_ref, out_ref, stage, units, total) = rest[:-6], rest[-6:]
-    parts = q_ref.shape[0]
+    refs, (early_ref, q_ref, out_ref, stage, units) = rest[:-5], rest[-5:]
     half = groups * slots
-    stage_units(refs, parcels, stage, parts, slots, groups)
-    total[...] = jnp.zeros_like(total)
-
-    @pl.loop(0, parts)
-    def _(k):
-        units[0 : 2 * half, :] = early_ref[k]
-        staged_rows(stage, k, units, 2 * half)
-        total[...] += lax.dot_general(q_ref[k], units[...], NT, preferred_element_type=jnp.float32)
+    stage_units(refs, parcels, stage, groups)
+    units[0 : 2 * half, :] = early_ref[...]
+    staged_rows(stage, units, 2 * half)
+    total = lax.dot_general(q_ref[...], units[...], NT, preferred_element_type=jnp.float32)
 
     row = lax.broadcasted_iota(jnp.int32, (groups * padded, 4 * half), 0)
     column = lax.broadcasted_iota(jnp.int32, (1, 4 * half), 1)
@@ -318,13 +306,13 @@
             place += jnp.where(after, padded - slots, 0)
     pick = jnp.where(row == place, 1.0, 0.0).astype(jnp.bfloat16)
     out = lax.dot_general(
-        pick, total[...].astype(jnp.bfloat16), NT, preferred_element_type=jnp.float32
+        pick, total.astype(jnp.bfloat16), NT, preferred_element_type=jnp.float32
     )
     out_ref[...] = out.astype(out_ref.dtype)
 
 
 def scores_of(late, early, queries, parcels, groups, slots, padded):
-    parts, count, width = queries.shape
+    count, width = queries.shape
     half = groups * slots
     vmem = pl.BlockSpec(memory_space=pltpu.VMEM)
     return pl.pallas_call(
@@ -333,9 +321,8 @@
         out_specs=vmem,
         out_shape=pltpu.VMEM((groups * padded, count), jnp.bfloat16),
         scratch_shapes=[
-            pltpu.VMEM((parts, 2 * half * width // LANES, LANES), jnp.float32),
+            pltpu.VMEM((2 * half * width // LANES, LANES), jnp.float32),
             pltpu.VMEM((4 * half, width), jnp.bfloat16),
-            pltpu.VMEM((count, 4 * half), jnp.float32),
         ],
         compiler_params=pltpu.CompilerParams(vmem_limit_bytes=24 << 20),
         cost_estimate=pl.CostEstimate(
@@ -400,21 +387,20 @@
     across_in = lax.ppermute(over_part + far_in, "tensor", across)
 
     here_slots, here, held = own_sum(
-        my_slots, own_part, near_in, query_block, examples // ways, 1
+        my_slots, own_part, near_in, query_block, examples // ways
     )
     units = unit_grads(here_slots, here, across_in, tokens, chunks, groups, slots)
-    parcels = (range(0, groups, 2), range(1, groups, 2))
+    parcels, after = PLANS[groups]
     arrived = [units[0]] + [None] * (groups - 1)
-    farthest = groups - 1
-    for k in (farthest, *range(groups - 2, 0, -2), *range(groups - 3, 0, -2)):
+    for k in (k for parcel in parcels for k in parcel if k):
         block = units[k]
-        if k % 2 and k < groups // 2:
-            block, _ = lax.optimization_barrier((block, arrived[farthest]))
+        if k in after:
+            block, _ = lax.optimization_barrier((block, arrived[after[k]]))
         arrived[k] = lax.ppermute(block, "dp", [(i, i ^ k) for i in range(groups)])
     own = [jnp.concatenate([arrived[k] for k in parcel], axis=0) for parcel in parcels]
     over_y = [lax.ppermute(x, "tensor", across) for x in own]
     over_core = [lax.ppermute(x, "tensor", core) for x in own]
-    early = staged(own + over_core, parcels, groups, slots, held.shape[0])
+    early = staged(own + over_core, parcels, groups, slots)
     over_both = [lax.ppermute(x, "tensor", core) for x in over_y]
     both = scores_of(over_y + over_both, early, held, parcels, groups, slots, padded)
     block = both.reshape(groups, padded, both.shape[1])
@@ -480,9 +466,8 @@
 
 
 def local(activations, out_grads, proj_in, proj_out, queries, candidates):
-    groups = lax.axis_size("dp")
     one = candidates.shape[1] == 1 and lax.axis_size("tensor") == 4
-    one = one and groups >= 4 and groups & (groups - 1) == 0
+    one = one and lax.axis_size("dp") in PLANS
     return (local_one if one else local_many)(
         activations, out_grads, proj_in, proj_out, queries, candidates
     )

time: 55.8 us -> 55.2 us (0.989)
  waiting for transfers between devices: 10.4 us -> 9.37 us
    ppermute x2, waiting for transfers between devices: 3.98 us -> 2.84 us  [local_one(): over_y = [lax.ppermute(x, 'tensor', across) for x in own]]
  transfers between devices with their start and end apart: 16 -> 16, of which waited for: 6 -> 9; matrix products, arithmetic and copies ran while one was open for 0% -> 0% of each run, Pallas kernels for 6% -> 6%
where the time goes in v6:
time: 55.2 us; the launch traced here: 55 us
  starting transfers between devices  18.3 us (33%)
  Pallas kernels  14.4 us (26%)
  blocking collectives  12.8 us (23%)
  waiting for transfers between devices  9.37 us (17%)
    all_to_all x1, blocking collectives, local_one(): lax.all_to_all(block, 'dp', split_axis=0, concat_axis=0, tiled=True)  12.8 us
    ppermute x7, starting transfers between devices, local_one(): arrived[k] = lax.ppermute(block, 'dp', [(i, i ^ k) for i in range(groups)])  11.1 us
    pallas_call x1, Pallas kernels, project(): pl.pallas_call(functools.partial(project_kernel, groups, ways, tokens, sl...  7.23 us
    ppermute x2, starting transfers between devices, local_one(): over_y = [lax.ppermute(x, 'tensor', across) for x in own]  3.17 us
    ppermute x1, starting transfers between devices, local_one(): across_in = lax.ppermute(over_part + far_in, 'tensor', across)  2.95 us
    ppermute x2, waiting for transfers between devices, local_one(): over_y = [lax.ppermute(x, 'tensor', across) for x in own]  2.84 us
    ppermute x1, waiting for transfers between devices, local_one(): across_in = lax.ppermute(over_part + far_in, 'tensor', across)  2.65 us
    pallas_call x1, Pallas kernels, own_sum(): pl.pallas_call(own_kernel, in_specs=[smem, vmem, vmem, pl.BlockSpec(memor...  2.54 us
  transfers between devices with their start and end apart: 16, of which 9 were waited for; matrix products, arithmetic and copies ran while one was open for 0% of the time, Pallas kernels for 6%

profile of v6, /device:TPU:0, one launch (start us, length us, event | category | flops | bytes accessed | tf_op | source)
XLA Modules:
  0.0 55.0 jit_solution(6387334767009413332)
XLA Ops:
  0.0 7.2 %project.1 = (f32[384,128]{1,0:T(8,128)S(1)}, f32[384,128]{1,0:T(8,128)S(1)}, f32[384,128]{1,0:T(8,128)S(1)}, f32[384,128]{1,0:T(8,128)S(1)}, s32[64]{0:T(128)S(4)}, /*index=5*/s32[1,64]{1,0:T(1,128)}) custom-call(s32[1,64]{1,0:T(1,128)} %bitcast.16, bf16[1536,3584]{1,0:T(8,128)(2,1)} %bitcast.11, bf16[1536,1024]{1,0:T(8,128)(2,1)} %bitcast.13, ...), custom_call_target="tpu_custom_call" | custom-call | flops 905969664 | bytes 14155776 | tf_op jit(solution)/shard_map/project/pallas_call | solution.py:124
  7.2 0.5 collective-permute-start.1
  7.8 0.1 collective-permute-start
  7.8 1.0 %collective-permute-done.1 = f32[384,128]{1,0:T(8,128)S(1)} collective-permute-done((f32[384,128]{1,0:T(8,128)S(1)}, f32[384,128]{1,0:T(8,128)S(1)}, u32[]{:S(2)}, u32[]{:S(2)}) %collective-permute-start.1) | collective-permute-done | bytes 196640 | tf_op jit(solution)/shard_map/ppermute | solution.py:385
  8.8 3.0 %collective-permute-start.2 = (f32[384,128]{1,0:T(8,128)S(1)}, f32[384,128]{1,0:T(8,128)S(1)}, u32[]{:S(2)}, u32[]{:S(2)}) collective-permute-start(f32[384,128]{1,0:T(8,128)S(1)} %add.3), channel_id=1, source_target_pairs={{0,2},{1,3},{2,0},{3,1},{4,6},{5,7},{6,4},{7,5},{8,10},{9,11},{10,... | collective-permute-start | bytes 589832 | tf_op jit(solution)/shard_map/ppermute | solution.py:387
  11.8 0.0 collective-permute-done.b_ref
  11.8 2.5 %own_sum.1 = (s32[16]{0:T(128)S(4)}, f32[384,128]{1,0:T(8,128)S(1)}, bf16[640,4096]{1,0:T(8,128)(2,1)S(1)}) custom-call(s32[64]{0:T(128)S(4)} %get-tuple-element.25.slot_ref, f32[384,128]{1,0:T(8,128)S(1)} %get-tuple-element.26.a_ref, f32[384,128]{1,0:T(8,128)S(1)} %collective-permute-done.b_ref, bf16[640,4096]{1,0:T(8,128)(2,1)} %bitcast.12), custom_call_target="tpu_custom_call" | custom-call | flops 49152 | bytes 5242880 | tf_op jit(solution)/shard_map/own_sum/pallas_call | solution.py:181
  14.3 0.0 copy-start
  14.4 2.6 %collective-permute-done.2.b_ref = f32[384,128]{1,0:T(8,128)S(1)} collective-permute-done((f32[384,128]{1,0:T(8,128)S(1)}, f32[384,128]{1,0:T(8,128)S(1)}, u32[]{:S(2)}, u32[]{:S(2)}) %collective-permute-start.2) | collective-permute-done | bytes 196640 | tf_op jit(solution)/shard_map/ppermute | solution.py:387
  17.0 0.7 %unit_grads.1 = (bf16[160,128]{1,0:T(8,128)(2,1)S(1)}, bf16[160,128]{1,0:T(8,128)(2,1)S(1)}, bf16[160,128]{1,0:T(8,128)(2,1)S(1)}, bf16[160,128]{1,0:T(8,128)(2,...) custom-call(s32[16]{0:T(128)S(4)} %get-tuple-element.28.row_ref, ...), custom_call_target="tpu_custom_call" | custom-call | flops 20000000 | bytes 1000000 | tf_op jit(solution)/shard_map/unit_grads/pallas_call | solution.py:233
  17.7 3.9 %collective-permute-start.3 = (bf16[160,128]{1,0:T(8,128)(2,1)S(1)}, bf16[160,128]{1,0:T(8,128)(2,1)S(1)}, u32[]{:S(2)}, u32[]{:S(2)}) collective-permute-start(bf16[160,128]{1,0:T(8,128)(2,1)S(1)} %get-tuple-element.33), channel_id=1, source_target_pairs={{0,24},{4,28},{8,16},{12,20},{16,8},{20,12},{24,0},{28,4},{1,25},{... | collective-permute-start | bytes 122888 | tf_op jit(solution)/shard_map/ppermute | solution.py:399
  21.6 0.4 collective-permute-start.4
  22.0 2.4 %collective-permute-start.5 = (bf16[160,128]{1,0:T(8,128)(2,1)S(1)}, bf16[160,128]{1,0:T(8,128)(2,1)S(1)}, u32[]{:S(2)}, u32[]{:S(2)}) collective-permute-start(bf16[160,128]{1,0:T(8,128)(2,1)S(1)} %get-tuple-element.35), channel_id=1, source_target_pairs={{0,28},{4,24},{8,20},{12,16},{16,12},{20,8},{24,4},{28,0},{1,29},{... | collective-permute-start | bytes 122888 | tf_op jit(solution)/shard_map/ppermute | solution.py:399
  24.4 2.5 %collective-permute-start.6 = (bf16[160,128]{1,0:T(8,128)(2,1)S(1)}, bf16[160,128]{1,0:T(8,128)(2,1)S(1)}, u32[]{:S(2)}, u32[]{:S(2)}) collective-permute-start(bf16[160,128]{1,0:T(8,128)(2,1)S(1)} %get-tuple-element.36), channel_id=1, source_target_pairs={{0,12},{4,8},{8,4},{12,0},{16,28},{20,24},{24,20},{28,16},{1,13},{... | collective-permute-start | bytes 122888 | tf_op jit(solution)/shard_map/ppermute | solution.py:399
  26.9 0.3 collective-permute-start.10
  27.3 0.2 collective-permute-done.4
  27.4 1.5 %collective-permute-start.8 = (bf16[160,128]{1,0:T(8,128)(2,1)S(1)}, bf16[160,128]{1,0:T(8,128)(2,1)S(1)}, u32[]{:S(2)}, u32[]{:S(2)}) collective-permute-start(bf16[160,128]{1,0:T(8,128)(2,1)S(1)} %get-tuple-element.38), channel_id=1, source_target_pairs={{0,4},{4,0},{8,12},{12,8},{16,20},{20,16},{24,28},{28,24},{1,5},{5... | collective-permute-start | bytes 122888 | tf_op jit(solution)/shard_map/ppermute | solution.py:399
  29.0 0.0 collective-permute-done.5
  29.0 0.0 collective-permute-start.9
  29.0 0.0 collective-permute-done.3
  29.0 0.7 %collective-permute-done.6 = bf16[160,128]{1,0:T(8,128)(2,1)S(1)} collective-permute-done((bf16[160,128]{1,0:T(8,128)(2,1)S(1)}, bf16[160,128]{1,0:T(8,128)(2,1)S(1)}, u32[]{:S(2)}, u32[]{:S(2)}) %collective-permute-start.6) | collective-permute-done | bytes 40992 | tf_op jit(solution)/shard_map/ppermute | solution.py:399
  29.8 1.6 %collective-permute-start.7 = (bf16[800,128]{1,0:T(8,128)(2,1)S(1)}, bf16[800,128]{1,0:T(8,128)(2,1)S(1)}, u32[]{:S(2)}, u32[]{:S(2)}) collective-permute-start(bf16[800,128]{1,0:T(8,128)(2,1)S(1)} %constant_dynamic-update-slice_fusion.rest_0_), channel_id=1, source_target_pairs={{0,2},{1,3},{2,0},{3,1},{4,6},{5,7},{6,4},{7,5},{8,10},{9,11},{10,... | collective-permute-start | bytes 614408 | tf_op jit(solution)/shard_map/ppermute | solution.py:401
  31.3 0.1 collective-permute-done.8
  31.4 1.5 %collective-permute-done.9 = bf16[160,128]{1,0:T(8,128)(2,1)S(1)} collective-permute-done((bf16[160,128]{1,0:T(8,128)(2,1)S(1)}, bf16[160,128]{1,0:T(8,128)(2,1)S(1)}, u32[]{:S(2)}, u32[]{:S(2)}) %collective-permute-start.9) | collective-permute-done | bytes 40992 | tf_op jit(solution)/shard_map/ppermute | solution.py:399
  33.0 0.0 collective-permute-done.10
  33.0 1.6 %collective-permute-start.11 = (bf16[480,128]{1,0:T(8,128)(2,1)S(1)}, bf16[480,128]{1,0:T(8,128)(2,1)S(1)}, u32[]{:S(2)}, u32[]{:S(2)}) collective-permute-start(bf16[480,128]{1,0:T(8,128)(2,1)S(1)} %constant_dynamic-update-slice_fusion.5.rest_1_), channel_id=1, source_target_pairs={{0,2},{1,3},{2,0},{3,1},{4,6},{5,7},{6,4},{7,5},{8,10},{9,11},{10,... | collective-permute-start | bytes 368648 | tf_op jit(solution)/shard_map/ppermute | solution.py:401
  34.6 0.0 collective-permute-start.14
  34.6 1.5 %collective-permute-done.7.rest_0_ = bf16[800,128]{1,0:T(8,128)(2,1)S(1)} collective-permute-done((bf16[800,128]{1,0:T(8,128)(2,1)S(1)}, bf16[800,128]{1,0:T(8,128)(2,1)S(1)}, u32[]{:S(2)}, u32[]{:S(2)}) %collective-permute-start.7) | collective-permute-done | bytes 204832 | tf_op jit(solution)/shard_map/ppermute | solution.py:401
  36.1 0.0 collective-permute-start.12
  36.1 0.5 collective-permute-start.15
  36.6 1.3 %collective-permute-done.11.rest_1_ = bf16[480,128]{1,0:T(8,128)(2,1)S(1)} collective-permute-done((bf16[480,128]{1,0:T(8,128)(2,1)S(1)}, bf16[480,128]{1,0:T(8,128)(2,1)S(1)}, u32[]{:S(2)}, u32[]{:S(2)}) %collective-permute-start.11) | collective-permute-done | bytes 122912 | tf_op jit(solution)/shard_map/ppermute | solution.py:401
  37.9 0.0 collective-permute-start.13
  37.9 0.0 collective-permute-done.15.rest_3_
  37.9 0.0 collective-permute-done.14.rest_2_
  37.9 0.9 %staged.1.rest_4_ = bf16[80,4096]{1,0:T(8,128)(2,1)S(1)} custom-call(bf16[800,128]{1,0:T(8,128)(2,1)S(1)} %constant_dynamic-update-slice_fusion.rest_0_, bf16[480,128]{1,0:T(8,128)(2,1)S(1)} %constant_dynamic-update-slice_fusion.5.rest_1_, bf16[800,128]{1,0:T(8,128)(2,1)S(1)} %collective-permute-done.14.rest_2_, ...), custom_call_target="tpu_custom_call" | custom-call | flops 327680 | bytes 2621440 | tf_op jit(solution)/shard_map/staged/pallas_call | solution.py:276
  38.9 0.4 collective-permute-done.13.rest_3_
  39.3 0.0 collective-permute-done.12.rest_2_
  39.3 2.1 %scores.1 = bf16[192,640]{1,0:T(8,128)(2,1)S(1)} custom-call(bf16[800,128]{1,0:T(8,128)(2,1)S(1)} %collective-permute-done.7.rest_0_, bf16[480,128]{1,0:T(8,128)(2,1)S(1)} %collective-permute-done.11.rest_1_, bf16[800,128]{1,0:T(8,128)(2,1)S(1)} %collective-permute-done.12.rest_2_, bf16[480,128]{1,0:T(8,128)(2,1)S(1)} %collective-permute-done.13.rest_3_, ...), custom_call_target="tpu_custom_call" | custom-call | flops 838860800 | bytes 5242880 | tf_op jit(solution)/shard_map/scores/pallas_call | solution.py:318
  41.4 12.8 %all_to_all.5 = bf16[8,24,640]{2,1,0:T(8,128)(2,1)S(1)} all-to-all(bf16[8,24,640]{2,1,0:T(8,128)(2,1)S(1)} %bitcast.9), channel_id=1, replica_groups=mesh['dp'=8,'tensor'=4] {'dp'}, dimensions={0} | all-to-all | bytes 491520 | tf_op jit(solution)/shard_map/all_to_all | solution.py:407
  54.1 0.0 copy-done
  54.2 0.9 %pick_rows.1 = f32[320,128]{1,0:T(8,128)} custom-call(s32[1,64]{1,0:T(1,128)S(1)} %copy-done, bf16[192,640]{1,0:T(8,128)(2,1)S(1)} %bitcast.10), custom_call_target="tpu_custom_call" | custom-call | flops 16000000 | bytes 400000 | tf_op jit(solution)/shard_map/pick_rows/pallas_call | solution.py:349
  (9 shorter events, 0.1 us)
Async XLA Ops:
  7.2 1.6 %collective-permute-start.1 = (f32[384,128]{1,0:T(8,128)S(1)}, f32[384,128]{1,0:T(8,128)S(1)}, u32[]{:S(2)}, u32[]{:S(2)}) collective-permute-start(f32[384,128]{1,0:T(8,128)S(1)} %get-tuple-element.31), channel_id=1, source_target_pairs={{0,1},{1,0},{2,3},{3,2},{4,5},{5,4},{6,7},{7,6},{8,9},{9,8},{10,11... | collective-permute-start | bytes 589832 | tf_op jit(solution)/shard_map/ppermute | solution.py:385
  7.8 4.1 %collective-permute-start = (f32[384,128]{1,0:T(8,128)S(1)}, f32[384,128]{1,0:T(8,128)S(1)}, u32[]{:S(2)}, u32[]{:S(2)}) collective-permute-start(f32[384,128]{1,0:T(8,128)S(1)} %get-tuple-element.27), channel_id=1, source_target_pairs={{0,1},{1,0},{2,3},{3,2},{4,5},{5,4},{6,7},{7,6},{8,9},{9,8},{10,11... | collective-permute-start | bytes 589832 | tf_op jit(solution)/shard_map/ppermute | solution.py:386
  8.8 8.2 %collective-permute-start.2 = (f32[384,128]{1,0:T(8,128)S(1)}, f32[384,128]{1,0:T(8,128)S(1)}, u32[]{:S(2)}, u32[]{:S(2)}) collective-permute-start(f32[384,128]{1,0:T(8,128)S(1)} %add.3), channel_id=1, source_target_pairs={{0,2},{1,3},{2,0},{3,1},{4,6},{5,7},{6,4},{7,5},{8,10},{9,11},{10,... | collective-permute-start | bytes 589832 | tf_op jit(solution)/shard_map/ppermute | solution.py:387
  14.3 39.8 %copy-start = (s32[1,64]{1,0:T(1,128)S(1)}, s32[1,64]{1,0:T(1,128)}, u32[]{:S(2)}) copy-start(s32[1,64]{1,0:T(1,128)} %get-tuple-element.24.row_ref) | copy-start | bytes 772
  17.7 11.2 %collective-permute-start.3 = (bf16[160,128]{1,0:T(8,128)(2,1)S(1)}, bf16[160,128]{1,0:T(8,128)(2,1)S(1)}, u32[]{:S(2)}, u32[]{:S(2)}) collective-permute-start(bf16[160,128]{1,0:T(8,128)(2,1)S(1)} %get-tuple-element.33), channel_id=1, source_target_pairs={{0,24},{4,28},{8,16},{12,20},{16,8},{20,12},{24,0},{28,4},{1,25},{... | collective-permute-start | bytes 122888 | tf_op jit(solution)/shard_map/ppermute | solution.py:399
  21.6 5.8 %collective-permute-start.4 = (bf16[160,128]{1,0:T(8,128)(2,1)S(1)}, bf16[160,128]{1,0:T(8,128)(2,1)S(1)}, u32[]{:S(2)}, u32[]{:S(2)}) collective-permute-start(bf16[160,128]{1,0:T(8,128)(2,1)S(1)} %get-tuple-element.34), channel_id=1, source_target_pairs={{0,20},{4,16},{8,28},{12,24},{16,4},{20,0},{24,12},{28,8},{1,21},{... | collective-permute-start | bytes 122888 | tf_op jit(solution)/shard_map/ppermute | solution.py:399
  22.0 7.0 %collective-permute-start.5 = (bf16[160,128]{1,0:T(8,128)(2,1)S(1)}, bf16[160,128]{1,0:T(8,128)(2,1)S(1)}, u32[]{:S(2)}, u32[]{:S(2)}) collective-permute-start(bf16[160,128]{1,0:T(8,128)(2,1)S(1)} %get-tuple-element.35), channel_id=1, source_target_pairs={{0,28},{4,24},{8,20},{12,16},{16,12},{20,8},{24,4},{28,0},{1,29},{... | collective-permute-start | bytes 122888 | tf_op jit(solution)/shard_map/ppermute | solution.py:399
  24.4 5.3 %collective-permute-start.6 = (bf16[160,128]{1,0:T(8,128)(2,1)S(1)}, bf16[160,128]{1,0:T(8,128)(2,1)S(1)}, u32[]{:S(2)}, u32[]{:S(2)}) collective-permute-start(bf16[160,128]{1,0:T(8,128)(2,1)S(1)} %get-tuple-element.36), channel_id=1, source_target_pairs={{0,12},{4,8},{8,4},{12,0},{16,28},{20,24},{24,20},{28,16},{1,13},{... | collective-permute-start | bytes 122888 | tf_op jit(solution)/shard_map/ppermute | solution.py:399
  26.9 6.0 %collective-permute-start.10 = (bf16[160,128]{1,0:T(8,128)(2,1)S(1)}, bf16[160,128]{1,0:T(8,128)(2,1)S(1)}, u32[]{:S(2)}, u32[]{:S(2)}) collective-permute-start(bf16[160,128]{1,0:T(8,128)(2,1)S(1)} %get-tuple-element.41), channel_id=1, source_target_pairs={{0,16},{4,20},{8,24},{12,28},{16,0},{20,4},{24,8},{28,12},{1,17},{... | collective-permute-start | bytes 122888 | tf_op jit(solution)/shard_map/ppermute | solution.py:399
  27.4 4.0 %collective-permute-start.8 = (bf16[160,128]{1,0:T(8,128)(2,1)S(1)}, bf16[160,128]{1,0:T(8,128)(2,1)S(1)}, u32[]{:S(2)}, u32[]{:S(2)}) collective-permute-start(bf16[160,128]{1,0:T(8,128)(2,1)S(1)} %get-tuple-element.38), channel_id=1, source_target_pairs={{0,4},{4,0},{8,12},{12,8},{16,20},{20,16},{24,28},{28,24},{1,5},{5... | collective-permute-start | bytes 122888 | tf_op jit(solution)/shard_map/ppermute | solution.py:399
  29.0 4.0 %collective-permute-start.9 = (bf16[160,128]{1,0:T(8,128)(2,1)S(1)}, bf16[160,128]{1,0:T(8,128)(2,1)S(1)}, u32[]{:S(2)}, u32[]{:S(2)}) collective-permute-start(bf16[160,128]{1,0:T(8,128)(2,1)S(1)} %get-tuple-element.40), channel_id=1, source_target_pairs={{0,8},{4,12},{8,0},{12,4},{16,24},{20,28},{24,16},{28,20},{1,9},{5... | collective-permute-start | bytes 122888 | tf_op jit(solution)/shard_map/ppermute | solution.py:399
  29.8 6.4 %collective-permute-start.7 = (bf16[800,128]{1,0:T(8,128)(2,1)S(1)}, bf16[800,128]{1,0:T(8,128)(2,1)S(1)}, u32[]{:S(2)}, u32[]{:S(2)}) collective-permute-start(bf16[800,128]{1,0:T(8,128)(2,1)S(1)} %constant_dynamic-update-slice_fusion.rest_0_), channel_id=1, source_target_pairs={{0,2},{1,3},{2,0},{3,1},{4,6},{5,7},{6,4},{7,5},{8,10},{9,11},{10,... | collective-permute-start | bytes 614408 | tf_op jit(solution)/shard_map/ppermute | solution.py:401
  33.0 4.9 %collective-permute-start.11 = (bf16[480,128]{1,0:T(8,128)(2,1)S(1)}, bf16[480,128]{1,0:T(8,128)(2,1)S(1)}, u32[]{:S(2)}, u32[]{:S(2)}) collective-permute-start(bf16[480,128]{1,0:T(8,128)(2,1)S(1)} %constant_dynamic-update-slice_fusion.5.rest_1_), channel_id=1, source_target_pairs={{0,2},{1,3},{2,0},{3,1},{4,6},{5,7},{6,4},{7,5},{8,10},{9,11},{10,... | collective-permute-start | bytes 368648 | tf_op jit(solution)/shard_map/ppermute | solution.py:401
  34.6 3.4 %collective-permute-start.14 = (bf16[800,128]{1,0:T(8,128)(2,1)S(1)}, bf16[800,128]{1,0:T(8,128)(2,1)S(1)}, u32[]{:S(2)}, u32[]{:S(2)}) collective-permute-start(bf16[800,128]{1,0:T(8,128)(2,1)S(1)} %constant_dynamic-update-slice_fusion.rest_0_), channel_id=1, source_target_pairs={{0,1},{1,0},{2,3},{3,2},{4,5},{5,4},{6,7},{7,6},{8,9},{9,8},{10,11... | collective-permute-start | bytes 614408 | tf_op jit(solution)/shard_map/ppermute | solution.py:402
  36.1 3.1 %collective-permute-start.12 = (bf16[800,128]{1,0:T(8,128)(2,1)S(1)}, bf16[800,128]{1,0:T(8,128)(2,1)S(1)}, u32[]{:S(2)}, u32[]{:S(2)}) collective-permute-start(bf16[800,128]{1,0:T(8,128)(2,1)S(1)} %collective-permute-done.7.rest_0_), channel_id=1, source_target_pairs={{0,1},{1,0},{2,3},{3,2},{4,5},{5,4},{6,7},{7,6},{8,9},{9,8},{10,11... | collective-permute-start | bytes 614408 | tf_op jit(solution)/shard_map/ppermute | solution.py:404
  36.1 1.8 %collective-permute-start.15 = (bf16[480,128]{1,0:T(8,128)(2,1)S(1)}, bf16[480,128]{1,0:T(8,128)(2,1)S(1)}, u32[]{:S(2)}, u32[]{:S(2)}) collective-permute-start(bf16[480,128]{1,0:T(8,128)(2,1)S(1)} %constant_dynamic-update-slice_fusion.5.rest_1_), channel_id=1, source_target_pairs={{0,1},{1,0},{2,3},{3,2},{4,5},{5,4},{6,7},{7,6},{8,9},{9,8},{10,11... | collective-permute-start | bytes 368648 | tf_op jit(solution)/shard_map/ppermute | solution.py:402
  37.9 1.3 %collective-permute-start.13 = (bf16[480,128]{1,0:T(8,128)(2,1)S(1)}, bf16[480,128]{1,0:T(8,128)(2,1)S(1)}, u32[]{:S(2)}, u32[]{:S(2)}) collective-permute-start(bf16[480,128]{1,0:T(8,128)(2,1)S(1)} %collective-permute-done.11.rest_1_), channel_id=1, source_target_pairs={{0,1},{1,0},{2,3},{3,2},{4,5},{5,4},{6,7},{7,6},{8,9},{9,8},{10,11... | collective-permute-start | bytes 368648 | tf_op jit(solution)/shard_map/ppermute | solution.py:404

commit v7 on v6

--- a/solution.py
+++ b/solution.py
@@ -19,12 +19,14 @@
     groups, ways, tokens, slots, padded, blocks,
     cand_hbm, act_hbm, grad_hbm, win_hbm, wout_hbm,
     own_ref, over_ref, near_ref, far_ref, slot_ref, pick_ref,
-    act, grad, win, wout, raw, dealt, cand, rank, start, act_sems, grad_sems, sems,
+    x, w, raw, dealt, cand, rank, start, act_sems, grad_sems, sems,
 ):
-    proj_rank = win.shape[0]
+    proj_rank = win_hbm.shape[0]
+    features = grad_hbm.shape[1]
+    total = x.shape[1]
     examples = cand.shape[1]
     share = examples // ways
-    step = act.shape[0] // act_sems.shape[0]
+    step = x.shape[0] // act_sems.shape[0]
     me = lax.axis_index("tensor")
     home = lax.axis_index("dp")
 
@@ -32,14 +34,17 @@
         return pl.ds(pl.multiple_of(i * step, step), step)
 
     def act_copy(i):
-        return pltpu.make_async_copy(act_hbm.at[piece(i)], act.at[piece(i)], act_sems.at[i])
+        there = x.at[piece(i), pl.ds(features, total - features)]
+        return pltpu.make_async_copy(act_hbm.at[piece(i)], there, act_sems.at[i])
 
     def grad_copy(i):
-        return pltpu.make_async_copy(grad_hbm.at[piece(i)], grad.at[piece(i)], grad_sems.at[i])
+        there = x.at[piece(i), pl.ds(0, features)]
+        return pltpu.make_async_copy(grad_hbm.at[piece(i)], there, grad_sems.at[i])
 
     cand_copy = pltpu.make_async_copy(cand_hbm, cand, sems.at[0])
     raw_copy = pltpu.make_async_copy(wout_hbm, raw, sems.at[1])
-    win_copy = pltpu.make_async_copy(win_hbm, win, sems.at[2])
+    there = w.at[pl.ds(proj_rank, proj_rank), pl.ds(features, total - features)]
+    win_copy = pltpu.make_async_copy(win_hbm, there, sems.at[2])
     cand_copy.start()
     raw_copy.start()
     win_copy.start()
@@ -73,7 +78,11 @@
     c = lax.broadcasted_iota(jnp.int32, (proj_rank, proj_rank), 1)
     pick = (c == jnp.where(r < half, 2 * r, 2 * (r - half) + 1)).astype(jnp.bfloat16)
     raw_copy.wait()
-    wout[...] = jnp.dot(pick, raw[...], preferred_element_type=jnp.float32).astype(jnp.bfloat16)
+    w[0:proj_rank, 0:features] = jnp.dot(
+        pick, raw[...], preferred_element_type=jnp.float32
+    ).astype(jnp.bfloat16)
+    w[proj_rank:, 0:features] = jnp.zeros((proj_rank, features), w.dtype)
+    w[0:proj_rank, features:] = jnp.zeros((proj_rank, total - features), w.dtype)
     win_copy.wait()
 
     done = 0
@@ -86,9 +95,7 @@
                 grad_copy(done // step + i * (rows // step) + j).wait()
             at = pl.multiple_of(done + i * rows, step)
             here = pl.ds(at, rows)
-            left = lax.dot_general(grad[here, :], wout[...], NT, preferred_element_type=jnp.float32)
-            right = lax.dot_general(act[here, :], win[...], NT, preferred_element_type=jnp.float32)
-            both = jnp.concatenate([left, right], axis=1)
+            both = lax.dot_general(x[here, :], w[...], NT, preferred_element_type=jnp.float32)
             first = done // tokens + i * (rows // tokens)
             for k in range(rows // tokens):
                 e = first + k
@@ -131,10 +138,8 @@
             jax.ShapeDtypeStruct((1, examples), jnp.int32),
         ],
         scratch_shapes=[
-            pltpu.VMEM(act.shape, jnp.bfloat16),
-            pltpu.VMEM(grad.shape, jnp.bfloat16),
-            pltpu.VMEM(win.shape, jnp.bfloat16),
-            pltpu.VMEM(wout.shape, jnp.bfloat16),
+            pltpu.VMEM((rows, act.shape[1] + grad.shape[1]), jnp.bfloat16),
+            pltpu.VMEM((2 * win.shape[0], act.shape[1] + grad.shape[1]), jnp.bfloat16),
             pltpu.VMEM(wout.shape, jnp.bfloat16),
             pltpu.VMEM((rows, LANES), jnp.float32),
             pltpu.SMEM((1, examples), jnp.int32),

time: 55.2 us -> 55 us (level)
  no operation moved by 1% of the time
where the time goes in v7:
time: 55 us; the launch traced here: 54.9 us
  starting transfers between devices  18.3 us (33%)
  Pallas kernels  14.2 us (26%)
  blocking collectives  12.8 us (23%)
  waiting for transfers between devices  9.39 us (17%)
    all_to_all x1, blocking collectives, local_one(): lax.all_to_all(block, 'dp', split_axis=0, concat_axis=0, tiled=True)  12.8 us
    ppermute x7, starting transfers between devices, local_one(): arrived[k] = lax.ppermute(block, 'dp', [(i, i ^ k) for i in range(groups)])  11.1 us
    pallas_call x1, Pallas kernels, project(): pl.pallas_call(functools.partial(project_kernel, groups, ways, tokens, sl...  7.05 us
    ppermute x2, starting transfers between devices, local_one(): over_y = [lax.ppermute(x, 'tensor', across) for x in own]  3.16 us
    ppermute x1, starting transfers between devices, local_one(): across_in = lax.ppermute(over_part + far_in, 'tensor', across)  2.95 us
    ppermute x2, waiting for transfers between devices, local_one(): over_y = [lax.ppermute(x, 'tensor', across) for x in own]  2.85 us
    ppermute x1, waiting for transfers between devices, local_one(): across_in = lax.ppermute(over_part + far_in, 'tensor', across)  2.65 us
    pallas_call x1, Pallas kernels, own_sum(): pl.pallas_call(own_kernel, in_specs=[smem, vmem, vmem, pl.BlockSpec(memor...  2.54 us
  transfers between devices with their start and end apart: 16, of which 9 were waited for; matrix products, arithmetic and copies ran while one was open for 0% of the time, Pallas kernels for 6%

profile of v7, /device:TPU:0, one launch (start us, length us, event | category | flops | bytes accessed | tf_op | source)
XLA Modules:
  0.0 54.9 jit_solution(16231953635932633223)
XLA Ops:
  0.0 7.1 %project.1 = (f32[384,128]{1,0:T(8,128)S(1)}, f32[384,128]{1,0:T(8,128)S(1)}, f32[384,128]{1,0:T(8,128)S(1)}, f32[384,128]{1,0:T(8,128)S(1)}, s32[64]{0:T(128)S(4)}, /*index=5*/s32[1,64]{1,0:T(1,128)}) custom-call(s32[1,64]{1,0:T(1,128)} %bitcast.16, bf16[1536,3584]{1,0:T(8,128)(2,1)} %bitcast.11, bf16[1536,1024]{1,0:T(8,128)(2,1)} %bitcast.13, ...), custom_call_target="tpu_custom_call" | custom-call | flops 905969664 | bytes 14155776 | tf_op jit(solution)/shard_map/project/pallas_call | solution.py:131
  7.1 0.5 collective-permute-start.1
  7.6 0.1 collective-permute-start
  7.7 1.0 %collective-permute-done.1 = f32[384,128]{1,0:T(8,128)S(1)} collective-permute-done((f32[384,128]{1,0:T(8,128)S(1)}, f32[384,128]{1,0:T(8,128)S(1)}, u32[]{:S(2)}, u32[]{:S(2)}) %collective-permute-start.1) | collective-permute-done | bytes 196640 | tf_op jit(solution)/shard_map/ppermute | solution.py:390
  8.7 3.0 %collective-permute-start.2 = (f32[384,128]{1,0:T(8,128)S(1)}, f32[384,128]{1,0:T(8,128)S(1)}, u32[]{:S(2)}, u32[]{:S(2)}) collective-permute-start(f32[384,128]{1,0:T(8,128)S(1)} %add.3), channel_id=1, source_target_pairs={{0,2},{1,3},{2,0},{3,1},{4,6},{5,7},{6,4},{7,5},{8,10},{9,11},{10,... | collective-permute-start | bytes 589832 | tf_op jit(solution)/shard_map/ppermute | solution.py:392
  11.6 0.0 collective-permute-done.b_ref
  11.6 2.5 %own_sum.1 = (s32[16]{0:T(128)S(4)}, f32[384,128]{1,0:T(8,128)S(1)}, bf16[640,4096]{1,0:T(8,128)(2,1)S(1)}) custom-call(s32[64]{0:T(128)S(4)} %get-tuple-element.25.slot_ref, f32[384,128]{1,0:T(8,128)S(1)} %get-tuple-element.26.a_ref, f32[384,128]{1,0:T(8,128)S(1)} %collective-permute-done.b_ref, bf16[640,4096]{1,0:T(8,128)(2,1)} %bitcast.12), custom_call_target="tpu_custom_call" | custom-call | flops 49152 | bytes 5242880 | tf_op jit(solution)/shard_map/own_sum/pallas_call | solution.py:186
  14.2 0.0 copy-start
  14.2 2.6 %collective-permute-done.2.b_ref = f32[384,128]{1,0:T(8,128)S(1)} collective-permute-done((f32[384,128]{1,0:T(8,128)S(1)}, f32[384,128]{1,0:T(8,128)S(1)}, u32[]{:S(2)}, u32[]{:S(2)}) %collective-permute-start.2) | collective-permute-done | bytes 196640 | tf_op jit(solution)/shard_map/ppermute | solution.py:392
  16.8 0.7 %unit_grads.1 = (bf16[160,128]{1,0:T(8,128)(2,1)S(1)}, bf16[160,128]{1,0:T(8,128)(2,1)S(1)}, bf16[160,128]{1,0:T(8,128)(2,1)S(1)}, bf16[160,128]{1,0:T(8,128)(2,...) custom-call(s32[16]{0:T(128)S(4)} %get-tuple-element.28.row_ref, ...), custom_call_target="tpu_custom_call" | custom-call | flops 20000000 | bytes 1000000 | tf_op jit(solution)/shard_map/unit_grads/pallas_call | solution.py:238
  17.5 3.9 %collective-permute-start.3 = (bf16[160,128]{1,0:T(8,128)(2,1)S(1)}, bf16[160,128]{1,0:T(8,128)(2,1)S(1)}, u32[]{:S(2)}, u32[]{:S(2)}) collective-permute-start(bf16[160,128]{1,0:T(8,128)(2,1)S(1)} %get-tuple-element.33), channel_id=1, source_target_pairs={{0,24},{4,28},{8,16},{12,20},{16,8},{20,12},{24,0},{28,4},{1,25},{... | collective-permute-start | bytes 122888 | tf_op jit(solution)/shard_map/ppermute | solution.py:404
  21.4 0.3 collective-permute-start.4
  21.8 2.5 %collective-permute-start.5 = (bf16[160,128]{1,0:T(8,128)(2,1)S(1)}, bf16[160,128]{1,0:T(8,128)(2,1)S(1)}, u32[]{:S(2)}, u32[]{:S(2)}) collective-permute-start(bf16[160,128]{1,0:T(8,128)(2,1)S(1)} %get-tuple-element.35), channel_id=1, source_target_pairs={{0,28},{4,24},{8,20},{12,16},{16,12},{20,8},{24,4},{28,0},{1,29},{... | collective-permute-start | bytes 122888 | tf_op jit(solution)/shard_map/ppermute | solution.py:404
  24.3 2.5 %collective-permute-start.6 = (bf16[160,128]{1,0:T(8,128)(2,1)S(1)}, bf16[160,128]{1,0:T(8,128)(2,1)S(1)}, u32[]{:S(2)}, u32[]{:S(2)}) collective-permute-start(bf16[160,128]{1,0:T(8,128)(2,1)S(1)} %get-tuple-element.36), channel_id=1, source_target_pairs={{0,12},{4,8},{8,4},{12,0},{16,28},{20,24},{24,20},{28,16},{1,13},{... | collective-permute-start | bytes 122888 | tf_op jit(solution)/shard_map/ppermute | solution.py:404
  26.8 0.3 collective-permute-start.10
  27.1 0.2 collective-permute-done.4
  27.2 1.5 %collective-permute-start.8 = (bf16[160,128]{1,0:T(8,128)(2,1)S(1)}, bf16[160,128]{1,0:T(8,128)(2,1)S(1)}, u32[]{:S(2)}, u32[]{:S(2)}) collective-permute-start(bf16[160,128]{1,0:T(8,128)(2,1)S(1)} %get-tuple-element.38), channel_id=1, source_target_pairs={{0,4},{4,0},{8,12},{12,8},{16,20},{20,16},{24,28},{28,24},{1,5},{5... | collective-permute-start | bytes 122888 | tf_op jit(solution)/shard_map/ppermute | solution.py:404
  28.8 0.0 collective-permute-done.5
  28.8 0.0 collective-permute-start.9
  28.8 0.0 collective-permute-done.3
  28.8 0.7 %collective-permute-done.6 = bf16[160,128]{1,0:T(8,128)(2,1)S(1)} collective-permute-done((bf16[160,128]{1,0:T(8,128)(2,1)S(1)}, bf16[160,128]{1,0:T(8,128)(2,1)S(1)}, u32[]{:S(2)}, u32[]{:S(2)}) %collective-permute-start.6) | collective-permute-done | bytes 40992 | tf_op jit(solution)/shard_map/ppermute | solution.py:404
  29.6 1.6 %collective-permute-start.7 = (bf16[800,128]{1,0:T(8,128)(2,1)S(1)}, bf16[800,128]{1,0:T(8,128)(2,1)S(1)}, u32[]{:S(2)}, u32[]{:S(2)}) collective-permute-start(bf16[800,128]{1,0:T(8,128)(2,1)S(1)} %constant_dynamic-update-slice_fusion.rest_0_), channel_id=1, source_target_pairs={{0,2},{1,3},{2,0},{3,1},{4,6},{5,7},{6,4},{7,5},{8,10},{9,11},{10,... | collective-permute-start | bytes 614408 | tf_op jit(solution)/shard_map/ppermute | solution.py:406
  31.2 0.1 collective-permute-done.8
  31.3 1.5 %collective-permute-done.9 = bf16[160,128]{1,0:T(8,128)(2,1)S(1)} collective-permute-done((bf16[160,128]{1,0:T(8,128)(2,1)S(1)}, bf16[160,128]{1,0:T(8,128)(2,1)S(1)}, u32[]{:S(2)}, u32[]{:S(2)}) %collective-permute-start.9) | collective-permute-done | bytes 40992 | tf_op jit(solution)/shard_map/ppermute | solution.py:404
  32.8 0.0 collective-permute-done.10
  32.8 1.6 %collective-permute-start.11 = (bf16[480,128]{1,0:T(8,128)(2,1)S(1)}, bf16[480,128]{1,0:T(8,128)(2,1)S(1)}, u32[]{:S(2)}, u32[]{:S(2)}) collective-permute-start(bf16[480,128]{1,0:T(8,128)(2,1)S(1)} %constant_dynamic-update-slice_fusion.5.rest_1_), channel_id=1, source_target_pairs={{0,2},{1,3},{2,0},{3,1},{4,6},{5,7},{6,4},{7,5},{8,10},{9,11},{10,... | collective-permute-start | bytes 368648 | tf_op jit(solution)/shard_map/ppermute | solution.py:406
  34.4 0.0 collective-permute-start.14
  34.4 1.5 %collective-permute-done.7.rest_0_ = bf16[800,128]{1,0:T(8,128)(2,1)S(1)} collective-permute-done((bf16[800,128]{1,0:T(8,128)(2,1)S(1)}, bf16[800,128]{1,0:T(8,128)(2,1)S(1)}, u32[]{:S(2)}, u32[]{:S(2)}) %collective-permute-start.7) | collective-permute-done | bytes 204832 | tf_op jit(solution)/shard_map/ppermute | solution.py:406
  36.0 0.0 collective-permute-start.12
  36.0 0.5 collective-permute-start.15
  36.5 1.3 %collective-permute-done.11.rest_1_ = bf16[480,128]{1,0:T(8,128)(2,1)S(1)} collective-permute-done((bf16[480,128]{1,0:T(8,128)(2,1)S(1)}, bf16[480,128]{1,0:T(8,128)(2,1)S(1)}, u32[]{:S(2)}, u32[]{:S(2)}) %collective-permute-start.11) | collective-permute-done | bytes 122912 | tf_op jit(solution)/shard_map/ppermute | solution.py:406
  37.8 0.0 collective-permute-start.13
  37.8 0.0 collective-permute-done.15.rest_3_
  37.8 0.0 collective-permute-done.14.rest_2_
  37.8 0.9 %staged.1.rest_4_ = bf16[80,4096]{1,0:T(8,128)(2,1)S(1)} custom-call(bf16[800,128]{1,0:T(8,128)(2,1)S(1)} %constant_dynamic-update-slice_fusion.rest_0_, bf16[480,128]{1,0:T(8,128)(2,1)S(1)} %constant_dynamic-update-slice_fusion.5.rest_1_, bf16[800,128]{1,0:T(8,128)(2,1)S(1)} %collective-permute-done.14.rest_2_, ...), custom_call_target="tpu_custom_call" | custom-call | flops 327680 | bytes 2621440 | tf_op jit(solution)/shard_map/staged/pallas_call | solution.py:281
  38.7 0.4 collective-permute-done.13.rest_3_
  39.1 0.0 collective-permute-done.12.rest_2_
  39.1 2.1 %scores.1 = bf16[192,640]{1,0:T(8,128)(2,1)S(1)} custom-call(bf16[800,128]{1,0:T(8,128)(2,1)S(1)} %collective-permute-done.7.rest_0_, bf16[480,128]{1,0:T(8,128)(2,1)S(1)} %collective-permute-done.11.rest_1_, bf16[800,128]{1,0:T(8,128)(2,1)S(1)} %collective-permute-done.12.rest_2_, bf16[480,128]{1,0:T(8,128)(2,1)S(1)} %collective-permute-done.13.rest_3_, ...), custom_call_target="tpu_custom_call" | custom-call | flops 838860800 | bytes 5242880 | tf_op jit(solution)/shard_map/scores/pallas_call | solution.py:323
  41.2 12.8 %all_to_all.5 = bf16[8,24,640]{2,1,0:T(8,128)(2,1)S(1)} all-to-all(bf16[8,24,640]{2,1,0:T(8,128)(2,1)S(1)} %bitcast.9), channel_id=1, replica_groups=mesh['dp'=8,'tensor'=4] {'dp'}, dimensions={0} | all-to-all | bytes 491520 | tf_op jit(solution)/shard_map/all_to_all | solution.py:412
  54.0 0.0 copy-done
  54.0 0.9 %pick_rows.1 = f32[320,128]{1,0:T(8,128)} custom-call(s32[1,64]{1,0:T(1,128)S(1)} %copy-done, bf16[192,640]{1,0:T(8,128)(2,1)S(1)} %bitcast.10), custom_call_target="tpu_custom_call" | custom-call | flops 16000000 | bytes 400000 | tf_op jit(solution)/shard_map/pick_rows/pallas_call | solution.py:354
  (9 shorter events, 0.1 us)
Async XLA Ops:
  7.1 1.6 %collective-permute-start.1 = (f32[384,128]{1,0:T(8,128)S(1)}, f32[384,128]{1,0:T(8,128)S(1)}, u32[]{:S(2)}, u32[]{:S(2)}) collective-permute-start(f32[384,128]{1,0:T(8,128)S(1)} %get-tuple-element.31), channel_id=1, source_target_pairs={{0,1},{1,0},{2,3},{3,2},{4,5},{5,4},{6,7},{7,6},{8,9},{9,8},{10,11... | collective-permute-start | bytes 589832 | tf_op jit(solution)/shard_map/ppermute | solution.py:390
  7.6 4.1 %collective-permute-start = (f32[384,128]{1,0:T(8,128)S(1)}, f32[384,128]{1,0:T(8,128)S(1)}, u32[]{:S(2)}, u32[]{:S(2)}) collective-permute-start(f32[384,128]{1,0:T(8,128)S(1)} %get-tuple-element.27), channel_id=1, source_target_pairs={{0,1},{1,0},{2,3},{3,2},{4,5},{5,4},{6,7},{7,6},{8,9},{9,8},{10,11... | collective-permute-start | bytes 589832 | tf_op jit(solution)/shard_map/ppermute | solution.py:391
  8.7 8.2 %collective-permute-start.2 = (f32[384,128]{1,0:T(8,128)S(1)}, f32[384,128]{1,0:T(8,128)S(1)}, u32[]{:S(2)}, u32[]{:S(2)}) collective-permute-start(f32[384,128]{1,0:T(8,128)S(1)} %add.3), channel_id=1, source_target_pairs={{0,2},{1,3},{2,0},{3,1},{4,6},{5,7},{6,4},{7,5},{8,10},{9,11},{10,... | collective-permute-start | bytes 589832 | tf_op jit(solution)/shard_map/ppermute | solution.py:392
  14.2 39.8 %copy-start = (s32[1,64]{1,0:T(1,128)S(1)}, s32[1,64]{1,0:T(1,128)}, u32[]{:S(2)}) copy-start(s32[1,64]{1,0:T(1,128)} %get-tuple-element.24.row_ref) | copy-start | bytes 772
  17.5 11.3 %collective-permute-start.3 = (bf16[160,128]{1,0:T(8,128)(2,1)S(1)}, bf16[160,128]{1,0:T(8,128)(2,1)S(1)}, u32[]{:S(2)}, u32[]{:S(2)}) collective-permute-start(bf16[160,128]{1,0:T(8,128)(2,1)S(1)} %get-tuple-element.33), channel_id=1, source_target_pairs={{0,24},{4,28},{8,16},{12,20},{16,8},{20,12},{24,0},{28,4},{1,25},{... | collective-permute-start | bytes 122888 | tf_op jit(solution)/shard_map/ppermute | solution.py:404
  21.4 5.8 %collective-permute-start.4 = (bf16[160,128]{1,0:T(8,128)(2,1)S(1)}, bf16[160,128]{1,0:T(8,128)(2,1)S(1)}, u32[]{:S(2)}, u32[]{:S(2)}) collective-permute-start(bf16[160,128]{1,0:T(8,128)(2,1)S(1)} %get-tuple-element.34), channel_id=1, source_target_pairs={{0,20},{4,16},{8,28},{12,24},{16,4},{20,0},{24,12},{28,8},{1,21},{... | collective-permute-start | bytes 122888 | tf_op jit(solution)/shard_map/ppermute | solution.py:404
  21.8 7.0 %collective-permute-start.5 = (bf16[160,128]{1,0:T(8,128)(2,1)S(1)}, bf16[160,128]{1,0:T(8,128)(2,1)S(1)}, u32[]{:S(2)}, u32[]{:S(2)}) collective-permute-start(bf16[160,128]{1,0:T(8,128)(2,1)S(1)} %get-tuple-element.35), channel_id=1, source_target_pairs={{0,28},{4,24},{8,20},{12,16},{16,12},{20,8},{24,4},{28,0},{1,29},{... | collective-permute-start | bytes 122888 | tf_op jit(solution)/shard_map/ppermute | solution.py:404
  24.3 5.3 %collective-permute-start.6 = (bf16[160,128]{1,0:T(8,128)(2,1)S(1)}, bf16[160,128]{1,0:T(8,128)(2,1)S(1)}, u32[]{:S(2)}, u32[]{:S(2)}) collective-permute-start(bf16[160,128]{1,0:T(8,128)(2,1)S(1)} %get-tuple-element.36), channel_id=1, source_target_pairs={{0,12},{4,8},{8,4},{12,0},{16,28},{20,24},{24,20},{28,16},{1,13},{... | collective-permute-start | bytes 122888 | tf_op jit(solution)/shard_map/ppermute | solution.py:404
  26.8 6.0 %collective-permute-start.10 = (bf16[160,128]{1,0:T(8,128)(2,1)S(1)}, bf16[160,128]{1,0:T(8,128)(2,1)S(1)}, u32[]{:S(2)}, u32[]{:S(2)}) collective-permute-start(bf16[160,128]{1,0:T(8,128)(2,1)S(1)} %get-tuple-element.41), channel_id=1, source_target_pairs={{0,16},{4,20},{8,24},{12,28},{16,0},{20,4},{24,8},{28,12},{1,17},{... | collective-permute-start | bytes 122888 | tf_op jit(solution)/shard_map/ppermute | solution.py:404
  27.2 4.0 %collective-permute-start.8 = (bf16[160,128]{1,0:T(8,128)(2,1)S(1)}, bf16[160,128]{1,0:T(8,128)(2,1)S(1)}, u32[]{:S(2)}, u32[]{:S(2)}) collective-permute-start(bf16[160,128]{1,0:T(8,128)(2,1)S(1)} %get-tuple-element.38), channel_id=1, source_target_pairs={{0,4},{4,0},{8,12},{12,8},{16,20},{20,16},{24,28},{28,24},{1,5},{5... | collective-permute-start | bytes 122888 | tf_op jit(solution)/shard_map/ppermute | solution.py:404
  28.8 4.0 %collective-permute-start.9 = (bf16[160,128]{1,0:T(8,128)(2,1)S(1)}, bf16[160,128]{1,0:T(8,128)(2,1)S(1)}, u32[]{:S(2)}, u32[]{:S(2)}) collective-permute-start(bf16[160,128]{1,0:T(8,128)(2,1)S(1)} %get-tuple-element.40), channel_id=1, source_target_pairs={{0,8},{4,12},{8,0},{12,4},{16,24},{20,28},{24,16},{28,20},{1,9},{5... | collective-permute-start | bytes 122888 | tf_op jit(solution)/shard_map/ppermute | solution.py:404
  29.6 6.4 %collective-permute-start.7 = (bf16[800,128]{1,0:T(8,128)(2,1)S(1)}, bf16[800,128]{1,0:T(8,128)(2,1)S(1)}, u32[]{:S(2)}, u32[]{:S(2)}) collective-permute-start(bf16[800,128]{1,0:T(8,128)(2,1)S(1)} %constant_dynamic-update-slice_fusion.rest_0_), channel_id=1, source_target_pairs={{0,2},{1,3},{2,0},{3,1},{4,6},{5,7},{6,4},{7,5},{8,10},{9,11},{10,... | collective-permute-start | bytes 614408 | tf_op jit(solution)/shard_map/ppermute | solution.py:406
  32.8 4.9 %collective-permute-start.11 = (bf16[480,128]{1,0:T(8,128)(2,1)S(1)}, bf16[480,128]{1,0:T(8,128)(2,1)S(1)}, u32[]{:S(2)}, u32[]{:S(2)}) collective-permute-start(bf16[480,128]{1,0:T(8,128)(2,1)S(1)} %constant_dynamic-update-slice_fusion.5.rest_1_), channel_id=1, source_target_pairs={{0,2},{1,3},{2,0},{3,1},{4,6},{5,7},{6,4},{7,5},{8,10},{9,11},{10,... | collective-permute-start | bytes 368648 | tf_op jit(solution)/shard_map/ppermute | solution.py:406
  34.4 3.4 %collective-permute-start.14 = (bf16[800,128]{1,0:T(8,128)(2,1)S(1)}, bf16[800,128]{1,0:T(8,128)(2,1)S(1)}, u32[]{:S(2)}, u32[]{:S(2)}) collective-permute-start(bf16[800,128]{1,0:T(8,128)(2,1)S(1)} %constant_dynamic-update-slice_fusion.rest_0_), channel_id=1, source_target_pairs={{0,1},{1,0},{2,3},{3,2},{4,5},{5,4},{6,7},{7,6},{8,9},{9,8},{10,11... | collective-permute-start | bytes 614408 | tf_op jit(solution)/shard_map/ppermute | solution.py:407
  36.0 3.2 %collective-permute-start.12 = (bf16[800,128]{1,0:T(8,128)(2,1)S(1)}, bf16[800,128]{1,0:T(8,128)(2,1)S(1)}, u32[]{:S(2)}, u32[]{:S(2)}) collective-permute-start(bf16[800,128]{1,0:T(8,128)(2,1)S(1)} %collective-permute-done.7.rest_0_), channel_id=1, source_target_pairs={{0,1},{1,0},{2,3},{3,2},{4,5},{5,4},{6,7},{7,6},{8,9},{9,8},{10,11... | collective-permute-start | bytes 614408 | tf_op jit(solution)/shard_map/ppermute | solution.py:409
  36.0 1.8 %collective-permute-start.15 = (bf16[480,128]{1,0:T(8,128)(2,1)S(1)}, bf16[480,128]{1,0:T(8,128)(2,1)S(1)}, u32[]{:S(2)}, u32[]{:S(2)}) collective-permute-start(bf16[480,128]{1,0:T(8,128)(2,1)S(1)} %constant_dynamic-update-slice_fusion.5.rest_1_), channel_id=1, source_target_pairs={{0,1},{1,0},{2,3},{3,2},{4,5},{5,4},{6,7},{7,6},{8,9},{9,8},{10,11... | collective-permute-start | bytes 368648 | tf_op jit(solution)/shard_map/ppermute | solution.py:407
  37.8 1.3 %collective-permute-start.13 = (bf16[480,128]{1,0:T(8,128)(2,1)S(1)}, bf16[480,128]{1,0:T(8,128)(2,1)S(1)}, u32[]{:S(2)}, u32[]{:S(2)}) collective-permute-start(bf16[480,128]{1,0:T(8,128)(2,1)S(1)} %collective-permute-done.11.rest_1_), channel_id=1, source_target_pairs={{0,1},{1,0},{2,3},{3,2},{4,5},{5,4},{6,7},{7,6},{8,9},{9,8},{10,11... | collective-permute-start | bytes 368648 | tf_op jit(solution)/shard_map/ppermute | solution.py:409

commit v8 on v7

--- a/solution.py
+++ b/solution.py
@@ -12,7 +12,7 @@
 NT = (((1,), (1,)), ((), ()))
 TN = (((0,), (0,)), ((), ()))
 
-PLANS = {8: (((0, 6, 5, 7, 3), (1, 2, 4)), {1: 5, 2: 7})}
+PLANS = {8: (((0, 4, 7, 3, 6), (5, 1, 2)), {2: 4})}
 
 
 def project_kernel(

time: 55 us -> 54.8 us (level)
  waiting for transfers between devices: 9.39 us -> 8.8 us
    ppermute x7, waiting for transfers between devices: 2.52 us -> 1.66 us  [local_one(): arrived[k] = lax.ppermute(block, 'dp', [(i, i ^ k) for i in range(groups)])]
where the time goes in v8:
time: 54.8 us; the launch traced here: 54.6 us
  starting transfers between devices  18.5 us (34%)
  Pallas kernels  14.2 us (26%)
  blocking collectives  12.9 us (24%)
  waiting for transfers between devices  8.8 us (16%)
    all_to_all x1, blocking collectives, local_one(): lax.all_to_all(block, 'dp', split_axis=0, concat_axis=0, tiled=True)  12.9 us
    ppermute x7, starting transfers between devices, local_one(): arrived[k] = lax.ppermute(block, 'dp', [(i, i ^ k) for i in range(groups)])  11.3 us
    pallas_call x1, Pallas kernels, project(): pl.pallas_call(functools.partial(project_kernel, groups, ways, tokens, sl...  7.05 us
    ppermute x2, starting transfers between devices, local_one(): over_y = [lax.ppermute(x, 'tensor', across) for x in own]  3.13 us
    ppermute x2, waiting for transfers between devices, local_one(): over_y = [lax.ppermute(x, 'tensor', across) for x in own]  3.11 us
    ppermute x1, starting transfers between devices, local_one(): across_in = lax.ppermute(over_part + far_in, 'tensor', across)  2.95 us
    ppermute x1, waiting for transfers between devices, local_one(): across_in = lax.ppermute(over_part + far_in, 'tensor', across)  2.65 us
    pallas_call x1, Pallas kernels, own_sum(): pl.pallas_call(own_kernel, in_specs=[smem, vmem, vmem, pl.BlockSpec(memor...  2.54 us
  transfers between devices with their start and end apart: 16, of which 9 were waited for; matrix products, arithmetic and copies ran while one was open for 0% of the time, Pallas kernels for 6%

profile of v8, /device:TPU:0, one launch (start us, length us, event | category | flops | bytes accessed | tf_op | source)
XLA Modules:
  0.0 54.6 jit_solution(661088971440391087)
XLA Ops:
  0.0 7.1 %project.1 = (f32[384,128]{1,0:T(8,128)S(1)}, f32[384,128]{1,0:T(8,128)S(1)}, f32[384,128]{1,0:T(8,128)S(1)}, f32[384,128]{1,0:T(8,128)S(1)}, s32[64]{0:T(128)S(4)}, /*index=5*/s32[1,64]{1,0:T(1,128)}) custom-call(s32[1,64]{1,0:T(1,128)} %bitcast.16, bf16[1536,3584]{1,0:T(8,128)(2,1)} %bitcast.11, bf16[1536,1024]{1,0:T(8,128)(2,1)} %bitcast.13, ...), custom_call_target="tpu_custom_call" | custom-call | flops 905969664 | bytes 14155776 | tf_op jit(solution)/shard_map/project/pallas_call | solution.py:131
  7.1 0.5 collective-permute-start.1
  7.6 0.1 collective-permute-start
  7.7 1.0 %collective-permute-done.1 = f32[384,128]{1,0:T(8,128)S(1)} collective-permute-done((f32[384,128]{1,0:T(8,128)S(1)}, f32[384,128]{1,0:T(8,128)S(1)}, u32[]{:S(2)}, u32[]{:S(2)}) %collective-permute-start.1) | collective-permute-done | bytes 196640 | tf_op jit(solution)/shard_map/ppermute | solution.py:390
  8.7 3.0 %collective-permute-start.2 = (f32[384,128]{1,0:T(8,128)S(1)}, f32[384,128]{1,0:T(8,128)S(1)}, u32[]{:S(2)}, u32[]{:S(2)}) collective-permute-start(f32[384,128]{1,0:T(8,128)S(1)} %add.3), channel_id=1, source_target_pairs={{0,2},{1,3},{2,0},{3,1},{4,6},{5,7},{6,4},{7,5},{8,10},{9,11},{10,... | collective-permute-start | bytes 589832 | tf_op jit(solution)/shard_map/ppermute | solution.py:392
  11.6 0.0 collective-permute-done.b_ref
  11.6 2.5 %own_sum.1 = (s32[16]{0:T(128)S(4)}, f32[384,128]{1,0:T(8,128)S(1)}, bf16[640,4096]{1,0:T(8,128)(2,1)S(1)}) custom-call(s32[64]{0:T(128)S(4)} %get-tuple-element.24.slot_ref, f32[384,128]{1,0:T(8,128)S(1)} %get-tuple-element.25.a_ref, f32[384,128]{1,0:T(8,128)S(1)} %collective-permute-done.b_ref, bf16[640,4096]{1,0:T(8,128)(2,1)} %bitcast.12), custom_call_target="tpu_custom_call" | custom-call | flops 49152 | bytes 5242880 | tf_op jit(solution)/shard_map/own_sum/pallas_call | solution.py:186
  14.2 0.0 copy-start
  14.2 2.6 %collective-permute-done.2.b_ref = f32[384,128]{1,0:T(8,128)S(1)} collective-permute-done((f32[384,128]{1,0:T(8,128)S(1)}, f32[384,128]{1,0:T(8,128)S(1)}, u32[]{:S(2)}, u32[]{:S(2)}) %collective-permute-start.2) | collective-permute-done | bytes 196640 | tf_op jit(solution)/shard_map/ppermute | solution.py:392
  16.8 0.7 %unit_grads.1 = (bf16[160,128]{1,0:T(8,128)(2,1)S(1)}, bf16[160,128]{1,0:T(8,128)(2,1)S(1)}, bf16[160,128]{1,0:T(8,128)(2,1)S(1)}, bf16[160,128]{1,0:T(8,128)(2,...) custom-call(s32[16]{0:T(128)S(4)} %get-tuple-element.27.row_ref, ...), custom_call_target="tpu_custom_call" | custom-call | flops 20000000 | bytes 1000000 | tf_op jit(solution)/shard_map/unit_grads/pallas_call | solution.py:238
  17.5 2.9 %collective-permute-start.3 = (bf16[160,128]{1,0:T(8,128)(2,1)S(1)}, bf16[160,128]{1,0:T(8,128)(2,1)S(1)}, u32[]{:S(2)}, u32[]{:S(2)}) collective-permute-start(bf16[160,128]{1,0:T(8,128)(2,1)S(1)} %get-tuple-element.32), channel_id=1, source_target_pairs={{0,16},{4,20},{8,24},{12,28},{16,0},{20,4},{24,8},{28,12},{1,17},{... | collective-permute-start | bytes 122888 | tf_op jit(solution)/shard_map/ppermute | solution.py:404
  20.4 2.3 %collective-permute-start.4 = (bf16[160,128]{1,0:T(8,128)(2,1)S(1)}, bf16[160,128]{1,0:T(8,128)(2,1)S(1)}, u32[]{:S(2)}, u32[]{:S(2)}) collective-permute-start(bf16[160,128]{1,0:T(8,128)(2,1)S(1)} %get-tuple-element.33), channel_id=1, source_target_pairs={{0,28},{4,24},{8,20},{12,16},{16,12},{20,8},{24,4},{28,0},{1,29},{... | collective-permute-start | bytes 122888 | tf_op jit(solution)/shard_map/ppermute | solution.py:404
  22.7 0.2 collective-permute-start.5
  22.9 2.9 %collective-permute-start.6 = (bf16[160,128]{1,0:T(8,128)(2,1)S(1)}, bf16[160,128]{1,0:T(8,128)(2,1)S(1)}, u32[]{:S(2)}, u32[]{:S(2)}) collective-permute-start(bf16[160,128]{1,0:T(8,128)(2,1)S(1)} %get-tuple-element.35), channel_id=1, source_target_pairs={{0,24},{4,28},{8,16},{12,20},{16,8},{20,12},{24,0},{28,4},{1,25},{... | collective-permute-start | bytes 122888 | tf_op jit(solution)/shard_map/ppermute | solution.py:404
  25.8 1.2 %collective-permute-start.8 = (bf16[160,128]{1,0:T(8,128)(2,1)S(1)}, bf16[160,128]{1,0:T(8,128)(2,1)S(1)}, u32[]{:S(2)}, u32[]{:S(2)}) collective-permute-start(bf16[160,128]{1,0:T(8,128)(2,1)S(1)} %get-tuple-element.36), channel_id=1, source_target_pairs={{0,20},{4,16},{8,28},{12,24},{16,4},{20,0},{24,12},{28,8},{1,21},{... | collective-permute-start | bytes 122888 | tf_op jit(solution)/shard_map/ppermute | solution.py:404
  27.1 0.0 collective-permute-done.3
  27.1 0.5 %collective-permute-start.9 = (bf16[160,128]{1,0:T(8,128)(2,1)S(1)}, bf16[160,128]{1,0:T(8,128)(2,1)S(1)}, u32[]{:S(2)}, u32[]{:S(2)}) collective-permute-start(bf16[160,128]{1,0:T(8,128)(2,1)S(1)} %get-tuple-element.37), channel_id=1, source_target_pairs={{0,4},{4,0},{8,12},{12,8},{16,20},{20,16},{24,28},{28,24},{1,5},{5... | collective-permute-start | bytes 122888 | tf_op jit(solution)/shard_map/ppermute | solution.py:404
  27.6 0.0 collective-permute-done.4
  27.6 1.2 %collective-permute-start.10 = (bf16[160,128]{1,0:T(8,128)(2,1)S(1)}, bf16[160,128]{1,0:T(8,128)(2,1)S(1)}, u32[]{:S(2)}, u32[]{:S(2)}) collective-permute-start(bf16[160,128]{1,0:T(8,128)(2,1)S(1)} %get-tuple-element.39), channel_id=1, source_target_pairs={{0,8},{4,12},{8,0},{12,4},{16,24},{20,28},{24,16},{28,20},{1,9},{5... | collective-permute-start | bytes 122888 | tf_op jit(solution)/shard_map/ppermute | solution.py:404
  28.9 0.0 collective-permute-done.5
  28.9 0.3 collective-permute-done.6
  29.2 1.6 %collective-permute-start.7 = (bf16[800,128]{1,0:T(8,128)(2,1)S(1)}, bf16[800,128]{1,0:T(8,128)(2,1)S(1)}, u32[]{:S(2)}, u32[]{:S(2)}) collective-permute-start(bf16[800,128]{1,0:T(8,128)(2,1)S(1)} %constant_dynamic-update-slice_fusion.rest_0_), channel_id=1, source_target_pairs={{0,2},{1,3},{2,0},{3,1},{4,6},{5,7},{6,4},{7,5},{8,10},{9,11},{10,... | collective-permute-start | bytes 614408 | tf_op jit(solution)/shard_map/ppermute | solution.py:406
  30.8 1.2 %collective-permute-done.8 = bf16[160,128]{1,0:T(8,128)(2,1)S(1)} collective-permute-done((bf16[160,128]{1,0:T(8,128)(2,1)S(1)}, bf16[160,128]{1,0:T(8,128)(2,1)S(1)}, u32[]{:S(2)}, u32[]{:S(2)}) %collective-permute-start.8) | collective-permute-done | bytes 40992 | tf_op jit(solution)/shard_map/ppermute | solution.py:404
  32.0 0.0 collective-permute-done.9
  32.0 0.1 collective-permute-done.10
  32.2 1.6 %collective-permute-start.11 = (bf16[480,128]{1,0:T(8,128)(2,1)S(1)}, bf16[480,128]{1,0:T(8,128)(2,1)S(1)}, u32[]{:S(2)}, u32[]{:S(2)}) collective-permute-start(bf16[480,128]{1,0:T(8,128)(2,1)S(1)} %constant_dynamic-update-slice_fusion.5.rest_1_), channel_id=1, source_target_pairs={{0,2},{1,3},{2,0},{3,1},{4,6},{5,7},{6,4},{7,5},{8,10},{9,11},{10,... | collective-permute-start | bytes 368648 | tf_op jit(solution)/shard_map/ppermute | solution.py:406
  33.7 0.0 collective-permute-start.14
  33.7 2.3 %collective-permute-done.7.rest_0_ = bf16[800,128]{1,0:T(8,128)(2,1)S(1)} collective-permute-done((bf16[800,128]{1,0:T(8,128)(2,1)S(1)}, bf16[800,128]{1,0:T(8,128)(2,1)S(1)}, u32[]{:S(2)}, u32[]{:S(2)}) %collective-permute-start.7) | collective-permute-done | bytes 204832 | tf_op jit(solution)/shard_map/ppermute | solution.py:406
  36.0 0.0 collective-permute-start.12
  36.0 0.5 collective-permute-start.15
  36.5 0.8 %collective-permute-done.11.rest_1_ = bf16[480,128]{1,0:T(8,128)(2,1)S(1)} collective-permute-done((bf16[480,128]{1,0:T(8,128)(2,1)S(1)}, bf16[480,128]{1,0:T(8,128)(2,1)S(1)}, u32[]{:S(2)}, u32[]{:S(2)}) %collective-permute-start.11) | collective-permute-done | bytes 122912 | tf_op jit(solution)/shard_map/ppermute | solution.py:406
  37.4 0.0 collective-permute-start.13
  37.4 0.3 collective-permute-done.15.rest_3_
  37.7 0.0 collective-permute-done.14.rest_2_
  37.7 0.9 %staged.1.rest_4_ = bf16[80,4096]{1,0:T(8,128)(2,1)S(1)} custom-call(bf16[800,128]{1,0:T(8,128)(2,1)S(1)} %constant_dynamic-update-slice_fusion.rest_0_, bf16[480,128]{1,0:T(8,128)(2,1)S(1)} %constant_dynamic-update-slice_fusion.5.rest_1_, bf16[800,128]{1,0:T(8,128)(2,1)S(1)} %collective-permute-done.14.rest_2_, ...), custom_call_target="tpu_custom_call" | custom-call | flops 327680 | bytes 2621440 | tf_op jit(solution)/shard_map/staged/pallas_call | solution.py:281
  38.6 0.1 collective-permute-done.13.rest_3_
  38.7 0.0 collective-permute-done.12.rest_2_
  38.7 2.1 %scores.1 = bf16[192,640]{1,0:T(8,128)(2,1)S(1)} custom-call(bf16[800,128]{1,0:T(8,128)(2,1)S(1)} %collective-permute-done.7.rest_0_, bf16[480,128]{1,0:T(8,128)(2,1)S(1)} %collective-permute-done.11.rest_1_, bf16[800,128]{1,0:T(8,128)(2,1)S(1)} %collective-permute-done.12.rest_2_, bf16[480,128]{1,0:T(8,128)(2,1)S(1)} %collective-permute-done.13.rest_3_, ...), custom_call_target="tpu_custom_call" | custom-call | flops 838860800 | bytes 5242880 | tf_op jit(solution)/shard_map/scores/pallas_call | solution.py:323
  40.8 12.9 %all_to_all.5 = bf16[8,24,640]{2,1,0:T(8,128)(2,1)S(1)} all-to-all(bf16[8,24,640]{2,1,0:T(8,128)(2,1)S(1)} %bitcast.9), channel_id=1, replica_groups=mesh['dp'=8,'tensor'=4] {'dp'}, dimensions={0} | all-to-all | bytes 491520 | tf_op jit(solution)/shard_map/all_to_all | solution.py:412
  53.7 0.0 copy-done
  53.7 0.9 %pick_rows.1 = f32[320,128]{1,0:T(8,128)} custom-call(s32[1,64]{1,0:T(1,128)S(1)} %copy-done, bf16[192,640]{1,0:T(8,128)(2,1)S(1)} %bitcast.10), custom_call_target="tpu_custom_call" | custom-call | flops 16000000 | bytes 400000 | tf_op jit(solution)/shard_map/pick_rows/pallas_call | solution.py:354
  (9 shorter events, 0.1 us)
Async XLA Ops:
  7.1 1.6 %collective-permute-start.1 = (f32[384,128]{1,0:T(8,128)S(1)}, f32[384,128]{1,0:T(8,128)S(1)}, u32[]{:S(2)}, u32[]{:S(2)}) collective-permute-start(f32[384,128]{1,0:T(8,128)S(1)} %get-tuple-element.30), channel_id=1, source_target_pairs={{0,1},{1,0},{2,3},{3,2},{4,5},{5,4},{6,7},{7,6},{8,9},{9,8},{10,11... | collective-permute-start | bytes 589832 | tf_op jit(solution)/shard_map/ppermute | solution.py:390
  7.6 4.1 %collective-permute-start = (f32[384,128]{1,0:T(8,128)S(1)}, f32[384,128]{1,0:T(8,128)S(1)}, u32[]{:S(2)}, u32[]{:S(2)}) collective-permute-start(f32[384,128]{1,0:T(8,128)S(1)} %get-tuple-element.26), channel_id=1, source_target_pairs={{0,1},{1,0},{2,3},{3,2},{4,5},{5,4},{6,7},{7,6},{8,9},{9,8},{10,11... | collective-permute-start | bytes 589832 | tf_op jit(solution)/shard_map/ppermute | solution.py:391
  8.7 8.2 %collective-permute-start.2 = (f32[384,128]{1,0:T(8,128)S(1)}, f32[384,128]{1,0:T(8,128)S(1)}, u32[]{:S(2)}, u32[]{:S(2)}) collective-permute-start(f32[384,128]{1,0:T(8,128)S(1)} %add.3), channel_id=1, source_target_pairs={{0,2},{1,3},{2,0},{3,1},{4,6},{5,7},{6,4},{7,5},{8,10},{9,11},{10,... | collective-permute-start | bytes 589832 | tf_op jit(solution)/shard_map/ppermute | solution.py:392
  14.2 39.5 %copy-start = (s32[1,64]{1,0:T(1,128)S(1)}, s32[1,64]{1,0:T(1,128)}, u32[]{:S(2)}) copy-start(s32[1,64]{1,0:T(1,128)} %get-tuple-element.23.row_ref) | copy-start | bytes 772
  17.5 9.5 %collective-permute-start.3 = (bf16[160,128]{1,0:T(8,128)(2,1)S(1)}, bf16[160,128]{1,0:T(8,128)(2,1)S(1)}, u32[]{:S(2)}, u32[]{:S(2)}) collective-permute-start(bf16[160,128]{1,0:T(8,128)(2,1)S(1)} %get-tuple-element.32), channel_id=1, source_target_pairs={{0,16},{4,20},{8,24},{12,28},{16,0},{20,4},{24,8},{28,12},{1,17},{... | collective-permute-start | bytes 122888 | tf_op jit(solution)/shard_map/ppermute | solution.py:404
  20.4 7.2 %collective-permute-start.4 = (bf16[160,128]{1,0:T(8,128)(2,1)S(1)}, bf16[160,128]{1,0:T(8,128)(2,1)S(1)}, u32[]{:S(2)}, u32[]{:S(2)}) collective-permute-start(bf16[160,128]{1,0:T(8,128)(2,1)S(1)} %get-tuple-element.33), channel_id=1, source_target_pairs={{0,28},{4,24},{8,20},{12,16},{16,12},{20,8},{24,4},{28,0},{1,29},{... | collective-permute-start | bytes 122888 | tf_op jit(solution)/shard_map/ppermute | solution.py:404
  22.7 6.2 %collective-permute-start.5 = (bf16[160,128]{1,0:T(8,128)(2,1)S(1)}, bf16[160,128]{1,0:T(8,128)(2,1)S(1)}, u32[]{:S(2)}, u32[]{:S(2)}) collective-permute-start(bf16[160,128]{1,0:T(8,128)(2,1)S(1)} %get-tuple-element.34), channel_id=1, source_target_pairs={{0,12},{4,8},{8,4},{12,0},{16,28},{20,24},{24,20},{28,16},{1,13},{... | collective-permute-start | bytes 122888 | tf_op jit(solution)/shard_map/ppermute | solution.py:404
  22.9 6.3 %collective-permute-start.6 = (bf16[160,128]{1,0:T(8,128)(2,1)S(1)}, bf16[160,128]{1,0:T(8,128)(2,1)S(1)}, u32[]{:S(2)}, u32[]{:S(2)}) collective-permute-start(bf16[160,128]{1,0:T(8,128)(2,1)S(1)} %get-tuple-element.35), channel_id=1, source_target_pairs={{0,24},{4,28},{8,16},{12,20},{16,8},{20,12},{24,0},{28,4},{1,25},{... | collective-permute-start | bytes 122888 | tf_op jit(solution)/shard_map/ppermute | solution.py:404
  25.8 6.2 %collective-permute-start.8 = (bf16[160,128]{1,0:T(8,128)(2,1)S(1)}, bf16[160,128]{1,0:T(8,128)(2,1)S(1)}, u32[]{:S(2)}, u32[]{:S(2)}) collective-permute-start(bf16[160,128]{1,0:T(8,128)(2,1)S(1)} %get-tuple-element.36), channel_id=1, source_target_pairs={{0,20},{4,16},{8,28},{12,24},{16,4},{20,0},{24,12},{28,8},{1,21},{... | collective-permute-start | bytes 122888 | tf_op jit(solution)/shard_map/ppermute | solution.py:404
  27.1 4.9 %collective-permute-start.9 = (bf16[160,128]{1,0:T(8,128)(2,1)S(1)}, bf16[160,128]{1,0:T(8,128)(2,1)S(1)}, u32[]{:S(2)}, u32[]{:S(2)}) collective-permute-start(bf16[160,128]{1,0:T(8,128)(2,1)S(1)} %get-tuple-element.37), channel_id=1, source_target_pairs={{0,4},{4,0},{8,12},{12,8},{16,20},{20,16},{24,28},{28,24},{1,5},{5... | collective-permute-start | bytes 122888 | tf_op jit(solution)/shard_map/ppermute | solution.py:404
  27.6 4.5 %collective-permute-start.10 = (bf16[160,128]{1,0:T(8,128)(2,1)S(1)}, bf16[160,128]{1,0:T(8,128)(2,1)S(1)}, u32[]{:S(2)}, u32[]{:S(2)}) collective-permute-start(bf16[160,128]{1,0:T(8,128)(2,1)S(1)} %get-tuple-element.39), channel_id=1, source_target_pairs={{0,8},{4,12},{8,0},{12,4},{16,24},{20,28},{24,16},{28,20},{1,9},{5... | collective-permute-start | bytes 122888 | tf_op jit(solution)/shard_map/ppermute | solution.py:404
  29.2 6.8 %collective-permute-start.7 = (bf16[800,128]{1,0:T(8,128)(2,1)S(1)}, bf16[800,128]{1,0:T(8,128)(2,1)S(1)}, u32[]{:S(2)}, u32[]{:S(2)}) collective-permute-start(bf16[800,128]{1,0:T(8,128)(2,1)S(1)} %constant_dynamic-update-slice_fusion.rest_0_), channel_id=1, source_target_pairs={{0,2},{1,3},{2,0},{3,1},{4,6},{5,7},{6,4},{7,5},{8,10},{9,11},{10,... | collective-permute-start | bytes 614408 | tf_op jit(solution)/shard_map/ppermute | solution.py:406
  32.2 5.2 %collective-permute-start.11 = (bf16[480,128]{1,0:T(8,128)(2,1)S(1)}, bf16[480,128]{1,0:T(8,128)(2,1)S(1)}, u32[]{:S(2)}, u32[]{:S(2)}) collective-permute-start(bf16[480,128]{1,0:T(8,128)(2,1)S(1)} %constant_dynamic-update-slice_fusion.5.rest_1_), channel_id=1, source_target_pairs={{0,2},{1,3},{2,0},{3,1},{4,6},{5,7},{6,4},{7,5},{8,10},{9,11},{10,... | collective-permute-start | bytes 368648 | tf_op jit(solution)/shard_map/ppermute | solution.py:406
  33.7 3.9 %collective-permute-start.14 = (bf16[800,128]{1,0:T(8,128)(2,1)S(1)}, bf16[800,128]{1,0:T(8,128)(2,1)S(1)}, u32[]{:S(2)}, u32[]{:S(2)}) collective-permute-start(bf16[800,128]{1,0:T(8,128)(2,1)S(1)} %constant_dynamic-update-slice_fusion.rest_0_), channel_id=1, source_target_pairs={{0,1},{1,0},{2,3},{3,2},{4,5},{5,4},{6,7},{7,6},{8,9},{9,8},{10,11... | collective-permute-start | bytes 614408 | tf_op jit(solution)/shard_map/ppermute | solution.py:407
  36.0 2.7 %collective-permute-start.12 = (bf16[800,128]{1,0:T(8,128)(2,1)S(1)}, bf16[800,128]{1,0:T(8,128)(2,1)S(1)}, u32[]{:S(2)}, u32[]{:S(2)}) collective-permute-start(bf16[800,128]{1,0:T(8,128)(2,1)S(1)} %collective-permute-done.7.rest_0_), channel_id=1, source_target_pairs={{0,1},{1,0},{2,3},{3,2},{4,5},{5,4},{6,7},{7,6},{8,9},{9,8},{10,11... | collective-permute-start | bytes 614408 | tf_op jit(solution)/shard_map/ppermute | solution.py:409
  36.0 1.6 %collective-permute-start.15 = (bf16[480,128]{1,0:T(8,128)(2,1)S(1)}, bf16[480,128]{1,0:T(8,128)(2,1)S(1)}, u32[]{:S(2)}, u32[]{:S(2)}) collective-permute-start(bf16[480,128]{1,0:T(8,128)(2,1)S(1)} %constant_dynamic-update-slice_fusion.5.rest_1_), channel_id=1, source_target_pairs={{0,1},{1,0},{2,3},{3,2},{4,5},{5,4},{6,7},{7,6},{8,9},{9,8},{10,11... | collective-permute-start | bytes 368648 | tf_op jit(solution)/shard_map/ppermute | solution.py:407
  37.4 1.3 %collective-permute-start.13 = (bf16[480,128]{1,0:T(8,128)(2,1)S(1)}, bf16[480,128]{1,0:T(8,128)(2,1)S(1)}, u32[]{:S(2)}, u32[]{:S(2)}) collective-permute-start(bf16[480,128]{1,0:T(8,128)(2,1)S(1)} %collective-permute-done.11.rest_1_), channel_id=1, source_target_pairs={{0,1},{1,0},{2,3},{3,2},{4,5},{5,4},{6,7},{7,6},{8,9},{9,8},{10,11... | collective-permute-start | bytes 368648 | tf_op jit(solution)/shard_map/ppermute | solution.py:409

commit v9 on v8

--- a/solution.py
+++ b/solution.py
@@ -12,7 +12,7 @@
 NT = (((1,), (1,)), ((), ()))
 TN = (((0,), (0,)), ((), ()))
 
-PLANS = {8: (((0, 4, 7, 3, 6), (5, 1, 2)), {2: 4})}
+PLANS = {8: (((0, 4, 7, 3, 6), (5, 1, 2)), {2: 7})}
 
 
 def project_kernel(

time: 54.8 us -> 54.7 us (level)
  no operation moved by 1% of the time
where the time goes in v9:
time: 54.7 us; the launch traced here: 54.5 us
  starting transfers between devices  18.5 us (34%)
  Pallas kernels  14.2 us (26%)
  blocking collectives  12.6 us (23%)
  waiting for transfers between devices  8.99 us (16%)
    all_to_all x1, blocking collectives, local_one(): lax.all_to_all(block, 'dp', split_axis=0, concat_axis=0, tiled=True)  12.6 us
    ppermute x7, starting transfers between devices, local_one(): arrived[k] = lax.ppermute(block, 'dp', [(i, i ^ k) for i in range(groups)])  11.3 us
    pallas_call x1, Pallas kernels, project(): pl.pallas_call(functools.partial(project_kernel, groups, ways, tokens, sl...  7.05 us
    ppermute x2, starting transfers between devices, local_one(): over_y = [lax.ppermute(x, 'tensor', across) for x in own]  3.15 us
    ppermute x1, starting transfers between devices, local_one(): across_in = lax.ppermute(over_part + far_in, 'tensor', across)  2.95 us
    ppermute x2, waiting for transfers between devices, local_one(): over_y = [lax.ppermute(x, 'tensor', across) for x in own]  2.84 us
    ppermute x1, waiting for transfers between devices, local_one(): across_in = lax.ppermute(over_part + far_in, 'tensor', across)  2.65 us
    pallas_call x1, Pallas kernels, own_sum(): pl.pallas_call(own_kernel, in_specs=[smem, vmem, vmem, pl.BlockSpec(memor...  2.54 us
  transfers between devices with their start and end apart: 16, of which 9 were waited for; matrix products, arithmetic and copies ran while one was open for 0% of the time, Pallas kernels for 6%

profile of v9, /device:TPU:0, one launch (start us, length us, event | category | flops | bytes accessed | tf_op | source)
XLA Modules:
  0.0 54.5 jit_solution(12397528663576413464)
XLA Ops:
  0.0 7.1 %project.1 = (f32[384,128]{1,0:T(8,128)S(1)}, f32[384,128]{1,0:T(8,128)S(1)}, f32[384,128]{1,0:T(8,128)S(1)}, f32[384,128]{1,0:T(8,128)S(1)}, s32[64]{0:T(128)S(4)}, /*index=5*/s32[1,64]{1,0:T(1,128)}) custom-call(s32[1,64]{1,0:T(1,128)} %bitcast.16, bf16[1536,3584]{1,0:T(8,128)(2,1)} %bitcast.11, bf16[1536,1024]{1,0:T(8,128)(2,1)} %bitcast.13, ...), custom_call_target="tpu_custom_call" | custom-call | flops 905969664 | bytes 14155776 | tf_op jit(solution)/shard_map/project/pallas_call | solution.py:131
  7.1 0.5 collective-permute-start.1
  7.6 0.1 collective-permute-start
  7.7 1.0 %collective-permute-done.1 = f32[384,128]{1,0:T(8,128)S(1)} collective-permute-done((f32[384,128]{1,0:T(8,128)S(1)}, f32[384,128]{1,0:T(8,128)S(1)}, u32[]{:S(2)}, u32[]{:S(2)}) %collective-permute-start.1) | collective-permute-done | bytes 196640 | tf_op jit(solution)/shard_map/ppermute | solution.py:390
  8.7 3.0 %collective-permute-start.2 = (f32[384,128]{1,0:T(8,128)S(1)}, f32[384,128]{1,0:T(8,128)S(1)}, u32[]{:S(2)}, u32[]{:S(2)}) collective-permute-start(f32[384,128]{1,0:T(8,128)S(1)} %add.3), channel_id=1, source_target_pairs={{0,2},{1,3},{2,0},{3,1},{4,6},{5,7},{6,4},{7,5},{8,10},{9,11},{10,... | collective-permute-start | bytes 589832 | tf_op jit(solution)/shard_map/ppermute | solution.py:392
  11.6 0.0 collective-permute-done.b_ref
  11.6 2.5 %own_sum.1 = (s32[16]{0:T(128)S(4)}, f32[384,128]{1,0:T(8,128)S(1)}, bf16[640,4096]{1,0:T(8,128)(2,1)S(1)}) custom-call(s32[64]{0:T(128)S(4)} %get-tuple-element.24.slot_ref, f32[384,128]{1,0:T(8,128)S(1)} %get-tuple-element.25.a_ref, f32[384,128]{1,0:T(8,128)S(1)} %collective-permute-done.b_ref, bf16[640,4096]{1,0:T(8,128)(2,1)} %bitcast.12), custom_call_target="tpu_custom_call" | custom-call | flops 49152 | bytes 5242880 | tf_op jit(solution)/shard_map/own_sum/pallas_call | solution.py:186
  14.2 0.0 copy-start
  14.2 2.6 %collective-permute-done.2.b_ref = f32[384,128]{1,0:T(8,128)S(1)} collective-permute-done((f32[384,128]{1,0:T(8,128)S(1)}, f32[384,128]{1,0:T(8,128)S(1)}, u32[]{:S(2)}, u32[]{:S(2)}) %collective-permute-start.2) | collective-permute-done | bytes 196640 | tf_op jit(solution)/shard_map/ppermute | solution.py:392
  16.8 0.7 %unit_grads.1 = (bf16[160,128]{1,0:T(8,128)(2,1)S(1)}, bf16[160,128]{1,0:T(8,128)(2,1)S(1)}, bf16[160,128]{1,0:T(8,128)(2,1)S(1)}, bf16[160,128]{1,0:T(8,128)(2,...) custom-call(s32[16]{0:T(128)S(4)} %get-tuple-element.27.row_ref, ...), custom_call_target="tpu_custom_call" | custom-call | flops 20000000 | bytes 1000000 | tf_op jit(solution)/shard_map/unit_grads/pallas_call | solution.py:238
  17.5 2.9 %collective-permute-start.3 = (bf16[160,128]{1,0:T(8,128)(2,1)S(1)}, bf16[160,128]{1,0:T(8,128)(2,1)S(1)}, u32[]{:S(2)}, u32[]{:S(2)}) collective-permute-start(bf16[160,128]{1,0:T(8,128)(2,1)S(1)} %get-tuple-element.32), channel_id=1, source_target_pairs={{0,16},{4,20},{8,24},{12,28},{16,0},{20,4},{24,8},{28,12},{1,17},{... | collective-permute-start | bytes 122888 | tf_op jit(solution)/shard_map/ppermute | solution.py:404
  20.4 2.3 %collective-permute-start.4 = (bf16[160,128]{1,0:T(8,128)(2,1)S(1)}, bf16[160,128]{1,0:T(8,128)(2,1)S(1)}, u32[]{:S(2)}, u32[]{:S(2)}) collective-permute-start(bf16[160,128]{1,0:T(8,128)(2,1)S(1)} %get-tuple-element.33), channel_id=1, source_target_pairs={{0,28},{4,24},{8,20},{12,16},{16,12},{20,8},{24,4},{28,0},{1,29},{... | collective-permute-start | bytes 122888 | tf_op jit(solution)/shard_map/ppermute | solution.py:404
  22.7 0.2 collective-permute-start.5
  22.9 2.9 %collective-permute-start.6 = (bf16[160,128]{1,0:T(8,128)(2,1)S(1)}, bf16[160,128]{1,0:T(8,128)(2,1)S(1)}, u32[]{:S(2)}, u32[]{:S(2)}) collective-permute-start(bf16[160,128]{1,0:T(8,128)(2,1)S(1)} %get-tuple-element.35), channel_id=1, source_target_pairs={{0,24},{4,28},{8,16},{12,20},{16,8},{20,12},{24,0},{28,4},{1,25},{... | collective-permute-start | bytes 122888 | tf_op jit(solution)/shard_map/ppermute | solution.py:404
  25.8 1.2 %collective-permute-start.8 = (bf16[160,128]{1,0:T(8,128)(2,1)S(1)}, bf16[160,128]{1,0:T(8,128)(2,1)S(1)}, u32[]{:S(2)}, u32[]{:S(2)}) collective-permute-start(bf16[160,128]{1,0:T(8,128)(2,1)S(1)} %get-tuple-element.36), channel_id=1, source_target_pairs={{0,20},{4,16},{8,28},{12,24},{16,4},{20,0},{24,12},{28,8},{1,21},{... | collective-permute-start | bytes 122888 | tf_op jit(solution)/shard_map/ppermute | solution.py:404
  27.1 0.4 collective-permute-done.4
  27.5 1.1 %collective-permute-start.9 = (bf16[160,128]{1,0:T(8,128)(2,1)S(1)}, bf16[160,128]{1,0:T(8,128)(2,1)S(1)}, u32[]{:S(2)}, u32[]{:S(2)}) collective-permute-start(bf16[160,128]{1,0:T(8,128)(2,1)S(1)} %get-tuple-element.37), channel_id=1, source_target_pairs={{0,4},{4,0},{8,12},{12,8},{16,20},{20,16},{24,28},{28,24},{1,5},{5... | collective-permute-start | bytes 122888 | tf_op jit(solution)/shard_map/ppermute | solution.py:404
  28.6 0.0 collective-permute-done.3
  28.6 0.7 %collective-permute-start.10 = (bf16[160,128]{1,0:T(8,128)(2,1)S(1)}, bf16[160,128]{1,0:T(8,128)(2,1)S(1)}, u32[]{:S(2)}, u32[]{:S(2)}) collective-permute-start(bf16[160,128]{1,0:T(8,128)(2,1)S(1)} %get-tuple-element.39), channel_id=1, source_target_pairs={{0,8},{4,12},{8,0},{12,4},{16,24},{20,28},{24,16},{28,20},{1,9},{5... | collective-permute-start | bytes 122888 | tf_op jit(solution)/shard_map/ppermute | solution.py:404
  29.3 0.0 collective-permute-done.5
  29.3 0.0 collective-permute-done.6
  29.4 1.6 %collective-permute-start.7 = (bf16[800,128]{1,0:T(8,128)(2,1)S(1)}, bf16[800,128]{1,0:T(8,128)(2,1)S(1)}, u32[]{:S(2)}, u32[]{:S(2)}) collective-permute-start(bf16[800,128]{1,0:T(8,128)(2,1)S(1)} %constant_dynamic-update-slice_fusion.rest_0_), channel_id=1, source_target_pairs={{0,2},{1,3},{2,0},{3,1},{4,6},{5,7},{6,4},{7,5},{8,10},{9,11},{10,... | collective-permute-start | bytes 614408 | tf_op jit(solution)/shard_map/ppermute | solution.py:406
  30.9 1.1 %collective-permute-done.8 = bf16[160,128]{1,0:T(8,128)(2,1)S(1)} collective-permute-done((bf16[160,128]{1,0:T(8,128)(2,1)S(1)}, bf16[160,128]{1,0:T(8,128)(2,1)S(1)}, u32[]{:S(2)}, u32[]{:S(2)}) %collective-permute-start.8) | collective-permute-done | bytes 40992 | tf_op jit(solution)/shard_map/ppermute | solution.py:404
  32.0 0.0 collective-permute-done.9
  32.0 0.6 %collective-permute-done.10 = bf16[160,128]{1,0:T(8,128)(2,1)S(1)} collective-permute-done((bf16[160,128]{1,0:T(8,128)(2,1)S(1)}, bf16[160,128]{1,0:T(8,128)(2,1)S(1)}, u32[]{:S(2)}, u32[]{:S(2)}) %collective-permute-start.10) | collective-permute-done | bytes 40992 | tf_op jit(solution)/shard_map/ppermute | solution.py:404
  32.6 1.6 %collective-permute-start.11 = (bf16[480,128]{1,0:T(8,128)(2,1)S(1)}, bf16[480,128]{1,0:T(8,128)(2,1)S(1)}, u32[]{:S(2)}, u32[]{:S(2)}) collective-permute-start(bf16[480,128]{1,0:T(8,128)(2,1)S(1)} %constant_dynamic-update-slice_fusion.5.rest_1_), channel_id=1, source_target_pairs={{0,2},{1,3},{2,0},{3,1},{4,6},{5,7},{6,4},{7,5},{8,10},{9,11},{10,... | collective-permute-start | bytes 368648 | tf_op jit(solution)/shard_map/ppermute | solution.py:406
  34.2 0.0 collective-permute-start.14
  34.2 1.8 %collective-permute-done.7.rest_0_ = bf16[800,128]{1,0:T(8,128)(2,1)S(1)} collective-permute-done((bf16[800,128]{1,0:T(8,128)(2,1)S(1)}, bf16[800,128]{1,0:T(8,128)(2,1)S(1)}, u32[]{:S(2)}, u32[]{:S(2)}) %collective-permute-start.7) | collective-permute-done | bytes 204832 | tf_op jit(solution)/shard_map/ppermute | solution.py:406
  36.0 0.0 collective-permute-start.12
  36.0 0.5 collective-permute-start.15
  36.5 1.0 %collective-permute-done.11.rest_1_ = bf16[480,128]{1,0:T(8,128)(2,1)S(1)} collective-permute-done((bf16[480,128]{1,0:T(8,128)(2,1)S(1)}, bf16[480,128]{1,0:T(8,128)(2,1)S(1)}, u32[]{:S(2)}, u32[]{:S(2)}) %collective-permute-start.11) | collective-permute-done | bytes 122912 | tf_op jit(solution)/shard_map/ppermute | solution.py:406
  37.6 0.0 collective-permute-start.13
  37.6 0.1 collective-permute-done.15.rest_3_
  37.7 0.0 collective-permute-done.14.rest_2_
  37.7 0.9 %staged.1.rest_4_ = bf16[80,4096]{1,0:T(8,128)(2,1)S(1)} custom-call(bf16[800,128]{1,0:T(8,128)(2,1)S(1)} %constant_dynamic-update-slice_fusion.rest_0_, bf16[480,128]{1,0:T(8,128)(2,1)S(1)} %constant_dynamic-update-slice_fusion.5.rest_1_, bf16[800,128]{1,0:T(8,128)(2,1)S(1)} %collective-permute-done.14.rest_2_, ...), custom_call_target="tpu_custom_call" | custom-call | flops 327680 | bytes 2621440 | tf_op jit(solution)/shard_map/staged/pallas_call | solution.py:281
  38.6 0.3 collective-permute-done.13.rest_3_
  38.9 0.0 collective-permute-done.12.rest_2_
  38.9 2.1 %scores.1 = bf16[192,640]{1,0:T(8,128)(2,1)S(1)} custom-call(bf16[800,128]{1,0:T(8,128)(2,1)S(1)} %collective-permute-done.7.rest_0_, bf16[480,128]{1,0:T(8,128)(2,1)S(1)} %collective-permute-done.11.rest_1_, bf16[800,128]{1,0:T(8,128)(2,1)S(1)} %collective-permute-done.12.rest_2_, bf16[480,128]{1,0:T(8,128)(2,1)S(1)} %collective-permute-done.13.rest_3_, ...), custom_call_target="tpu_custom_call" | custom-call | flops 838860800 | bytes 5242880 | tf_op jit(solution)/shard_map/scores/pallas_call | solution.py:323
  41.0 12.6 %all_to_all.5 = bf16[8,24,640]{2,1,0:T(8,128)(2,1)S(1)} all-to-all(bf16[8,24,640]{2,1,0:T(8,128)(2,1)S(1)} %bitcast.9), channel_id=1, replica_groups=mesh['dp'=8,'tensor'=4] {'dp'}, dimensions={0} | all-to-all | bytes 491520 | tf_op jit(solution)/shard_map/all_to_all | solution.py:412
  53.6 0.0 copy-done
  53.6 0.9 %pick_rows.1 = f32[320,128]{1,0:T(8,128)} custom-call(s32[1,64]{1,0:T(1,128)S(1)} %copy-done, bf16[192,640]{1,0:T(8,128)(2,1)S(1)} %bitcast.10), custom_call_target="tpu_custom_call" | custom-call | flops 16000000 | bytes 400000 | tf_op jit(solution)/shard_map/pick_rows/pallas_call | solution.py:354
  (9 shorter events, 0.1 us)
Async XLA Ops:
  7.1 1.6 %collective-permute-start.1 = (f32[384,128]{1,0:T(8,128)S(1)}, f32[384,128]{1,0:T(8,128)S(1)}, u32[]{:S(2)}, u32[]{:S(2)}) collective-permute-start(f32[384,128]{1,0:T(8,128)S(1)} %get-tuple-element.30), channel_id=1, source_target_pairs={{0,1},{1,0},{2,3},{3,2},{4,5},{5,4},{6,7},{7,6},{8,9},{9,8},{10,11... | collective-permute-start | bytes 589832 | tf_op jit(solution)/shard_map/ppermute | solution.py:390
  7.6 4.1 %collective-permute-start = (f32[384,128]{1,0:T(8,128)S(1)}, f32[384,128]{1,0:T(8,128)S(1)}, u32[]{:S(2)}, u32[]{:S(2)}) collective-permute-start(f32[384,128]{1,0:T(8,128)S(1)} %get-tuple-element.26), channel_id=1, source_target_pairs={{0,1},{1,0},{2,3},{3,2},{4,5},{5,4},{6,7},{7,6},{8,9},{9,8},{10,11... | collective-permute-start | bytes 589832 | tf_op jit(solution)/shard_map/ppermute | solution.py:391
  8.7 8.2 %collective-permute-start.2 = (f32[384,128]{1,0:T(8,128)S(1)}, f32[384,128]{1,0:T(8,128)S(1)}, u32[]{:S(2)}, u32[]{:S(2)}) collective-permute-start(f32[384,128]{1,0:T(8,128)S(1)} %add.3), channel_id=1, source_target_pairs={{0,2},{1,3},{2,0},{3,1},{4,6},{5,7},{6,4},{7,5},{8,10},{9,11},{10,... | collective-permute-start | bytes 589832 | tf_op jit(solution)/shard_map/ppermute | solution.py:392
  14.2 39.5 %copy-start = (s32[1,64]{1,0:T(1,128)S(1)}, s32[1,64]{1,0:T(1,128)}, u32[]{:S(2)}) copy-start(s32[1,64]{1,0:T(1,128)} %get-tuple-element.23.row_ref) | copy-start | bytes 772
  17.5 11.1 %collective-permute-start.3 = (bf16[160,128]{1,0:T(8,128)(2,1)S(1)}, bf16[160,128]{1,0:T(8,128)(2,1)S(1)}, u32[]{:S(2)}, u32[]{:S(2)}) collective-permute-start(bf16[160,128]{1,0:T(8,128)(2,1)S(1)} %get-tuple-element.32), channel_id=1, source_target_pairs={{0,16},{4,20},{8,24},{12,28},{16,0},{20,4},{24,8},{28,12},{1,17},{... | collective-permute-start | bytes 122888 | tf_op jit(solution)/shard_map/ppermute | solution.py:404
  20.4 7.1 %collective-permute-start.4 = (bf16[160,128]{1,0:T(8,128)(2,1)S(1)}, bf16[160,128]{1,0:T(8,128)(2,1)S(1)}, u32[]{:S(2)}, u32[]{:S(2)}) collective-permute-start(bf16[160,128]{1,0:T(8,128)(2,1)S(1)} %get-tuple-element.33), channel_id=1, source_target_pairs={{0,28},{4,24},{8,20},{12,16},{16,12},{20,8},{24,4},{28,0},{1,29},{... | collective-permute-start | bytes 122888 | tf_op jit(solution)/shard_map/ppermute | solution.py:404
  22.7 6.6 %collective-permute-start.5 = (bf16[160,128]{1,0:T(8,128)(2,1)S(1)}, bf16[160,128]{1,0:T(8,128)(2,1)S(1)}, u32[]{:S(2)}, u32[]{:S(2)}) collective-permute-start(bf16[160,128]{1,0:T(8,128)(2,1)S(1)} %get-tuple-element.34), channel_id=1, source_target_pairs={{0,12},{4,8},{8,4},{12,0},{16,28},{20,24},{24,20},{28,16},{1,13},{... | collective-permute-start | bytes 122888 | tf_op jit(solution)/shard_map/ppermute | solution.py:404
  22.9 6.4 %collective-permute-start.6 = (bf16[160,128]{1,0:T(8,128)(2,1)S(1)}, bf16[160,128]{1,0:T(8,128)(2,1)S(1)}, u32[]{:S(2)}, u32[]{:S(2)}) collective-permute-start(bf16[160,128]{1,0:T(8,128)(2,1)S(1)} %get-tuple-element.35), channel_id=1, source_target_pairs={{0,24},{4,28},{8,16},{12,20},{16,8},{20,12},{24,0},{28,4},{1,25},{... | collective-permute-start | bytes 122888 | tf_op jit(solution)/shard_map/ppermute | solution.py:404
  25.8 6.2 %collective-permute-start.8 = (bf16[160,128]{1,0:T(8,128)(2,1)S(1)}, bf16[160,128]{1,0:T(8,128)(2,1)S(1)}, u32[]{:S(2)}, u32[]{:S(2)}) collective-permute-start(bf16[160,128]{1,0:T(8,128)(2,1)S(1)} %get-tuple-element.36), channel_id=1, source_target_pairs={{0,20},{4,16},{8,28},{12,24},{16,4},{20,0},{24,12},{28,8},{1,21},{... | collective-permute-start | bytes 122888 | tf_op jit(solution)/shard_map/ppermute | solution.py:404
  27.5 4.5 %collective-permute-start.9 = (bf16[160,128]{1,0:T(8,128)(2,1)S(1)}, bf16[160,128]{1,0:T(8,128)(2,1)S(1)}, u32[]{:S(2)}, u32[]{:S(2)}) collective-permute-start(bf16[160,128]{1,0:T(8,128)(2,1)S(1)} %get-tuple-element.37), channel_id=1, source_target_pairs={{0,4},{4,0},{8,12},{12,8},{16,20},{20,16},{24,28},{28,24},{1,5},{5... | collective-permute-start | bytes 122888 | tf_op jit(solution)/shard_map/ppermute | solution.py:404
  28.6 4.0 %collective-permute-start.10 = (bf16[160,128]{1,0:T(8,128)(2,1)S(1)}, bf16[160,128]{1,0:T(8,128)(2,1)S(1)}, u32[]{:S(2)}, u32[]{:S(2)}) collective-permute-start(bf16[160,128]{1,0:T(8,128)(2,1)S(1)} %get-tuple-element.39), channel_id=1, source_target_pairs={{0,8},{4,12},{8,0},{12,4},{16,24},{20,28},{24,16},{28,20},{1,9},{5... | collective-permute-start | bytes 122888 | tf_op jit(solution)/shard_map/ppermute | solution.py:404
  29.4 6.7 %collective-permute-start.7 = (bf16[800,128]{1,0:T(8,128)(2,1)S(1)}, bf16[800,128]{1,0:T(8,128)(2,1)S(1)}, u32[]{:S(2)}, u32[]{:S(2)}) collective-permute-start(bf16[800,128]{1,0:T(8,128)(2,1)S(1)} %constant_dynamic-update-slice_fusion.rest_0_), channel_id=1, source_target_pairs={{0,2},{1,3},{2,0},{3,1},{4,6},{5,7},{6,4},{7,5},{8,10},{9,11},{10,... | collective-permute-start | bytes 614408 | tf_op jit(solution)/shard_map/ppermute | solution.py:406
  32.6 4.9 %collective-permute-start.11 = (bf16[480,128]{1,0:T(8,128)(2,1)S(1)}, bf16[480,128]{1,0:T(8,128)(2,1)S(1)}, u32[]{:S(2)}, u32[]{:S(2)}) collective-permute-start(bf16[480,128]{1,0:T(8,128)(2,1)S(1)} %constant_dynamic-update-slice_fusion.5.rest_1_), channel_id=1, source_target_pairs={{0,2},{1,3},{2,0},{3,1},{4,6},{5,7},{6,4},{7,5},{8,10},{9,11},{10,... | collective-permute-start | bytes 368648 | tf_op jit(solution)/shard_map/ppermute | solution.py:406
  34.2 3.5 %collective-permute-start.14 = (bf16[800,128]{1,0:T(8,128)(2,1)S(1)}, bf16[800,128]{1,0:T(8,128)(2,1)S(1)}, u32[]{:S(2)}, u32[]{:S(2)}) collective-permute-start(bf16[800,128]{1,0:T(8,128)(2,1)S(1)} %constant_dynamic-update-slice_fusion.rest_0_), channel_id=1, source_target_pairs={{0,1},{1,0},{2,3},{3,2},{4,5},{5,4},{6,7},{7,6},{8,9},{9,8},{10,11... | collective-permute-start | bytes 614408 | tf_op jit(solution)/shard_map/ppermute | solution.py:407
  36.0 2.9 %collective-permute-start.12 = (bf16[800,128]{1,0:T(8,128)(2,1)S(1)}, bf16[800,128]{1,0:T(8,128)(2,1)S(1)}, u32[]{:S(2)}, u32[]{:S(2)}) collective-permute-start(bf16[800,128]{1,0:T(8,128)(2,1)S(1)} %collective-permute-done.7.rest_0_), channel_id=1, source_target_pairs={{0,1},{1,0},{2,3},{3,2},{4,5},{5,4},{6,7},{7,6},{8,9},{9,8},{10,11... | collective-permute-start | bytes 614408 | tf_op jit(solution)/shard_map/ppermute | solution.py:409
  36.0 1.6 %collective-permute-start.15 = (bf16[480,128]{1,0:T(8,128)(2,1)S(1)}, bf16[480,128]{1,0:T(8,128)(2,1)S(1)}, u32[]{:S(2)}, u32[]{:S(2)}) collective-permute-start(bf16[480,128]{1,0:T(8,128)(2,1)S(1)} %constant_dynamic-update-slice_fusion.5.rest_1_), channel_id=1, source_target_pairs={{0,1},{1,0},{2,3},{3,2},{4,5},{5,4},{6,7},{7,6},{8,9},{9,8},{10,11... | collective-permute-start | bytes 368648 | tf_op jit(solution)/shard_map/ppermute | solution.py:407
  37.6 1.3 %collective-permute-start.13 = (bf16[480,128]{1,0:T(8,128)(2,1)S(1)}, bf16[480,128]{1,0:T(8,128)(2,1)S(1)}, u32[]{:S(2)}, u32[]{:S(2)}) collective-permute-start(bf16[480,128]{1,0:T(8,128)(2,1)S(1)} %collective-permute-done.11.rest_1_), channel_id=1, source_target_pairs={{0,1},{1,0},{2,3},{3,2},{4,5},{5,4},{6,7},{7,6},{8,9},{9,8},{10,11... | collective-permute-start | bytes 368648 | tf_op jit(solution)/shard_map/ppermute | solution.py:409
